TPU v7x, 32 devices: a whole 2x2x4 slice. The times are simulated.
32 devices in a mesh: ctx: 8 (over z, x), head: 4 (over y, core).
Axes of the slice: x: 2, y: 2, z: 4, core: 2. Of those that a mesh axis runs over, the one named last changes fastest.
Arguments:
- values: bfloat16 [8192, 5120], P(('ctx', 'head')), may hold values from -6 to 6
- state_in: bfloat16 [8192, 128], P('ctx'), may hold values from -0.5 to 0.5
- state_out: bfloat16 [8192, 128], P('ctx'), may hold values from -6 to 6
- log_decay: float32 [8192, 80], P('ctx', 'head'), may hold values from -1 to 0
- level_class: int32 [8192], P('ctx'), may hold values from 0 to 31
- level_table: float32 [32, 8, 80], P(None, None, 'head'), may hold values from 0.2 to 2
- skip_gain: float32 [80], P('head'), may hold values from 0.5 to 2
- norm_gain: float32 [5120], P('head'), may hold values from 0.1 to 1.9
- out_weight: bfloat16 [5120, 2560], P('head', 'ctx'), may hold values from -0.078125 to 0.078125
Outputs:
- projected: bfloat16 [8192, 2560], P(('ctx', 'head'))
All inputs are finite; a program needn't handle non-finite values.
Results may differ from a plain program's by a relative error of at most 0.0049.
Values may be sent and summed in bfloat16 or wider, within the bound.
No kernel may reach another device: no remote copies, remote signals or barrier semaphores. Data moves between devices by JAX's collectives and lax.ppermute only.
A program may use at most 128 MiB of HBM per device.

v0:
```python
import functools

import jax
import jax.numpy as jnp
from jax import lax
from jax.experimental import pallas as pl
from jax.experimental.pallas import tpu as pltpu
from jax.sharding import PartitionSpec as P

CH = 64
EPSILON = 1e-05
LANES = 128
F32 = jnp.float32
BF16 = jnp.bfloat16
VMEM_LIMIT = 40 * 1024 * 1024


def dot(a, b):
    return lax.dot_general(a, b, (((1,), (0,)), ((), ())), preferred_element_type=F32)


def dot_nt(a, b):
    return lax.dot_general(a, b, (((1,), (1,)), ((), ())), preferred_element_type=F32)


def swap(value, axis, distance):
    pairs = [(source, source ^ distance) for source in range(lax.axis_size(axis))]
    return lax.ppermute(value, axis, pairs)


def tie(value, *after):
    return lax.optimization_barrier((value,) + after)[0]


def three_parts(x):
    high = x.astype(BF16)
    rest = x - high.astype(F32)
    middle = rest.astype(BF16)
    low = (rest - middle.astype(F32)).astype(BF16)
    return high, middle, low


def two_parts(x):
    high = x.astype(BF16)
    return high, (x - high.astype(F32)).astype(BF16)


def merge_rows(stretches):
    rows = [("own", c, 0) for c in range(stretches - 1)]
    for c in range(stretches - 1):
        k = 0
        while (c >> k) & 1:
            rows.append(("merge", c, k))
            k += 1
    return rows


def head_rows(head, width):
    return slice(head * width, (head + 1) * width)


def exact_dot(x, ones):
    return sum(dot(part, ones) for part in three_parts(x))


def split_kernel(me_ref, *refs):
    half = len(refs) // 2
    for value_ref, part_ref in zip(refs[:half], refs[half:]):
        part_ref[...] = jnp.transpose(value_ref[...])


def fade_kernel(blocks, me_ref, decay_ref, own_ref, side_ref, *refs):
    far_refs, total_ref = refs[:-1], refs[-1]
    head_count, tokens = decay_ref.shape
    rows = tokens // blocks
    row = lax.broadcasted_iota(jnp.int32, (rows, rows), 0)
    col = lax.broadcasted_iota(jnp.int32, (rows, rows), 1)
    later = jnp.where(row > col, 1.0, 0.0).astype(BF16)
    me = me_ref[0]
    after = jnp.zeros((head_count, 1), F32)
    for block in reversed(range(blocks)):
        decay = decay_ref[:, block * rows : (block + 1) * rows]
        left = exact_dot(decay, later)
        fade = jnp.exp(left + after)
        after = after + left[:, 0:1] + decay[:, 0:1]
        own_index = me ^ block

        @pl.when(own_index == 0)
        def _():
            own_ref[...] = fade

        @pl.when(own_index == 1)
        def _():
            side_ref[...] = fade

        for i, far_ref in enumerate(far_refs):
            for j in range(2):

                @pl.when(own_index == 2 * (i + 1) + j)
                def _():
                    far_ref[j] = fade

    total_ref[...] = jnp.zeros_like(total_ref)
    total_ref[:head_count, :] = jnp.broadcast_to(after, (head_count, LANES))


def pack_kernel(*refs):
    side_ref, *got_refs, out_ref = refs
    out_ref[0] = side_ref[...]
    for i, got_ref in enumerate(got_refs):
        out_ref[i + 1] = got_ref[0]


def factors_kernel(
    levels, blocks, decay_ref, class_ref, table_ref, in_ref, out_ref,
    lift_ref, read_ref, cross_ref, merge_ref, score_ref, masked_ref, reader_ref, pair_ref,
):
    head_count, tokens = decay_ref.shape
    stretches = tokens // CH
    rows = tokens // blocks
    per_block = rows // CH
    local = read_ref.shape[0] - 1
    state_size = in_ref.shape[1]
    padded = table_ref.shape[0] // levels
    classes = table_ref.shape[1]
    row = lax.broadcasted_iota(jnp.int32, (rows, rows), 0)
    col = lax.broadcasted_iota(jnp.int32, (rows, rows), 1)
    inside = (row // CH == col // CH) & (row <= col)
    upto = jnp.where(inside, 1.0, 0.0).astype(BF16)
    within, starts = [], [jnp.zeros((head_count, 1), F32)]
    for g in range(blocks):
        within.append(exact_dot(decay_ref[:, g * rows : (g + 1) * rows], upto))
        for s in range(per_block):
            last = (s + 1) * CH
            starts.append(starts[-1] + within[-1][:, last - 1 : last])
    class_row = lax.broadcasted_iota(jnp.int32, (classes, rows), 0)
    lane = lax.broadcasted_iota(jnp.int32, (head_count, rows), 1) // CH
    token = lax.broadcasted_iota(jnp.int32, (rows, state_size), 0) // CH

    def by_stretch(columns):
        spread = jnp.broadcast_to(columns[0], (head_count, rows))
        for s in range(1, per_block):
            spread = jnp.where(lane == s, columns[s], spread)
        return spread

    for g in range(blocks):
        at = slice(g * rows, (g + 1) * rows)
        onehot = jnp.where(class_ref[:, at] == class_row, 1.0, 0.0).astype(BF16)
        weights = sum(dot(part, onehot) for part in three_parts(table_ref[...]))
        weight = lambda level: weights[level * padded : level * padded + head_count, :]
        lift_ref[g] = jnp.exp(-within[g])
        read_ref[0, g] = jnp.exp(within[g]) * weight(0)
        first = g * per_block
        for level in range(1, local + 1):
            begins, active = [], []
            for c in range(first, first + per_block):
                upper = (c >> (level - 1)) & 1
                begins.append(starts[c] - starts[(c >> (level - 1)) << (level - 1)])
                active.append(jnp.full((head_count, 1), float(upper), F32))
            factor = jnp.exp(within[g] + by_stretch(begins)) * weight(level)
            read_ref[level, g] = factor * by_stretch(active)
        far = jnp.exp(within[g] + by_stretch(starts[first : first + per_block]))
        for level in range(local + 1, levels):
            cross_ref[level - local - 1, g] = far * weight(level)
        own_in, own_out = in_ref[at, :], out_ref[at, :]
        scores = jnp.where(inside, dot_nt(own_in, own_out), 0.0)
        score_ref[g, 0], score_ref[g, 1] = two_parts(scores)
        for s in range(per_block):
            masked = jnp.where(token == s, own_in.astype(F32), 0.0).astype(BF16)
            masked_ref[g, :, s * state_size : (s + 1) * state_size] = masked
        turned = jnp.transpose(own_out.astype(F32))
        reader = turned.astype(BF16)
        reader_ref[g, :state_size, :] = reader
        reader_ref[g, state_size:, :] = reader
        pairs = max(per_block // 2, 1)
        place = lax.broadcasted_iota(jnp.int32, (state_size, rows), 1) // (2 * CH)
        for j in range(pairs):
            alone = jnp.where(place == j, turned, 0.0).astype(BF16)
            pair_ref[g, j * state_size : (j + 1) * state_size, :] = alone
    for i, (kind, c, k) in enumerate(merge_rows(stretches)):
        first = c if kind == "own" else c + 1 - 2**k
        merge_ref[i] = jnp.broadcast_to(jnp.exp(starts[c + 1] - starts[first]), (head_count, LANES))


def partial_state_kernel(count, *refs):
    value_refs, refs = refs[:count], refs[count:]
    fade_refs, (in_ref, keep_ref, send_ref, faded) = refs[:count], refs[count:]
    own_in = in_ref[...]
    for r in [*range(1, count, 2), *range(0, count, 2)]:
        fade = fade_refs[r][...].reshape(fade_refs[r].shape[-2:])
        head_count = fade.shape[0]
        width = value_refs[r].shape[0] // head_count
        for h in range(head_count):
            at = head_rows(h, width)
            faded[at, :] = (fade[h : h + 1, :] * value_refs[r][at, :].astype(F32)).astype(BF16)
        state = dot(faded[...], own_in)
        if r % 2 == 1:
            send_ref[r // 2] = state.astype(BF16)
        else:
            keep_ref[r // 2] = state


def fold_kernel(*refs):
    count = len(refs) // 3
    for keep_ref, got_ref, far_ref in zip(refs[:count], refs[count : 2 * count], refs[2 * count :]):
        far_ref[...] = (keep_ref[0] + got_ref[0].astype(F32)).astype(BF16)


def pack_state(sent_ref, state, total):
    channels = state.shape[0]
    sent_ref[:channels, :] = state.astype(BF16)
    high, middle, low = (part.astype(F32) for part in three_parts(total))
    lane = lax.broadcasted_iota(jnp.int32, total.shape, 1)
    parts = jnp.where(lane < LANES // 4, high, jnp.where(lane < LANES // 2, middle, low))
    sent_ref[channels:, :] = parts.astype(BF16)


def first_kernel(own_ref, core_ref, total_ref, *refs):
    *far_refs, running_ref, sent_ref = refs
    running = own_ref[0] + core_ref[0].astype(F32)
    for far_ref in far_refs:
        running = running + far_ref[...].astype(F32)
    running_ref[...] = running
    pack_state(sent_ref, running, total_ref[...])


def merge_kernel(
    bit, head_count, place_ref, running_ref, total_ref, offset_ref, got_ref,
    next_running_ref, next_total_ref, next_offset_ref, factor_ref, sent_ref,
):
    channels = running_ref.shape[0]
    width = channels // head_count
    place = place_ref[0]
    upper = place // 2**bit % 2 == 1
    total = total_ref[...]
    parts = got_ref[channels:, :].astype(F32)
    middle, low = LANES // 4, LANES // 2
    partner = parts[:, 0:1] + parts[:, middle : middle + 1] + parts[:, low : low + 1]
    partner = jnp.broadcast_to(partner, total.shape)
    fading = jnp.exp(jnp.where(upper, total, partner))
    for h in range(head_count):
        at = head_rows(h, width)
        got, running = got_ref[at, :].astype(F32), running_ref[at, :]
        lower, higher = jnp.where(upper, got, running), jnp.where(upper, running, got)
        next_running_ref[at, :] = fading[h : h + 1, :] * lower + higher
    joined = total + partner
    next_total_ref[...] = joined
    offset = jnp.where(upper, offset_ref[...] + partner, offset_ref[...])
    next_offset_ref[...] = offset
    next_upper = place // 2 ** (bit + 1) % 2 == 1
    factor_ref[...] = jnp.where(next_upper, jnp.exp(offset), 0.0)
    pack_state(sent_ref, next_running_ref[...], joined)


def local_kernel(near, me_ref, *refs):
    groups = refs[-1].shape[0]
    value_refs, refs = refs[:groups], refs[groups:]
    lift_ref, read_ref, merge_ref, score_ref, masked_ref, reader_ref, pair_ref = refs[:7]
    skip_ref, cross_ref, *refs = refs[7:]
    factor_refs, state_refs, refs = refs[:near], refs[near : 2 * near], refs[2 * near :]
    pre_ref, lifted, sums, operand, pairs_ref, nodes = refs
    channels, group_rows = value_refs[0].shape
    head_count = lift_ref.shape[1]
    width = channels // head_count
    me = me_ref[0]
    per_group = group_rows // CH
    stretches = groups * per_group
    state_size = reader_ref.shape[1] // 2
    place = {kind: i for i, kind in enumerate(merge_rows(stretches))}
    heads = [(h, head_rows(h, width)) for h in range(head_count)]
    for r, value_ref in enumerate(value_refs):
        g = me ^ r
        lift = lift_ref[g]
        for h, at in heads:
            lifted[at, :] = (lift[h : h + 1, :] * value_ref[at, :].astype(F32)).astype(BF16)
        direct = dot(lifted[...], score_ref[g, 0]) + dot(lifted[...], score_ref[g, 1])
        read = read_ref[0, g]
        terms = []
        for level, (state_ref, factor_ref) in enumerate(zip(state_refs, factor_refs)):
            gained = dot(state_ref[:channels, :], reader_ref[g, :state_size, :])
            scale = cross_ref[level, g] * factor_ref[:head_count, 0:1]
            terms.append((scale, gained))
        for h, at in heads:
            total = read[h : h + 1, :] * direct[at, :]
            total = total + skip_ref[h : h + 1, :] * value_ref[at, :].astype(F32)
            for scale, gained in terms:
                total = total + scale[h : h + 1, :] * gained[at, :]
            pre_ref[g, at, :] = total
        nodes[g] = dot(lifted[...], masked_ref[g])

    for g in range(groups):
        terms = []
        level = per_group.bit_length()
        while 2 ** (level - 1) < stretches:
            if (g * per_group >> (level - 1)) & 1:
                terms.append((read_ref[level, g], dot(operand[level - 1], reader_ref[g])))
            level += 1
        for s in range(per_group):
            c = g * per_group + s
            if c + 1 == stretches:
                break
            merges = [merge_ref[place["own", c, 0]]]
            k = 0
            while (c >> k) & 1:
                merges.append(merge_ref[place["merge", c, k]])
                k += 1
            for h, at in heads:
                node = nodes[g, at, s * state_size : (s + 1) * state_size]
                node = node * merges[0][h : h + 1, :]
                for i, merge in enumerate(merges[1:]):
                    node = node + merge[h : h + 1, :] * sums[i, at, :]
                sums[k, at, :] = node
                high, low = two_parts(node)
                if k == 0 and per_group > 1:
                    pairs_ref[at, s // 2 * state_size : (s // 2 + 1) * state_size] = high
                else:
                    operand[k, at, :state_size] = high
                    operand[k, at, state_size:] = low
            if 1 <= k < per_group.bit_length() - 1:
                scale = read_ref[k + 1, g]
                lane = lax.broadcasted_iota(jnp.int32, scale.shape, 1) // (CH << (k + 1))
                scale = jnp.where(lane == s >> (k + 1), scale, 0.0)
                terms.append((scale, dot(operand[k], reader_ref[g])))
        if per_group > 1:
            terms.append((read_ref[1, g], dot(pairs_ref[...], pair_ref[g])))
        for h, at in heads:
            total = pre_ref[g, at, :]
            for scale, gained in terms:
                total = total + scale[h : h + 1, :] * gained[at, :]
            pre_ref[g, at, :] = total


def finish_kernel(
    half, me_ref, pre_ref, reader_ref, cross_ref, factor_ref, state_ref, gain_ref, *refs
):
    keep_refs, send_ref = refs[:half], refs[half]
    groups, channels, _ = pre_ref.shape
    head_count = cross_ref.shape[2]
    width = channels // head_count
    state_size = reader_ref.shape[1] // 2
    me = me_ref[0]
    state = state_ref[:channels, :]
    for r in range(groups):
        g = me ^ r
        gained = dot(state, reader_ref[g, :state_size, :])
        scale = cross_ref[0, g] * factor_ref[:head_count, 0:1]
        for h in range(head_count):
            at = head_rows(h, width)
            total = pre_ref[g, at, :] + scale[h : h + 1, :] * gained[at, :]
            mean_square = jnp.sum(total * total, axis=0, keepdims=True) * (1.0 / width)
            normed = total * lax.rsqrt(mean_square + EPSILON) * gain_ref[at, 0:1]
            if r % 2 == 0:
                keep_refs[r // 2][at, :] = normed.astype(BF16)
            else:
                send_ref[r // 2, at, :] = normed.astype(BF16)


def project_kernel(place_ref, *refs):
    *refs, out_ref = refs
    rows = out_ref.shape[0]
    kept_refs, other_refs, refs = refs[:rows], refs[rows : 2 * rows], refs[2 * rows :]
    count = len(refs) // 2
    weights, partners = refs[:count], refs[count:]
    width = weights[0].shape[0]
    turn = place_ref[0] % count
    for i, (kept_ref, other_ref) in enumerate(zip(kept_refs, other_refs)):
        for j, (weight, partner) in enumerate(zip(weights, partners)):
            found = dot(weight[...], kept_ref[...]) + dot(partner[...], other_ref[0])
            at = pl.ds(pl.multiple_of((turn ^ j) * width, width), width)
            out_ref[i, at, :] = found.astype(out_ref.dtype)


def assemble_kernel(place_ref, *refs):
    out_ref = refs[-1]
    width = refs[0].shape[0]
    groups = out_ref.shape[1] // width
    each = (len(refs) - 1) // groups
    for p in range(groups):
        own_ref, *far_refs = refs[p * each : (p + 1) * each]
        total = own_ref[...]
        for far_ref in far_refs:
            total = total + far_ref[...].astype(F32)
        start = pl.multiple_of((place_ref[0] ^ p) * width, width)
        out_ref[:, pl.ds(start, width)] = jnp.transpose(total).astype(BF16)


def whole(shape):
    return pl.BlockSpec(shape, lambda *_: (0,) * len(shape))


def on_device(
    values,
    state_in,
    state_out,
    log_decay,
    level_class,
    level_table,
    skip_gain,
    norm_gain,
    out_weight,
):
    heads_size = lax.axis_size("head")
    ctx_size = lax.axis_size("ctx")
    ctx_bits = ctx_size.bit_length() - 1
    me = lax.axis_index("head")
    me1 = me.reshape(1).astype(jnp.int32)
    position = lax.axis_index("ctx")
    place1 = position.reshape(1).astype(jnp.int32)
    tokens = state_in.shape[0]
    rows_dev = values.shape[0]
    head_count = log_decay.shape[1]
    features = values.shape[1] // heads_size
    state_size = state_in.shape[1]
    columns = out_weight.shape[1]
    stretches = tokens // CH
    per_group = rows_dev // CH
    local = stretches.bit_length() - 1
    levels = level_table.shape[1]
    classes = level_table.shape[0]
    extra = -(-head_count // 16) * 16
    padded = -(-head_count // 8) * 8
    half = heads_size // 2
    near = ctx_bits - 1
    params = pltpu.CompilerParams(vmem_limit_bytes=VMEM_LIMIT)
    cheap = pl.CostEstimate(flops=0, bytes_accessed=0, transcendentals=0)
    smem = pl.BlockSpec(memory_space=pltpu.SMEM)
    vmem = pl.BlockSpec(memory_space=pltpu.VMEM)

    def kernel_call(body, name, out_shape, **kwargs):
        return pl.pallas_call(
            body, out_shape=out_shape, compiler_params=params, cost_estimate=cheap, name=name, **kwargs
        )

    def shape(dims, kind=BF16):
        return jax.ShapeDtypeStruct(dims, kind)

    def part(array, index):
        return pl.BlockSpec((1,) + array.shape[1:], lambda *_: (index,) + (0,) * (array.ndim - 1))

    def fenced(body, *operands):
        shapes = jax.eval_shape(body, *operands)
        zeros = lambda *_: jax.tree.map(lambda leaf: jnp.zeros(leaf.shape, leaf.dtype), shapes)
        return lax.cond(position < ctx_size, body, zeros, *operands)

    held, partners = {0: out_weight.T}, {}
    for bit in range(ctx_bits):
        held[2**bit] = swap(held[0], "ctx", 2**bit)

    decays = log_decay.T
    own_fade, side_fade, *far_fades, total = kernel_call(
        functools.partial(fade_kernel, heads_size),
        "fade",
        tuple(
            [shape((head_count, rows_dev), F32)] * 2
            + [shape((2, head_count, rows_dev), F32)] * (half - 1)
            + [shape((extra, LANES), F32)]
        ),
        in_specs=[smem, vmem],
    )(me1, decays)

    got_fades = []
    for i, far in enumerate(far_fades):
        got_fades.append(swap(tie(far, *got_fades), "head", 2 * (i + 1)))
    sides = kernel_call(
        pack_kernel,
        "pack_fades",
        shape((half, head_count, rows_dev), F32),
        grid=(1,),
        in_specs=[whole(side_fade.shape)] + [part(got, 1) for got in got_fades],
        out_specs=whole((half, head_count, rows_dev)),
    )(side_fade, *got_fades)
    sides = swap(sides, "head", 1)

    portions = kernel_call(
        split_kernel,
        "split_values",
        tuple([shape((features, rows_dev))] * heads_size),
        grid_spec=pltpu.PrefetchScalarGridSpec(
            num_scalar_prefetch=1,
            grid=(1,),
            in_specs=[
                pl.BlockSpec((rows_dev, features), lambda i, m, r=r: (0, m[0] ^ r))
                for r in range(heads_size)
            ],
            out_specs=[whole((features, rows_dev))] * heads_size,
        ),
    )(me1, *[values] * heads_size)
    value_head = swap(portions[2], "head", 2)

    fades, fade_specs = [], []
    for r in range(heads_size):
        if r == 0:
            fades.append(own_fade)
            fade_specs.append(whole(own_fade.shape))
        else:
            fades.append(sides if r % 2 else got_fades[r // 2 - 1])
            fade_specs.append(part(fades[-1], r // 2 if r % 2 else 0))
    keep, send = kernel_call(
        lambda me_ref, *refs: partial_state_kernel(heads_size, *refs),
        "partial_states",
        (shape((half, features, state_size), F32), shape((half, features, state_size))),
        grid_spec=pltpu.PrefetchScalarGridSpec(
            num_scalar_prefetch=1,
            grid=(1,),
            in_specs=[whole((features, rows_dev))] * heads_size
            + fade_specs
            + [pl.BlockSpec((rows_dev, state_size), lambda i, m: (m[0], 0))],
            out_specs=[whole((half, features, state_size))] * 2,
            scratch_shapes=[pltpu.VMEM((features, rows_dev), BF16)],
        ),
    )(me1, *portions, *fades, state_in)

    def core_sum(keep, send):
        got = swap(send, "head", 1)
        far = kernel_call(
            fold_kernel,
            "fold",
            tuple([shape((features, state_size))] * (half - 1)),
            in_specs=[part(keep, i) for i in range(1, half)] * 2,
            out_specs=tuple([whole((features, state_size))] * (half - 1)),
            grid=(1,),
        )(*[keep] * (half - 1), *[got] * (half - 1))
        return got, far

    core_states, far_states = fenced(core_sum, keep, send)

    merge_count = len(merge_rows(stretches))
    grouped = (heads_size, head_count, rows_dev)
    pair_rows = max(per_group // 2, 1) * state_size

    def step(bit, running, total, offset, got):
        return kernel_call(
            functools.partial(merge_kernel, bit, head_count),
            "merge",
            (
                shape((features, state_size), F32),
                shape((extra, LANES), F32),
                shape((extra, LANES), F32),
                shape((extra, LANES), F32),
                shape((features + extra, state_size)),
            ),
            in_specs=[smem] + [vmem] * 4,
        )(place1, running, total, offset, got)

    def near_chain(
        keep, core_states, far_states, total, decays, level_class, level_table, state_in, state_out, portion
    ):
        got_states, latest = [], []
        for i, far in enumerate(far_states):
            latest = [swap(tie(far, *latest), "head", 2 * (i + 1))]
            got_states += latest
        running, sent = kernel_call(
            first_kernel,
            "first_state",
            (shape((features, state_size), F32), shape((features + extra, state_size))),
            grid=(1,),
            in_specs=[part(keep, 0), part(core_states, 0), whole(total.shape)]
            + [whole((features, state_size))] * len(got_states),
            out_specs=(whole((features, state_size)), whole((features + extra, state_size))),
        )(keep, core_states, total, *got_states)
        moved, passed, after = {}, {}, []
        for r, array in portion.items():
            moved[r] = swap(tie(array, *after), "head", 1)
            after = [moved[r]]
        after = [running]
        for r, array in moved.items():
            passed[r] = swap(tie(array, *after), "head", r - 1)
            after = [passed[r]]
        table = jnp.transpose(level_table, (1, 2, 0))
        table = jnp.pad(table, ((0, 0), (0, padded - head_count), (0, 0)))
        tables = kernel_call(
            functools.partial(factors_kernel, levels, heads_size),
            "factors",
            (
                shape(grouped, F32),
                shape((local + 1,) + grouped, F32),
                shape((ctx_bits,) + grouped, F32),
                shape((merge_count, head_count, LANES), F32),
                shape((heads_size, 2, rows_dev, rows_dev)),
                shape((heads_size, rows_dev, per_group * state_size)),
                shape((heads_size, 2 * state_size, rows_dev)),
                shape((heads_size, pair_rows, rows_dev)),
            ),
        )(
            tie(decays, running),
            level_class.reshape(1, tokens),
            table.reshape(levels * padded, classes),
            state_in,
            state_out,
        )
        offset = jnp.zeros((extra, LANES), F32)
        factors = [jnp.broadcast_to((position % 2).astype(F32), (extra, LANES))]
        states = []
        for bit in range(near):
            got = swap(sent, "ctx", 2**bit)
            states.append(tie(got, tables[0]) if bit == 0 else got)
            running, total, offset, factor, sent = step(bit, running, total, offset, states[-1])
            factors.append(factor)
        return states, factors, sent, tables, passed

    states, factors, sent, tables, passed = fenced(
        near_chain, keep, core_states, tie(far_states, value_head), total, decays, level_class,
        level_table, state_in, state_out, {r: portions[r] for r in range(3, heads_size, 2)},
    )
    states, passed = list(states), dict(passed)
    passed[2] = value_head
    sent = tie(sent, *[held[2**bit] for bit in range(ctx_bits)])
    for r in range(4, heads_size, 2):
        passed[r] = swap(tie(portions[r], sent), "head", r)

    for r in range(2, ctx_size):
        low = r & -r
        if r not in held and low > 1:
            held[r] = swap(tie(held[r ^ low], sent), "ctx", low)
    for bit in range(2, ctx_bits):
        held[2**bit + 1] = swap(tie(held[2**bit], sent), "ctx", 1)
    for r in (0, 1):
        partners[r] = swap(tie(held[r], sent), "head", 1)

    skips = jnp.broadcast_to(skip_gain[:, None], (head_count, rows_dev))
    gains = norm_gain[:, None]

    def read_levels(sent, tables, factors, states, arrays, skips, gains):
        lift, read, cross, merge, scores, masked, readers, pairs = tables
        state = swap(sent, "ctx", 2**near)
        arrays = [arrays[0], swap(arrays[1], "head", 1)] + list(arrays[2:])
        pre = kernel_call(
            functools.partial(local_kernel, near),
            "local_levels",
            shape((heads_size, features, rows_dev), F32),
            in_specs=[smem] + [vmem] * (heads_size + 9 + 2 * near),
            scratch_shapes=[
                pltpu.VMEM((features, rows_dev), BF16),
                pltpu.VMEM((max(local, 1), features, state_size), F32),
                pltpu.VMEM((max(local, 1), features, 2 * state_size), BF16),
                pltpu.VMEM((features, pair_rows), BF16),
                pltpu.VMEM((heads_size, features, per_group * state_size), F32),
            ],
        )(
            me1, *arrays, lift, read, merge, scores, masked, readers, pairs, skips, cross,
            *factors[:near], *states,
        )
        return kernel_call(
            functools.partial(finish_kernel, half),
            "finish",
            tuple([shape((features, rows_dev))] * half + [shape((half, features, rows_dev))]),
            grid=(1,),
            in_specs=[
                smem,
                whole(pre.shape),
                whole(readers.shape),
                part(cross, near),
                whole((extra, LANES)),
                whole((features + extra, state_size)),
                whole((features, 1)),
            ],
            out_specs=[whole((features, rows_dev))] * half + [whole((half, features, rows_dev))],
        )(me1, pre, readers, cross, factors[near], state, gains)

    arrays = [portions[0], portions[1]] + [passed[r] for r in range(2, heads_size)]
    *kept, sides = fenced(read_levels, sent, tables, factors, states, arrays, skips, gains)

    early_blocks = set(held)
    done = [held[r] for r in held if r not in (0, 1)] + [kept[0]]
    held[3] = swap(tie(held[1], *done), "ctx", 2)
    for r in range(5, ctx_size, 2):
        if r not in held:
            held[r] = swap(tie(held[r ^ 1], *done), "ctx", 1)

    count = 1
    while count * columns % 128 and 2 * count <= ctx_size:
        count *= 2

    others = swap(sides, "head", 1)
    firsts = list(range(0, ctx_size, count))
    group_of = lambda first: range(first, first + count)

    def project(name, first, kept, others, blocks, partners, kind):
        rows = len(kept)
        return kernel_call(
            project_kernel,
            name,
            shape((rows, count * columns, rows_dev), kind),
            in_specs=[smem]
            + [whole((features, rows_dev))] * rows
            + [part(others, first + i) for i in range(rows)]
            + [whole((columns, features))] * (2 * count),
            out_specs=whole((rows, count * columns, rows_dev)),
            grid=(1,),
        )(place1, *kept, *[others] * rows, *blocks, *partners)

    def far_rows(first, kept, others, blocks, partners):
        return project(
            "project_far", 1, kept[1:], others,
            [blocks[r] for r in group_of(first)], [partners[r] for r in group_of(first)], BF16,
        )

    def own_rows(first, kept, others, blocks, partners):
        return project(
            "project_own", 0, kept[:1], others,
            [blocks[r] for r in group_of(first)], [partners[r] for r in group_of(first)], F32,
        )[0]

    def send_rows(far, *after):
        far = tie(far, *after)
        return [swap(far[i - 1], "head", 2 * i) for i in range(1, half)]

    def first_groups(kept, others, blocks, partners):
        more = {r: swap(blocks[r], "head", 1) for r in blocks if r not in partners}
        partners = {**partners, **more}
        fars = [far_rows(first, kept, others, blocks, partners) for first in early_groups]
        return fars[1:], send_rows(fars[0]), more

    def last_groups(kept, others, blocks, partners, early):
        partners, results, arrived = dict(partners), {}, []
        for first in late_groups:
            for r in group_of(first):
                if r not in partners:
                    partners[r] = swap(blocks[r], "head", 1)
            got = send_rows(far_rows(first, kept, others, blocks, partners), *arrived)
            results[first] = [own_rows(first, kept, others, blocks, partners)] + got
            arrived = got
        owns = [own_rows(first, kept, others, early, partners) for first in early_groups[1:]]
        return results, owns

    early_groups = [f for f in firsts if all(r in early_blocks for r in group_of(f))] or firsts[:1]
    late_groups = [f for f in firsts if f not in early_groups]
    early = {r: held[r] for f in early_groups for r in group_of(f)}
    late = {r: held[r] for f in late_groups for r in group_of(f)}
    fars, got, more = fenced(first_groups, kept, others, early, partners)
    partners = {**partners, **more}
    sent_groups = [got]
    for far in fars:
        sent_groups.append(send_rows(far, *sent_groups[-1]))
    own = own_rows(early_groups[0], [tie(kept[0], *fars)], others, early, partners)
    if late_groups:
        late[late_groups[0]] = tie(late[late_groups[0]], own)
    results, owns = fenced(last_groups, kept, others, late, partners, early)
    for first, own, got in zip(early_groups, [own] + owns, sent_groups):
        results[first] = [own] + got
    pieces = [piece for first in firsts for piece in results[first]]
    return kernel_call(
        assemble_kernel,
        "assemble",
        shape((rows_dev, ctx_size * columns)),
        in_specs=[smem] + [vmem] * len(pieces),
    )(place1 // count, *pieces)


def solution(mesh):
    return jax.shard_map(
        on_device,
        mesh=mesh,
        in_specs=(
            P(("ctx", "head"), None),
            P("ctx", None),
            P("ctx", None),
            P("ctx", "head"),
            P("ctx"),
            P(None, None, "head"),
            P("head"),
            P("head"),
            P("head", "ctx"),
        ),
        out_specs=P(("ctx", "head"), None),
        check_vma=False,
    )
```

profile of v0, /device:TPU:0, one launch (start us, length us, event | category | flops | bytes accessed | tf_op | source)
XLA Modules:
  0.0 146.3 jit_solution(7199054958435258819)
XLA Ops:
  0.0 4.0 %collective-permute-start.22 = (bf16[320,1280]{1,0:T(8,128)(2,1)}, bf16[320,1280]{1,0:T(8,128)(2,1)}, u32[]{:S(2)}, u32[]{:S(2)}) collective-permute-start(bf16[320,1280]{1,0:T(8,128)(2,1)} %bitcast.22), channel_id=1, source_target_pairs={{0,16},{4,20},{8,24},{12,28},{16,0},{20,4},{24,8},{28,12},{1,17},{... | collective-permute-start | bytes 2457608 | tf_op jit(solution)/shard_map/ppermute | solution.py:28
  13.6 13.6 %collective-permute-done.18.refs_1_.refs_6_ = f32[2,20,256]{2,1,0:T(8,128)S(1)} collective-permute-done((f32[2,20,256]{2,1,0:T(8,128)S(1)}, f32[2,20,256]{2,1,0:T(8,128)S(1)}, u32[]{:S(2)}, u32[]{:S(2)}) %collective-permute-start.18) | collective-permute-done | bytes 40992 | tf_op jit(solution)/shard_map/ppermute | solution.py:28
  30.8 3.3 %conditional.5 = (bf16[2,1280,128]{2,1,0:T(8,128)(2,1)}, bf16[1280,128]{1,0:T(8,128)(2,1)S(1)}) conditional(s32[]{:T(128)} %convert_element_type.7, () %tuple.60, (bf16[2,1280,128]{2,1,0:T(8,128)(2,1)S(1)}, f32[2,1280,128]{2,1,0:T(8,128)S(1)}) %tuple.61), branch_computations={%region_0.0_spmd, %region_1.0_spmd} | conditional | bytes 2621496 | solution.py:443
  34.1 33.4 %conditional.6 = (bf16[1312,128]{1,0:T(8,128)(2,1)}, bf16[1312,128]{1,0:T(8,128)(2,1)}, f32[32,128]{1,0:T(8,128)S(1)}, f32[32,128]{1,0:T(8,128)}, f32[32,128]{1,...) conditional(s32[]{:T(128)} %convert_element_type.7, () %tuple.59, ...), branch_computations={%region_2.0_spmd, %region_3.4_spmd} | conditional | flops 12 | bytes 11883085 | solution.py:443
  35.9 8.4 %collective-permute-done.12.refs_0_ = bf16[1280,128]{1,0:T(8,128)(2,1)S(1)} collective-permute-done((bf16[1280,128]{1,0:T(8,128)(2,1)S(1)}, bf16[1280,128]{1,0:T(8,128)(2,1)S(1)}, u32[]{:S(2)}, u32[]{:S(2)}) %collective-permute-start.12) | collective-permute-done | bytes 327712 | tf_op jit(solution)/shard_map/cond/branch_1_fun/ppermute | solution.py:28
  47.7 2.6 %factors.1 = (f32[4,20,256]{2,1,0:T(8,128)S(1)}, f32[5,4,20,256]{3,2,1,0:T(8,128)}, f32[3,4,20,256]{3,2,1,0:T(8,128)S(1)}, f32[26,20,128]{2,1,0:T(8,128)}, bf16[...) custom-call(f32[20,1024]{1,0:T(8,128)S(1)} %copy-done.10, ...), custom_call_target="tpu_custom_call" | custom-call | tf_op jit(solution)/shard_map/cond/branch_1_fun/factors/pallas_call | solution.py:571
  50.4 4.7 %collective-permute-done.13.got_ref = bf16[1312,128]{1,0:T(8,128)(2,1)} collective-permute-done((bf16[1312,128]{1,0:T(8,128)(2,1)S(1)}, bf16[1312,128]{1,0:T(8,128)(2,1)}, u32[]{:S(2)}, u32[]{:S(2)}) %collective-permute-start.13) | collective-permute-done | bytes 335904 | tf_op jit(solution)/shard_map/cond/branch_1_fun/ppermute | solution.py:28
  57.3 8.1 %collective-permute-done.14.got_ref = bf16[1312,128]{1,0:T(8,128)(2,1)} collective-permute-done((bf16[1312,128]{1,0:T(8,128)(2,1)S(1)}, bf16[1312,128]{1,0:T(8,128)(2,1)}, u32[]{:S(2)}, u32[]{:S(2)}) %collective-permute-start.14) | collective-permute-done | bytes 335904 | tf_op jit(solution)/shard_map/cond/branch_1_fun/ppermute | solution.py:28
  68.7 26.7 %conditional.7 = ((bf16[1280,256]{1,0:T(8,128)(2,1)S(1)}, bf16[1280,256]{1,0:T(8,128)(2,1)}, bf16[2,1280,256]{2,1,0:T(8,128)(2,1)})) conditional(s32[]{:T(128)} %convert_element_type.7, () %tuple.58, (bf16[1280,256]{1,0:T(8,128)(2,1)}, f32[20]{0:T(128)}, s32[1]{0:T(128)}, bf16[1280,256]{1,0:T(8,128)(2,1)S(1)}, bf16[1280,256]{1,0:T(8,128)(2,1)}, ...), branch_computations={%region_4.5_spmd, %region_5.6_spmd} | conditional | bytes 3995816 | solution.py:443
  71.8 10.9 %local_levels.1.pre_ref = f32[4,1280,256]{2,1,0:T(8,128)S(1)} custom-call(s32[1]{0:T(128)} %get-tuple-element.153.me_ref, bf16[1280,256]{1,0:T(8,128)(2,1)S(1)} %get-tuple-element.154.refs_0_, bf16[1280,256]{1,0:T(8,128)(2,1)S(1)} %collective-permute-done.1.refs_1_, bf16[1280,256]{1,0:T(8,128)(2,1)} %get-tuple-element.156.refs_2_, ...), custom_call_target="tpu_custom_call" | custom-call | tf_op jit(solution)/shard_map/cond/branch_1_fun/local_levels/pallas_call | solution.py:627
  82.7 8.6 %collective-permute-done.2.state_ref = bf16[1312,128]{1,0:T(8,128)(2,1)S(1)} collective-permute-done((bf16[1312,128]{1,0:T(8,128)(2,1)}, bf16[1312,128]{1,0:T(8,128)(2,1)S(1)}, u32[]{:S(2)}, u32[]{:S(2)}) %collective-permute-start.2) | collective-permute-done | bytes 335904 | tf_op jit(solution)/shard_map/cond/branch_1_fun/ppermute | solution.py:28
  91.3 4.1 %finish.1 = (bf16[1280,256]{1,0:T(8,128)(2,1)S(1)}, bf16[1280,256]{1,0:T(8,128)(2,1)}, bf16[2,1280,256]{2,1,0:T(8,128)(2,1)}) custom-call(s32[1]{0:T(128)} %get-tuple-element.153.me_ref, f32[4,1280,256]{2,1,0:T(8,128)S(1)} %local_levels.1.pre_ref, bf16[4,256,256]{2,1,0:T(8,128)(2,1)S(1)} %get-tuple-element.163.refs_9_.reader_ref, ...), custom_call_target="tpu_custom_call" | custom-call | tf_op jit(solution)/shard_map/cond/branch_1_fun/finish/pallas_call | solution.py:643
  100.9 13.4 %conditional.8 = (bf16[1,640,256]{2,1,0:T(8,128)(2,1)}, bf16[640,256]{1,0:T(8,128)(2,1)}, bf16[320,1280]{1,0:T(8,128)(2,1)}, bf16[320,1280]{1,0:T(8,128)(2,1)}) conditional(s32[]{:T(128)} %convert_element_type.7, () %tuple.66, (bf16[320,1280]{1,0:T(8,128)(2,1)}, bf16[320,1280]{1,0:T(8,128)(2,1)}, s32[1]{0:T(128)}, bf16[1280,256]{1,0:T(8,128)(2,1)}, ...), branch_computations={%region_6.7_spmd, %region_7.8_spmd} | conditional | bytes 7864472 | solution.py:443
  101.4 2.9 %project_far.5 = bf16[1,640,256]{2,1,0:T(8,128)(2,1)S(1)} custom-call(s32[1]{0:T(128)} %get-tuple-element.174.place_ref, bf16[1280,256]{1,0:T(8,128)(2,1)} %get-tuple-element.175.refs_0_, bf16[2,1280,256]{2,1,0:T(8,128)(2,1)S(1)} %get-tuple-element.176.refs_1_, bf16[320,1280]{1,0:T(8,128)(2,1)S(1)} %get-tuple-element.179.refs_2_, ...), custom_call_target="tpu_custom_call" | custom-call | tf_op jit(solution)/shard_map/cond/branch_1_fun/project_far/pallas_call | solution.py:680
  105.8 3.8 %project_far.4 = bf16[1,640,256]{2,1,0:T(8,128)(2,1)} custom-call(s32[1]{0:T(128)} %get-tuple-element.174.place_ref, bf16[1280,256]{1,0:T(8,128)(2,1)} %get-tuple-element.175.refs_0_, bf16[2,1280,256]{2,1,0:T(8,128)(2,1)S(1)} %get-tuple-element.176.refs_1_, bf16[320,1280]{1,0:T(8,128)(2,1)} %get-tuple-element.177.refs_2_, ...), custom_call_target="tpu_custom_call" | custom-call | tf_op jit(solution)/shard_map/cond/branch_1_fun/project_far/pallas_call | solution.py:680
  109.6 4.6 %collective-permute-done.5 = bf16[640,256]{1,0:T(8,128)(2,1)} collective-permute-done((bf16[640,256]{1,0:T(8,128)(2,1)S(1)}, bf16[640,256]{1,0:T(8,128)(2,1)}, u32[]{:S(2)}, u32[]{:S(2)}) %collective-permute-start.5) | collective-permute-done | bytes 327712 | tf_op jit(solution)/shard_map/cond/branch_1_fun/ppermute | solution.py:28
  115.7 3.0 %project_own.7 = f32[1,640,256]{2,1,0:T(8,128)S(1)} custom-call(s32[1]{0:T(128)} %bitcast.9.place_ref, bf16[1280,256]{1,0:T(8,128)(2,1)S(1)} %get-tuple-element.281.refs_0_, bf16[2,1280,256]{2,1,0:T(8,128)(2,1)S(1)} %collective-permute-done.24.refs_1_, bf16[320,1280]{1,0:T(8,128)(2,1)} %bitcast.25, bf16[320,1280]{1,0:T(8,128)(2,1)} %collective-permute-done.20.refs_3_, ...), custom_call_target="tpu_custom_call" | custom-call | tf_op jit(solution)/shard_map/project_own/pallas_call | solution.py:680
  118.8 25.0 %conditional.9 = (f32[640,256]{1,0:T(8,128)S(1)}, bf16[640,256]{1,0:T(8,128)(2,1)S(1)}, f32[640,256]{1,0:T(8,128)S(1)}, bf16[640,256]{1,0:T(8,128)(2,1)}, f32[640,256]{1,0:T(8,128)S(1)}) conditional(s32[]{:T(128)} %convert_element_type.7, () %tuple.72, (bf16[320,1280]{1,0:T(8,128)(2,1)S(1)}, bf16[320,1280]{1,0:T(8,128)(2,1)}, s32[1]{0:T(128)}, ...), branch_computations={%region_8.9_spmd, %region_9.10_spmd} | conditional | bytes 18350416 | solution.py:443
  122.6 2.4 %project_far.6 = bf16[1,640,256]{2,1,0:T(8,128)(2,1)S(1)} custom-call(s32[1]{0:T(128)} %get-tuple-element.183.place_ref, bf16[1280,256]{1,0:T(8,128)(2,1)} %get-tuple-element.188.refs_0_, bf16[2,1280,256]{2,1,0:T(8,128)(2,1)S(1)} %get-tuple-element.185.refs_1_, bf16[320,1280]{1,0:T(8,128)(2,1)S(1)} %get-tuple-element.186.refs_2_, ...), custom_call_target="tpu_custom_call" | custom-call | tf_op jit(solution)/shard_map/cond/branch_1_fun/project_far/pallas_call | solution.py:680
  126.3 2.6 %project_far.7 = bf16[1,640,256]{2,1,0:T(8,128)(2,1)S(1)} custom-call(s32[1]{0:T(128)} %get-tuple-element.183.place_ref, bf16[1280,256]{1,0:T(8,128)(2,1)} %get-tuple-element.188.refs_0_, bf16[2,1280,256]{2,1,0:T(8,128)(2,1)S(1)} %get-tuple-element.185.refs_1_, bf16[320,1280]{1,0:T(8,128)(2,1)} %get-tuple-element.189.refs_2_, ...), custom_call_target="tpu_custom_call" | custom-call | tf_op jit(solution)/shard_map/cond/branch_1_fun/project_far/pallas_call | solution.py:680
  128.9 5.9 %collective-permute-done.8 = bf16[640,256]{1,0:T(8,128)(2,1)S(1)} collective-permute-done((bf16[640,256]{1,0:T(8,128)(2,1)S(1)}, bf16[640,256]{1,0:T(8,128)(2,1)S(1)}, u32[]{:S(2)}, u32[]{:S(2)}) %collective-permute-start.8) | collective-permute-done | bytes 327712 | tf_op jit(solution)/shard_map/cond/branch_1_fun/ppermute | solution.py:28
  136.0 2.9 %project_own.6 = f32[1,640,256]{2,1,0:T(8,128)S(1)} custom-call(s32[1]{0:T(128)} %get-tuple-element.183.place_ref, bf16[1280,256]{1,0:T(8,128)(2,1)S(1)} %get-tuple-element.184.refs_0_, bf16[2,1280,256]{2,1,0:T(8,128)(2,1)S(1)} %get-tuple-element.185.refs_1_, bf16[320,1280]{1,0:T(8,128)(2,1)} %get-tuple-element.192.refs_2_, ...), custom_call_target="tpu_custom_call" | custom-call | tf_op jit(solution)/shard_map/cond/branch_1_fun/project_own/pallas_call | solution.py:680
  141.1 2.5 %project_own.5 = f32[1,640,256]{2,1,0:T(8,128)S(1)} custom-call(s32[1]{0:T(128)} %get-tuple-element.183.place_ref, bf16[1280,256]{1,0:T(8,128)(2,1)S(1)} %get-tuple-element.184.refs_0_, bf16[2,1280,256]{2,1,0:T(8,128)(2,1)S(1)} %get-tuple-element.185.refs_1_, bf16[320,1280]{1,0:T(8,128)(2,1)} %get-tuple-element.189.refs_2_, ...), custom_call_target="tpu_custom_call" | custom-call | tf_op jit(solution)/shard_map/cond/branch_1_fun/project_own/pallas_call | solution.py:680
  143.8 2.6 %assemble.1 = bf16[256,2560]{1,0:T(8,128)(2,1)} custom-call(s32[1]{0:T(128)S(6)} %select_n.12.place_ref, f32[640,256]{1,0:T(8,128)S(1)} %bitcast.17, bf16[640,256]{1,0:T(8,128)(2,1)} %get-tuple-element.282.refs_1_, f32[640,256]{1,0:T(8,128)S(1)} %get-tuple-element.288.refs_2_, bf16[640,256]{1,0:T(8,128)(2,1)S(1)} %get-tuple-element.289.refs_3_, ...), custom_call_target="tpu_custom_call" | custom-call | tf_op jit(solution)/shard_map/assemble/pallas_call | solution.py:742
  (99 shorter events, 47.9 us)
Async XLA Ops:
  0.0 67.6 %collective-permute-start.22 = (bf16[320,1280]{1,0:T(8,128)(2,1)}, bf16[320,1280]{1,0:T(8,128)(2,1)}, u32[]{:S(2)}, u32[]{:S(2)}) collective-permute-start(bf16[320,1280]{1,0:T(8,128)(2,1)} %bitcast.22), channel_id=1, source_target_pairs={{0,16},{4,20},{8,24},{12,28},{16,0},{20,4},{24,8},{28,12},{1,17},{... | collective-permute-start | bytes 2457608 | tf_op jit(solution)/shard_map/ppermute | solution.py:28
  4.0 63.6 %collective-permute-start.20 = (bf16[320,1280]{1,0:T(8,128)(2,1)}, bf16[320,1280]{1,0:T(8,128)(2,1)}, u32[]{:S(2)}, u32[]{:S(2)}) collective-permute-start(bf16[320,1280]{1,0:T(8,128)(2,1)} %bitcast.23), channel_id=1, source_target_pairs={{0,4},{4,0},{8,12},{12,8},{16,20},{20,16},{24,28},{28,24},{1,5},{5... | collective-permute-start | bytes 2457608 | tf_op jit(solution)/shard_map/ppermute | solution.py:28
  5.5 62.1 %collective-permute-start.21 = (bf16[320,1280]{1,0:T(8,128)(2,1)}, bf16[320,1280]{1,0:T(8,128)(2,1)S(1)}, u32[]{:S(2)}, u32[]{:S(2)}) collective-permute-start(bf16[320,1280]{1,0:T(8,128)(2,1)} %bitcast.24), channel_id=1, source_target_pairs={{0,8},{4,12},{8,0},{12,4},{16,24},{20,28},{24,16},{28,20},{1,9},{5... | collective-permute-start | bytes 2457608 | tf_op jit(solution)/shard_map/ppermute | solution.py:28
  10.5 23.6 %collective-permute-start.17 = (bf16[1280,256]{1,0:T(8,128)(2,1)S(1)}, bf16[1280,256]{1,0:T(8,128)(2,1)}, u32[]{:S(2)}, u32[]{:S(2)}) collective-permute-start(bf16[1280,256]{1,0:T(8,128)(2,1)S(1)} %get-tuple-element.247.refs_2_), channel_id=1, source_target_pairs={{0,2},{1,3},{2,0},{3,1},{4,6},{5,7},{6,4},{7,5},{8,10},{9,11},{10,... | collective-permute-start | bytes 1966088 | tf_op jit(solution)/shard_map/ppermute | solution.py:28
  13.0 14.2 %collective-permute-start.18 = (f32[2,20,256]{2,1,0:T(8,128)S(1)}, f32[2,20,256]{2,1,0:T(8,128)S(1)}, u32[]{:S(2)}, u32[]{:S(2)}) collective-permute-start(f32[2,20,256]{2,1,0:T(8,128)S(1)} %get-tuple-element.251), channel_id=1, source_target_pairs={{0,2},{1,3},{2,0},{3,1},{4,6},{5,7},{6,4},{7,5},{8,10},{9,11},{10,... | collective-permute-start | bytes 122888 | tf_op jit(solution)/shard_map/ppermute | solution.py:28
  34.1 12.0 %collective-permute-start.15 = (bf16[1280,256]{1,0:T(8,128)(2,1)}, bf16[1280,256]{1,0:T(8,128)(2,1)}, u32[]{:S(2)}, u32[]{:S(2)}) collective-permute-start(bf16[1280,256]{1,0:T(8,128)(2,1)} %get-tuple-element.151), channel_id=1, source_target_pairs={{0,1},{1,0},{2,3},{3,2},{4,5},{5,4},{6,7},{7,6},{8,9},{9,8},{10,11... | collective-permute-start | bytes 1966088 | tf_op jit(solution)/shard_map/cond/branch_1_fun/ppermute | solution.py:28
  34.4 10.0 %collective-permute-start.12 = (bf16[1280,128]{1,0:T(8,128)(2,1)S(1)}, bf16[1280,128]{1,0:T(8,128)(2,1)S(1)}, u32[]{:S(2)}, u32[]{:S(2)}) collective-permute-start(bf16[1280,128]{1,0:T(8,128)(2,1)S(1)} %get-tuple-element.124), channel_id=1, source_target_pairs={{0,2},{1,3},{2,0},{3,1},{4,6},{5,7},{6,4},{7,5},{8,10},{9,11},{10,... | collective-permute-start | bytes 983048 | tf_op jit(solution)/shard_map/cond/branch_1_fun/ppermute | solution.py:28
  45.5 9.5 %collective-permute-start.13 = (bf16[1312,128]{1,0:T(8,128)(2,1)S(1)}, bf16[1312,128]{1,0:T(8,128)(2,1)}, u32[]{:S(2)}, u32[]{:S(2)}) collective-permute-start(bf16[1312,128]{1,0:T(8,128)(2,1)S(1)} %get-tuple-element.125), channel_id=1, source_target_pairs={{0,4},{4,0},{8,12},{12,8},{16,20},{20,16},{24,28},{28,24},{1,5},{5... | collective-permute-start | bytes 1007624 | tf_op jit(solution)/shard_map/cond/branch_1_fun/ppermute | solution.py:28
  46.1 21.4 %collective-permute-start.16 = (bf16[1280,256]{1,0:T(8,128)(2,1)}, bf16[1280,256]{1,0:T(8,128)(2,1)}, u32[]{:S(2)}, u32[]{:S(2)}) collective-permute-start(bf16[1280,256]{1,0:T(8,128)(2,1)} %collective-permute-done.15), channel_id=1, source_target_pairs={{0,2},{1,3},{2,0},{3,1},{4,6},{5,7},{6,4},{7,5},{8,10},{9,11},{10,... | collective-permute-start | bytes 1966088 | tf_op jit(solution)/shard_map/cond/branch_1_fun/ppermute | solution.py:28
  56.8 8.5 %collective-permute-start.14 = (bf16[1312,128]{1,0:T(8,128)(2,1)S(1)}, bf16[1312,128]{1,0:T(8,128)(2,1)}, u32[]{:S(2)}, u32[]{:S(2)}) collective-permute-start(bf16[1312,128]{1,0:T(8,128)(2,1)S(1)} %get-tuple-element.136), channel_id=1, source_target_pairs={{0,8},{4,12},{8,0},{12,4},{16,24},{20,28},{24,16},{28,20},{1,9},{5... | collective-permute-start | bytes 1007624 | tf_op jit(solution)/shard_map/cond/branch_1_fun/ppermute | solution.py:28
  67.6 28.3 %collective-permute-start.23 = (bf16[320,1280]{1,0:T(8,128)(2,1)}, bf16[320,1280]{1,0:T(8,128)(2,1)}, u32[]{:S(2)}, u32[]{:S(2)}) collective-permute-start(bf16[320,1280]{1,0:T(8,128)(2,1)} %collective-permute-done.22), channel_id=1, source_target_pairs={{0,4},{4,0},{8,12},{12,8},{16,20},{20,16},{24,28},{28,24},{1,5},{5... | collective-permute-start | bytes 2457608 | tf_op jit(solution)/shard_map/ppermute | solution.py:28
  68.2 27.7 %collective-permute-start.27 = (bf16[320,1280]{1,0:T(8,128)(2,1)}, bf16[320,1280]{1,0:T(8,128)(2,1)}, u32[]{:S(2)}, u32[]{:S(2)}) collective-permute-start(bf16[320,1280]{1,0:T(8,128)(2,1)} %collective-permute-done.22), channel_id=1, source_target_pairs={{0,8},{4,12},{8,0},{12,4},{16,24},{20,28},{24,16},{28,20},{1,9},{5... | collective-permute-start | bytes 2457608 | tf_op jit(solution)/shard_map/ppermute | solution.py:28
  68.8 22.5 %collective-permute-start.2 = (bf16[1312,128]{1,0:T(8,128)(2,1)}, bf16[1312,128]{1,0:T(8,128)(2,1)S(1)}, u32[]{:S(2)}, u32[]{:S(2)}) collective-permute-start(bf16[1312,128]{1,0:T(8,128)(2,1)} %get-tuple-element.172), channel_id=1, source_target_pairs={{0,16},{4,20},{8,24},{12,28},{16,0},{20,4},{24,8},{28,12},{1,17},{... | collective-permute-start | bytes 1007624 | tf_op jit(solution)/shard_map/cond/branch_1_fun/ppermute | solution.py:28
  95.4 5.5 %collective-permute-start.24 = (bf16[2,1280,256]{2,1,0:T(8,128)(2,1)}, bf16[2,1280,256]{2,1,0:T(8,128)(2,1)S(1)}, u32[]{:S(2)}, u32[]{:S(2)}) collective-permute-start(bf16[2,1280,256]{2,1,0:T(8,128)(2,1)} %get-tuple-element.277), channel_id=1, source_target_pairs={{0,1},{1,0},{2,3},{3,2},{4,5},{5,4},{6,7},{7,6},{8,9},{9,8},{10,11... | collective-permute-start | bytes 3932168 | tf_op jit(solution)/shard_map/ppermute | solution.py:28
  95.4 5.3 %collective-permute-start.26 = (bf16[320,1280]{1,0:T(8,128)(2,1)}, bf16[320,1280]{1,0:T(8,128)(2,1)}, u32[]{:S(2)}, u32[]{:S(2)}) collective-permute-start(bf16[320,1280]{1,0:T(8,128)(2,1)} %collective-permute-done.20.refs_3_), channel_id=1, source_target_pairs={{0,1},{1,0},{2,3},{3,2},{4,5},{5,4},{6,7},{7,6},{8,9},{9,8},{10,11... | collective-permute-start | bytes 2457608 | tf_op jit(solution)/shard_map/ppermute | solution.py:28
  95.9 5.0 %collective-permute-start.25 = (bf16[320,1280]{1,0:T(8,128)(2,1)S(1)}, bf16[320,1280]{1,0:T(8,128)(2,1)}, u32[]{:S(2)}, u32[]{:S(2)}) collective-permute-start(bf16[320,1280]{1,0:T(8,128)(2,1)S(1)} %bitcast.26), channel_id=1, source_target_pairs={{0,1},{1,0},{2,3},{3,2},{4,5},{5,4},{6,7},{7,6},{8,9},{9,8},{10,11... | collective-permute-start | bytes 2457608 | tf_op jit(solution)/shard_map/ppermute | solution.py:28
  95.9 22.8 %collective-permute-start.29 = (bf16[320,1280]{1,0:T(8,128)(2,1)}, bf16[320,1280]{1,0:T(8,128)(2,1)}, u32[]{:S(2)}, u32[]{:S(2)}) collective-permute-start(bf16[320,1280]{1,0:T(8,128)(2,1)} %collective-permute-done.27), channel_id=1, source_target_pairs={{0,4},{4,0},{8,12},{12,8},{16,20},{20,16},{24,28},{28,24},{1,5},{5... | collective-permute-start | bytes 2457608 | tf_op jit(solution)/shard_map/ppermute | solution.py:28
  97.4 21.3 %collective-permute-start.28 = (bf16[320,1280]{1,0:T(8,128)(2,1)}, bf16[320,1280]{1,0:T(8,128)(2,1)}, u32[]{:S(2)}, u32[]{:S(2)}) collective-permute-start(bf16[320,1280]{1,0:T(8,128)(2,1)} %collective-permute-done.20.refs_3_), channel_id=1, source_target_pairs={{0,8},{4,12},{8,0},{12,4},{16,24},{20,28},{24,16},{28,20},{1,9},{5... | collective-permute-start | bytes 2457608 | tf_op jit(solution)/shard_map/ppermute | solution.py:28
  104.3 10.0 %collective-permute-start.5 = (bf16[640,256]{1,0:T(8,128)(2,1)S(1)}, bf16[640,256]{1,0:T(8,128)(2,1)}, u32[]{:S(2)}, u32[]{:S(2)}) collective-permute-start(bf16[640,256]{1,0:T(8,128)(2,1)S(1)} %bitcast.20), channel_id=1, source_target_pairs={{0,2},{1,3},{2,0},{3,1},{4,6},{5,7},{6,4},{7,5},{8,10},{9,11},{10,... | collective-permute-start | bytes 983048 | tf_op jit(solution)/shard_map/cond/branch_1_fun/ppermute | solution.py:28
  114.3 29.5 %collective-permute-start.30 = (bf16[640,256]{1,0:T(8,128)(2,1)}, bf16[640,256]{1,0:T(8,128)(2,1)S(1)}, u32[]{:S(2)}, u32[]{:S(2)}) collective-permute-start(bf16[640,256]{1,0:T(8,128)(2,1)} %bitcast.14), channel_id=1, source_target_pairs={{0,2},{1,3},{2,0},{3,1},{4,6},{5,7},{6,4},{7,5},{8,10},{9,11},{10,... | collective-permute-start | bytes 983048 | tf_op jit(solution)/shard_map/ppermute | solution.py:28
  119.4 6.9 %collective-permute-start.10 = (bf16[320,1280]{1,0:T(8,128)(2,1)}, bf16[320,1280]{1,0:T(8,128)(2,1)S(1)}, u32[]{:S(2)}, u32[]{:S(2)}) collective-permute-start(bf16[320,1280]{1,0:T(8,128)(2,1)} %get-tuple-element.190.refs_3_), channel_id=1, source_target_pairs={{0,1},{1,0},{2,3},{3,2},{4,5},{5,4},{6,7},{7,6},{8,9},{9,8},{10,11... | collective-permute-start | bytes 2457608 | tf_op jit(solution)/shard_map/cond/branch_1_fun/ppermute | solution.py:28
  119.4 6.8 %collective-permute-start.9 = (bf16[320,1280]{1,0:T(8,128)(2,1)}, bf16[320,1280]{1,0:T(8,128)(2,1)S(1)}, u32[]{:S(2)}, u32[]{:S(2)}) collective-permute-start(bf16[320,1280]{1,0:T(8,128)(2,1)} %get-tuple-element.189.refs_2_), channel_id=1, source_target_pairs={{0,1},{1,0},{2,3},{3,2},{4,5},{5,4},{6,7},{7,6},{8,9},{9,8},{10,11... | collective-permute-start | bytes 2457608 | tf_op jit(solution)/shard_map/cond/branch_1_fun/ppermute | solution.py:28
  124.9 9.8 %collective-permute-start.8 = (bf16[640,256]{1,0:T(8,128)(2,1)S(1)}, bf16[640,256]{1,0:T(8,128)(2,1)S(1)}, u32[]{:S(2)}, u32[]{:S(2)}) collective-permute-start(bf16[640,256]{1,0:T(8,128)(2,1)S(1)} %bitcast.21), channel_id=1, source_target_pairs={{0,2},{1,3},{2,0},{3,1},{4,6},{5,7},{6,4},{7,5},{8,10},{9,11},{10,... | collective-permute-start | bytes 983048 | tf_op jit(solution)/shard_map/cond/branch_1_fun/ppermute | solution.py:28
  134.8 9.0 %collective-permute-start.11 = (bf16[640,256]{1,0:T(8,128)(2,1)S(1)}, bf16[640,256]{1,0:T(8,128)(2,1)}, u32[]{:S(2)}, u32[]{:S(2)}) collective-permute-start(bf16[640,256]{1,0:T(8,128)(2,1)S(1)} %bitcast.19), channel_id=1, source_target_pairs={{0,2},{1,3},{2,0},{3,1},{4,6},{5,7},{6,4},{7,5},{8,10},{9,11},{10,... | collective-permute-start | bytes 983048 | tf_op jit(solution)/shard_map/cond/branch_1_fun/ppermute | solution.py:28
  (22 other events, 147.3 us)
where the time goes:
time: 147 us; the launch traced here: 146 us
  waiting for transfers between devices  62.1 us (42%)
  Pallas kernels  53.5 us (36%)
  starting transfers between devices  26.8 us (18%)
  local copies, waits for them, and re-layouts  3.47 us (2%)
    ppermute x31, waiting for transfers between devices, swap(): return lax.ppermute(value, axis, pairs)  62.1 us
    ppermute x31, starting transfers between devices, swap(): return lax.ppermute(value, axis, pairs)  26.8 us
    pallas_call x8, Pallas kernels, project(): kernel_call(project_kernel, name, shape((rows, count * columns, rows_dev)...  22.2 us
    pallas_call x1, Pallas kernels, read_levels(): kernel_call(functools.partial(local_kernel, near), 'local_levels', shape(...  10.9 us
    pallas_call x1, Pallas kernels, read_levels(): kernel_call(functools.partial(finish_kernel, half), 'finish', tuple([shap...  4.06 us
    pallas_call x2, Pallas kernels, step(): kernel_call(functools.partial(merge_kernel, bit, head_count), 'merge', (s...  4 us
  transfers between devices with their start and end apart: 31, of which 15 were waited for; matrix products, arithmetic and copies ran while one was open for 1% of the time, Pallas kernels for 35%

commit v1 on v0

--- a/solution.py
+++ b/solution.py
@@ -182,17 +182,25 @@
         merge_ref[i] = jnp.broadcast_to(jnp.exp(starts[c + 1] - starts[first]), (head_count, LANES))
 
 
-def partial_state_kernel(count, *refs):
-    value_refs, refs = refs[:count], refs[count:]
+def load(refs, pieces, at):
+    parts = [refs[i][at, first : first + count] for i, first, count in pieces]
+    return parts[0] if len(parts) == 1 else jnp.concatenate(parts, axis=1)
+
+
+def partial_state_kernel(pieces, *refs):
+    count = len(pieces)
+    arrays = sum(len(parts) for parts in pieces)
+    value_refs, refs = refs[:arrays], refs[arrays:]
     fade_refs, (in_ref, keep_ref, send_ref, faded) = refs[:count], refs[count:]
     own_in = in_ref[...]
     for r in [*range(1, count, 2), *range(0, count, 2)]:
         fade = fade_refs[r][...].reshape(fade_refs[r].shape[-2:])
         head_count = fade.shape[0]
-        width = value_refs[r].shape[0] // head_count
+        width = value_refs[0].shape[0] // head_count
         for h in range(head_count):
             at = head_rows(h, width)
-            faded[at, :] = (fade[h : h + 1, :] * value_refs[r][at, :].astype(F32)).astype(BF16)
+            value = load(value_refs, pieces[r], at).astype(F32)
+            faded[at, :] = (fade[h : h + 1, :] * value).astype(BF16)
         state = dot(faded[...], own_in)
         if r % 2 == 1:
             send_ref[r // 2] = state.astype(BF16)
@@ -252,14 +260,16 @@
     pack_state(sent_ref, next_running_ref[...], joined)
 
 
-def local_kernel(near, me_ref, *refs):
+def local_kernel(near, pieces, me_ref, *refs):
     groups = refs[-1].shape[0]
-    value_refs, refs = refs[:groups], refs[groups:]
+    arrays = 1 + max(i for parts in pieces for i, _, _ in parts)
+    value_refs, refs = refs[:arrays], refs[arrays:]
     lift_ref, read_ref, merge_ref, score_ref, masked_ref, reader_ref, pair_ref = refs[:7]
     skip_ref, cross_ref, *refs = refs[7:]
     factor_refs, state_refs, refs = refs[:near], refs[near : 2 * near], refs[2 * near :]
     pre_ref, lifted, sums, operand, pairs_ref, nodes = refs
     channels, group_rows = value_refs[0].shape
+    assert len(pieces) == groups
     head_count = lift_ref.shape[1]
     width = channels // head_count
     me = me_ref[0]
@@ -268,11 +278,12 @@
     state_size = reader_ref.shape[1] // 2
     place = {kind: i for i, kind in enumerate(merge_rows(stretches))}
     heads = [(h, head_rows(h, width)) for h in range(head_count)]
-    for r, value_ref in enumerate(value_refs):
+    for r in range(groups):
         g = me ^ r
         lift = lift_ref[g]
         for h, at in heads:
-            lifted[at, :] = (lift[h : h + 1, :] * value_ref[at, :].astype(F32)).astype(BF16)
+            value = load(value_refs, pieces[r], at).astype(F32)
+            lifted[at, :] = (lift[h : h + 1, :] * value).astype(BF16)
         direct = dot(lifted[...], score_ref[g, 0]) + dot(lifted[...], score_ref[g, 1])
         read = read_ref[0, g]
         terms = []
@@ -282,7 +293,7 @@
             terms.append((scale, gained))
         for h, at in heads:
             total = read[h : h + 1, :] * direct[at, :]
-            total = total + skip_ref[h : h + 1, :] * value_ref[at, :].astype(F32)
+            total = total + skip_ref[h : h + 1, :] * load(value_refs, pieces[r], at).astype(F32)
             for scale, gained in terms:
                 total = total + scale[h : h + 1, :] * gained[at, :]
             pre_ref[g, at, :] = total
@@ -471,22 +482,30 @@
     )(side_fade, *got_fades)
     sides = swap(sides, "head", 1)
 
+    early = rows_dev // 2
+    cuts = [(r, first, early) for r in (2,) for first in (0, early)]
+    cuts = [(0, 0, rows_dev), (1, 0, rows_dev)] + cuts
+    cuts += [(r, 0, rows_dev) for r in range(3, heads_size)]
     portions = kernel_call(
         split_kernel,
         "split_values",
-        tuple([shape((features, rows_dev))] * heads_size),
+        tuple(shape((features, count)) for _, _, count in cuts),
         grid_spec=pltpu.PrefetchScalarGridSpec(
             num_scalar_prefetch=1,
             grid=(1,),
             in_specs=[
-                pl.BlockSpec((rows_dev, features), lambda i, m, r=r: (0, m[0] ^ r))
-                for r in range(heads_size)
+                pl.BlockSpec((count, features), lambda i, m, r=r, at=first // count: (at, m[0] ^ r))
+                for r, first, count in cuts
             ],
-            out_specs=[whole((features, rows_dev))] * heads_size,
+            out_specs=[whole((features, count)) for _, _, count in cuts],
         ),
-    )(me1, *[values] * heads_size)
-    value_head = swap(portions[2], "head", 2)
-
+    )(me1, *[values] * len(cuts))
+    portion = {(r, first): array for (r, first, _), array in zip(cuts, portions)}
+    value_head = swap(tie(portion[2, 0], *got_fades), "head", 2)
+
+    pieces = [[] for _ in range(heads_size)]
+    for i, (r, _, count) in enumerate(cuts):
+        pieces[r].append((i, 0, count))
     fades, fade_specs = [], []
     for r in range(heads_size):
         if r == 0:
@@ -496,13 +515,13 @@
             fades.append(sides if r % 2 else got_fades[r // 2 - 1])
             fade_specs.append(part(fades[-1], r // 2 if r % 2 else 0))
     keep, send = kernel_call(
-        lambda me_ref, *refs: partial_state_kernel(heads_size, *refs),
+        lambda me_ref, *refs: partial_state_kernel(pieces, *refs),
         "partial_states",
         (shape((half, features, state_size), F32), shape((half, features, state_size))),
         grid_spec=pltpu.PrefetchScalarGridSpec(
             num_scalar_prefetch=1,
             grid=(1,),
-            in_specs=[whole((features, rows_dev))] * heads_size
+            in_specs=[whole(array.shape) for array in portions]
             + fade_specs
             + [pl.BlockSpec((rows_dev, state_size), lambda i, m: (m[0], 0))],
             out_specs=[whole((half, features, state_size))] * 2,
@@ -542,30 +561,20 @@
             in_specs=[smem] + [vmem] * 4,
         )(place1, running, total, offset, got)
 
-    def near_chain(
-        keep, core_states, far_states, total, decays, level_class, level_table, state_in, state_out, portion
+    def chip_sum(
+        keep, core_states, far_states, total, decays, level_class, level_table, state_in, state_out,
+        second, crossing,
     ):
         got_states, latest = [], []
         for i, far in enumerate(far_states):
             latest = [swap(tie(far, *latest), "head", 2 * (i + 1))]
             got_states += latest
-        running, sent = kernel_call(
-            first_kernel,
-            "first_state",
-            (shape((features, state_size), F32), shape((features + extra, state_size))),
-            grid=(1,),
-            in_specs=[part(keep, 0), part(core_states, 0), whole(total.shape)]
-            + [whole((features, state_size))] * len(got_states),
-            out_specs=(whole((features, state_size)), whole((features + extra, state_size))),
-        )(keep, core_states, total, *got_states)
-        moved, passed, after = {}, {}, []
-        for r, array in portion.items():
-            moved[r] = swap(tie(array, *after), "head", 1)
-            after = [moved[r]]
-        after = [running]
-        for r, array in moved.items():
-            passed[r] = swap(tie(array, *after), "head", r - 1)
-            after = [passed[r]]
+        moved, after = [], []
+        for array in crossing:
+            moved.append(swap(tie(array, *after), "head", 1))
+            after = moved[-1:]
+        if moved:
+            moved[0] = jnp.concatenate([second, moved[0]], axis=1)
         table = jnp.transpose(level_table, (1, 2, 0))
         table = jnp.pad(table, ((0, 0), (0, padded - head_count), (0, 0)))
         tables = kernel_call(
@@ -582,31 +591,50 @@
                 shape((heads_size, pair_rows, rows_dev)),
             ),
         )(
-            tie(decays, running),
+            decays,
             level_class.reshape(1, tokens),
             table.reshape(levels * padded, classes),
             state_in,
             state_out,
         )
+        got_states[-1] = tie(got_states[-1], tables[0], *moved)
+        running, sent = kernel_call(
+            first_kernel,
+            "first_state",
+            (shape((features, state_size), F32), shape((features + extra, state_size))),
+            grid=(1,),
+            in_specs=[part(keep, 0), part(core_states, 0), whole(total.shape)]
+            + [whole((features, state_size))] * len(got_states),
+            out_specs=(whole((features, state_size)), whole((features + extra, state_size))),
+        )(keep, core_states, total, *got_states)
+        return running, sent, tables, moved
+
+    def near_steps(running, total, sent):
         offset = jnp.zeros((extra, LANES), F32)
         factors = [jnp.broadcast_to((position % 2).astype(F32), (extra, LANES))]
         states = []
         for bit in range(near):
-            got = swap(sent, "ctx", 2**bit)
-            states.append(tie(got, tables[0]) if bit == 0 else got)
+            states.append(swap(sent, "ctx", 2**bit))
             running, total, offset, factor, sent = step(bit, running, total, offset, states[-1])
             factors.append(factor)
-        return states, factors, sent, tables, passed
-
-    states, factors, sent, tables, passed = fenced(
-        near_chain, keep, core_states, tie(far_states, value_head), total, decays, level_class,
-        level_table, state_in, state_out, {r: portions[r] for r in range(3, heads_size, 2)},
+        return states, factors, sent
+
+    running, sent, tables, moved = fenced(
+        chip_sum, keep, core_states, tie(far_states, value_head), total, decays, level_class,
+        level_table, state_in, state_out, portion[2, early],
+        [portion[r, 0] for r in range(3, heads_size, 2)],
     )
-    states, passed = list(states), dict(passed)
-    passed[2] = value_head
+    passed, after = {}, []
+    for i, array in enumerate(moved):
+        passed[2 * i + 3] = swap(tie(array, *after), "head", 2 * i + 2)
+        after = [passed[2 * i + 3]]
+    for r in range(4, heads_size, 2):
+        passed[r] = swap(tie(portion[r, 0], *after), "head", r)
+        after = [passed[r]]
+    states, factors, sent = fenced(near_steps, running, total, sent)
+    states = list(states)
     sent = tie(sent, *[held[2**bit] for bit in range(ctx_bits)])
-    for r in range(4, heads_size, 2):
-        passed[r] = swap(tie(portions[r], sent), "head", r)
+    last_state = swap(sent, "ctx", 2**near)
 
     for r in range(2, ctx_size):
         low = r & -r
@@ -620,46 +648,47 @@
     skips = jnp.broadcast_to(skip_gain[:, None], (head_count, rows_dev))
     gains = norm_gain[:, None]
 
-    def read_levels(sent, tables, factors, states, arrays, skips, gains):
-        lift, read, cross, merge, scores, masked, readers, pairs = tables
-        state = swap(sent, "ctx", 2**near)
-        arrays = [arrays[0], swap(arrays[1], "head", 1)] + list(arrays[2:])
-        pre = kernel_call(
-            functools.partial(local_kernel, near),
-            "local_levels",
-            shape((heads_size, features, rows_dev), F32),
-            in_specs=[smem] + [vmem] * (heads_size + 9 + 2 * near),
-            scratch_shapes=[
-                pltpu.VMEM((features, rows_dev), BF16),
-                pltpu.VMEM((max(local, 1), features, state_size), F32),
-                pltpu.VMEM((max(local, 1), features, 2 * state_size), BF16),
-                pltpu.VMEM((features, pair_rows), BF16),
-                pltpu.VMEM((heads_size, features, per_group * state_size), F32),
-            ],
-        )(
-            me1, *arrays, lift, read, merge, scores, masked, readers, pairs, skips, cross,
-            *factors[:near], *states,
-        )
-        return kernel_call(
-            functools.partial(finish_kernel, half),
-            "finish",
-            tuple([shape((features, rows_dev))] * half + [shape((half, features, rows_dev))]),
-            grid=(1,),
-            in_specs=[
-                smem,
-                whole(pre.shape),
-                whole(readers.shape),
-                part(cross, near),
-                whole((extra, LANES)),
-                whole((features + extra, state_size)),
-                whole((features, 1)),
-            ],
-            out_specs=[whole((features, rows_dev))] * half + [whole((half, features, rows_dev))],
-        )(me1, pre, readers, cross, factors[near], state, gains)
-
-    arrays = [portions[0], portions[1]] + [passed[r] for r in range(2, heads_size)]
-    *kept, sides = fenced(read_levels, sent, tables, factors, states, arrays, skips, gains)
-
+    lift, read, cross, merge, scores, masked, readers, pairs = tables
+    arrays = [portion[0, 0], swap(tie(portion[1, 0], sent), "head", 1), value_head]
+    pieces = [[(0, 0, rows_dev)], [(1, 0, rows_dev)], [(2, 0, early)]]
+    for r in range(3, heads_size):
+        first = rows_dev - early if r == 3 else 0
+        if r == 3:
+            pieces[2].append((len(arrays), 0, first))
+        pieces.append([(len(arrays), first, rows_dev)])
+        arrays.append(passed[r])
+    pre = kernel_call(
+        functools.partial(local_kernel, near, pieces),
+        "local_levels",
+        shape((heads_size, features, rows_dev), F32),
+        in_specs=[smem] + [vmem] * (len(arrays) + 9 + 2 * near),
+        scratch_shapes=[
+            pltpu.VMEM((features, rows_dev), BF16),
+            pltpu.VMEM((max(local, 1), features, state_size), F32),
+            pltpu.VMEM((max(local, 1), features, 2 * state_size), BF16),
+            pltpu.VMEM((features, pair_rows), BF16),
+            pltpu.VMEM((heads_size, features, per_group * state_size), F32),
+        ],
+    )(
+        me1, *arrays, lift, read, merge, scores, masked, readers, pairs, skips, cross,
+        *factors[:near], *states,
+    )
+    *kept, sides = kernel_call(
+        functools.partial(finish_kernel, half),
+        "finish",
+        tuple([shape((features, rows_dev))] * half + [shape((half, features, rows_dev))]),
+        grid=(1,),
+        in_specs=[
+            smem,
+            whole(pre.shape),
+            whole(readers.shape),
+            part(cross, near),
+            whole((extra, LANES)),
+            whole((features + extra, state_size)),
+            whole((features, 1)),
+        ],
+        out_specs=[whole((features, rows_dev))] * half + [whole((half, features, rows_dev))],
+    )(me1, pre, readers, cross, factors[near], last_state, gains)
     early_blocks = set(held)
     done = [held[r] for r in held if r not in (0, 1)] + [kept[0]]
     held[3] = swap(tie(held[1], *done), "ctx", 2)

time: 147 us -> 134 us (0.912)
  waiting for transfers between devices: 62.1 us -> 51.2 us
  starting transfers between devices: 26.8 us -> 20.7 us
  local copies, waits for them, and re-layouts: 3.47 us -> 6.36 us
    ppermute x31, waiting for transfers between devices: 62.1 us -> 51.2 us  [swap(): return lax.ppermute(value, axis, pairs)]
    ppermute x31, starting transfers between devices: 26.8 us -> 20.7 us  [swap(): return lax.ppermute(value, axis, pairs)]
    cond x14 -> x7, local copies, waits for them, and re-layouts: 0.03 us -> 2.48 us
  transfers between devices with their start and end apart: 31 -> 31, of which waited for: 15 -> 16; matrix products, arithmetic and copies ran while one was open for 1% -> 3% of each run, Pallas kernels for 35% -> 39%
where the time goes in v1:
time: 134 us; the launch traced here: 133 us
  Pallas kernels  54.4 us (41%)
  waiting for transfers between devices  51.2 us (38%)
  starting transfers between devices  20.7 us (15%)
  local copies, waits for them, and re-layouts  6.36 us (5%)
    ppermute x31, waiting for transfers between devices, swap(): return lax.ppermute(value, axis, pairs)  51.2 us
    pallas_call x8, Pallas kernels, project(): kernel_call(project_kernel, name, shape((rows, count * columns, rows_dev)...  22.6 us
    ppermute x31, starting transfers between devices, swap(): return lax.ppermute(value, axis, pairs)  20.7 us
    pallas_call x1, Pallas kernels, on_device(): kernel_call(functools.partial(local_kernel, near, pieces), 'local_levels'...  11 us
    pallas_call x2, Pallas kernels, step(): kernel_call(functools.partial(merge_kernel, bit, head_count), 'merge', (s...  4.19 us
    pallas_call x1, Pallas kernels, chip_sum(): kernel_call(functools.partial(factors_kernel, levels, heads_size), 'facto...  3.69 us
  transfers between devices with their start and end apart: 31, of which 16 were waited for; matrix products, arithmetic and copies ran while one was open for 3% of the time, Pallas kernels for 39%

profile of v1, /device:TPU:0, one launch (start us, length us, event | category | flops | bytes accessed | tf_op | source)
XLA Modules:
  0.0 132.9 jit_solution(15503280082169695244)
XLA Ops:
  0.0 4.0 %collective-permute-start.19 = (bf16[320,1280]{1,0:T(8,128)(2,1)}, bf16[320,1280]{1,0:T(8,128)(2,1)}, u32[]{:S(2)}, u32[]{:S(2)}) collective-permute-start(bf16[320,1280]{1,0:T(8,128)(2,1)} %bitcast.22), channel_id=1, source_target_pairs={{0,16},{4,20},{8,24},{12,28},{16,0},{20,4},{24,8},{28,12},{1,17},{... | collective-permute-start | bytes 2457608 | tf_op jit(solution)/shard_map/ppermute | solution.py:28
  17.9 3.3 %conditional.5 = (bf16[2,1280,128]{2,1,0:T(8,128)(2,1)}, bf16[1280,128]{1,0:T(8,128)(2,1)S(1)}) conditional(s32[]{:T(128)} %convert_element_type.7, () %tuple.61, (bf16[2,1280,128]{2,1,0:T(8,128)(2,1)S(1)}, f32[2,1280,128]{2,1,0:T(8,128)S(1)}) %tuple.62), branch_computations={%region_0.0_spmd, %region_1.0_spmd} | conditional | bytes 2621496 | solution.py:454
  22.2 11.4 %conditional.6 = (f32[1280,128]{1,0:T(8,128)S(1)}, bf16[1312,128]{1,0:T(8,128)(2,1)S(1)}, f32[4,20,256]{2,1,0:T(8,128)}, f32[5,4,20,256]{3,2,1,0:T(8,128)}, f32[...) conditional(s32[]{:T(128)} %convert_element_type.7, () %tuple.60, ...), branch_computations={%region_2.0_spmd, %region_3.4_spmd} | conditional | bytes 7295176 | solution.py:454
  26.1 3.7 %factors.1 = (f32[4,20,256]{2,1,0:T(8,128)}, f32[5,4,20,256]{3,2,1,0:T(8,128)}, f32[3,4,20,256]{3,2,1,0:T(8,128)}, f32[26,20,128]{2,1,0:T(8,128)}, bf16[4,2,256,...) custom-call(f32[20,1024]{1,0:T(8,128)} %get-tuple-element.89.decay_r, ...), custom_call_target="tpu_custom_call" | custom-call | tf_op jit(solution)/shard_map/cond/branch_1_fun/factors/pallas_call | solution.py:580
  34.4 21.2 %conditional.7 = (bf16[1312,128]{1,0:T(8,128)(2,1)}, bf16[1312,128]{1,0:T(8,128)(2,1)}, f32[32,128]{1,0:T(8,128)S(1)}, f32[32,128]{1,0:T(8,128)S(1)}, f32[32,128]{1,0:T(8,128)S(1)}, /*index=5*/bf16[1312,128]{1,0:T(8,128)(2,1)}) conditional(s32[]{:T(128)} %convert_element_type.7, () %tuple.59, (bf16[1312,128]{1,0:T(8,128)(2,1)S(1)}, s32[1]{0:T(128)}, ...), branch_computations={%region_4.5_spmd, %region_5.6_spmd} | conditional | flops 12 | bytes 2719997 | solution.py:454
  35.0 8.3 %collective-permute-done.1.got_ref = bf16[1312,128]{1,0:T(8,128)(2,1)} collective-permute-done((bf16[1312,128]{1,0:T(8,128)(2,1)S(1)}, bf16[1312,128]{1,0:T(8,128)(2,1)}, u32[]{:S(2)}, u32[]{:S(2)}) %collective-permute-start.1) | collective-permute-done | bytes 335904 | tf_op jit(solution)/shard_map/cond/branch_1_fun/ppermute | solution.py:28
  45.7 7.7 %collective-permute-done.2.got_ref = bf16[1312,128]{1,0:T(8,128)(2,1)} collective-permute-done((bf16[1312,128]{1,0:T(8,128)(2,1)}, bf16[1312,128]{1,0:T(8,128)(2,1)}, u32[]{:S(2)}, u32[]{:S(2)}) %collective-permute-start.2) | collective-permute-done | bytes 335904 | tf_op jit(solution)/shard_map/cond/branch_1_fun/ppermute | solution.py:28
  57.9 11.0 %local_levels.1.pre_ref = f32[4,1280,256]{2,1,0:T(8,128)S(1)} custom-call(s32[1]{0:T(128)} %bitcast.10.me_ref, bf16[1280,256]{1,0:T(8,128)(2,1)S(1)} %get-tuple-element.195.refs_0_, bf16[1280,256]{1,0:T(8,128)(2,1)S(1)} %collective-permute-done.20.refs_1_, bf16[1280,128]{1,0:T(8,128)(2,1)S(1)} %collective-permute-done.16.refs_2_, ...), custom_call_target="tpu_custom_call" | custom-call | tf_op jit(solution)/shard_map/local_levels/pallas_call | solution.py:660
  68.9 5.4 %collective-permute-done.22.state_ref = bf16[1312,128]{1,0:T(8,128)(2,1)S(1)} collective-permute-done((bf16[1312,128]{1,0:T(8,128)(2,1)}, bf16[1312,128]{1,0:T(8,128)(2,1)S(1)}, u32[]{:S(2)}, u32[]{:S(2)}) %collective-permute-start.22) | collective-permute-done | bytes 335904 | tf_op jit(solution)/shard_map/ppermute | solution.py:28
  74.3 2.7 %finish.1 = (bf16[1280,256]{1,0:T(8,128)(2,1)S(1)}, bf16[1280,256]{1,0:T(8,128)(2,1)}, bf16[2,1280,256]{2,1,0:T(8,128)(2,1)S(1)}) custom-call(s32[1]{0:T(128)} %bitcast.10.me_ref, f32[4,1280,256]{2,1,0:T(8,128)S(1)} %local_levels.1.pre_ref, bf16[4,256,256]{2,1,0:T(8,128)(2,1)S(1)} %copy-done.1, f32[3,4,20,256]{3,2,1,0:T(8,128)S(1)} %copy-done.3, ...), custom_call_target="tpu_custom_call" | custom-call | tf_op jit(solution)/shard_map/finish/pallas_call | solution.py:676
  77.5 7.0 %collective-permute-done.27 = bf16[320,1280]{1,0:T(8,128)(2,1)} collective-permute-done((bf16[320,1280]{1,0:T(8,128)(2,1)}, bf16[320,1280]{1,0:T(8,128)(2,1)}, u32[]{:S(2)}, u32[]{:S(2)}) %collective-permute-start.27) | collective-permute-done | bytes 819232 | tf_op jit(solution)/shard_map/ppermute | solution.py:28
  86.0 13.3 %conditional.8 = (bf16[1,640,256]{2,1,0:T(8,128)(2,1)}, bf16[640,256]{1,0:T(8,128)(2,1)}, bf16[320,1280]{1,0:T(8,128)(2,1)}, bf16[320,1280]{1,0:T(8,128)(2,1)}) conditional(s32[]{:T(128)} %convert_element_type.7, () %tuple.69, (bf16[320,1280]{1,0:T(8,128)(2,1)}, bf16[320,1280]{1,0:T(8,128)(2,1)}, s32[1]{0:T(128)}, bf16[1280,256]{1,0:T(8,128)(2,1)}, ...), branch_computations={%region_6.7_spmd, %region_7.8_spmd} | conditional | bytes 7864472 | solution.py:454
  86.5 2.9 %project_far.5 = bf16[1,640,256]{2,1,0:T(8,128)(2,1)S(1)} custom-call(s32[1]{0:T(128)} %get-tuple-element.119.place_ref, bf16[1280,256]{1,0:T(8,128)(2,1)} %get-tuple-element.120.refs_0_, bf16[2,1280,256]{2,1,0:T(8,128)(2,1)S(1)} %get-tuple-element.121.refs_1_, bf16[320,1280]{1,0:T(8,128)(2,1)S(1)} %get-tuple-element.124.refs_2_, ...), custom_call_target="tpu_custom_call" | custom-call | tf_op jit(solution)/shard_map/cond/branch_1_fun/project_far/pallas_call | solution.py:709
  90.3 3.9 %project_far.4 = bf16[1,640,256]{2,1,0:T(8,128)(2,1)} custom-call(s32[1]{0:T(128)} %get-tuple-element.119.place_ref, bf16[1280,256]{1,0:T(8,128)(2,1)} %get-tuple-element.120.refs_0_, bf16[2,1280,256]{2,1,0:T(8,128)(2,1)S(1)} %get-tuple-element.121.refs_1_, bf16[320,1280]{1,0:T(8,128)(2,1)} %get-tuple-element.122.refs_2_, ...), custom_call_target="tpu_custom_call" | custom-call | tf_op jit(solution)/shard_map/cond/branch_1_fun/project_far/pallas_call | solution.py:709
  94.2 5.0 %collective-permute-done.5 = bf16[640,256]{1,0:T(8,128)(2,1)} collective-permute-done((bf16[640,256]{1,0:T(8,128)(2,1)S(1)}, bf16[640,256]{1,0:T(8,128)(2,1)}, u32[]{:S(2)}, u32[]{:S(2)}) %collective-permute-start.5) | collective-permute-done | bytes 327712 | tf_op jit(solution)/shard_map/cond/branch_1_fun/ppermute | solution.py:28
  100.1 2.9 %project_own.7 = f32[1,640,256]{2,1,0:T(8,128)S(1)} custom-call(s32[1]{0:T(128)} %bitcast.9.place_ref, bf16[1280,256]{1,0:T(8,128)(2,1)S(1)} %get-tuple-element.236.refs_0_, bf16[2,1280,256]{2,1,0:T(8,128)(2,1)S(1)} %collective-permute-done.24.refs_1_, bf16[320,1280]{1,0:T(8,128)(2,1)} %bitcast.25, bf16[320,1280]{1,0:T(8,128)(2,1)} %collective-permute-done.17.refs_3_, ...), custom_call_target="tpu_custom_call" | custom-call | tf_op jit(solution)/shard_map/project_own/pallas_call | solution.py:709
  105.2 25.2 %conditional.9 = (f32[640,256]{1,0:T(8,128)S(1)}, bf16[640,256]{1,0:T(8,128)(2,1)S(1)}, f32[640,256]{1,0:T(8,128)S(1)}, bf16[640,256]{1,0:T(8,128)(2,1)}, f32[640,256]{1,0:T(8,128)S(1)}) conditional(s32[]{:T(128)} %convert_element_type.7, () %tuple.75, (bf16[320,1280]{1,0:T(8,128)(2,1)}, bf16[320,1280]{1,0:T(8,128)(2,1)}, s32[1]{0:T(128)}, ...), branch_computations={%region_8.9_spmd, %region_9.10_spmd} | conditional | bytes 18350416 | solution.py:454
  108.9 2.6 %project_far.6 = bf16[1,640,256]{2,1,0:T(8,128)(2,1)S(1)} custom-call(s32[1]{0:T(128)} %get-tuple-element.128.place_ref, bf16[1280,256]{1,0:T(8,128)(2,1)} %get-tuple-element.133.refs_0_, bf16[2,1280,256]{2,1,0:T(8,128)(2,1)S(1)} %get-tuple-element.130.refs_1_, bf16[320,1280]{1,0:T(8,128)(2,1)} %get-tuple-element.131.refs_2_, ...), custom_call_target="tpu_custom_call" | custom-call | tf_op jit(solution)/shard_map/cond/branch_1_fun/project_far/pallas_call | solution.py:709
  112.4 2.6 %project_far.7 = bf16[1,640,256]{2,1,0:T(8,128)(2,1)S(1)} custom-call(s32[1]{0:T(128)} %get-tuple-element.128.place_ref, bf16[1280,256]{1,0:T(8,128)(2,1)} %get-tuple-element.133.refs_0_, bf16[2,1280,256]{2,1,0:T(8,128)(2,1)S(1)} %get-tuple-element.130.refs_1_, bf16[320,1280]{1,0:T(8,128)(2,1)} %get-tuple-element.134.refs_2_, ...), custom_call_target="tpu_custom_call" | custom-call | tf_op jit(solution)/shard_map/cond/branch_1_fun/project_far/pallas_call | solution.py:709
  115.0 6.3 %collective-permute-done.8 = bf16[640,256]{1,0:T(8,128)(2,1)S(1)} collective-permute-done((bf16[640,256]{1,0:T(8,128)(2,1)S(1)}, bf16[640,256]{1,0:T(8,128)(2,1)S(1)}, u32[]{:S(2)}, u32[]{:S(2)}) %collective-permute-start.8) | collective-permute-done | bytes 327712 | tf_op jit(solution)/shard_map/cond/branch_1_fun/ppermute | solution.py:28
  122.2 2.9 %project_own.6 = f32[1,640,256]{2,1,0:T(8,128)S(1)} custom-call(s32[1]{0:T(128)} %get-tuple-element.128.place_ref, bf16[1280,256]{1,0:T(8,128)(2,1)S(1)} %get-tuple-element.129.refs_0_, bf16[2,1280,256]{2,1,0:T(8,128)(2,1)S(1)} %get-tuple-element.130.refs_1_, bf16[320,1280]{1,0:T(8,128)(2,1)} %get-tuple-element.137.refs_2_, ...), custom_call_target="tpu_custom_call" | custom-call | tf_op jit(solution)/shard_map/cond/branch_1_fun/project_own/pallas_call | solution.py:709
  125.1 2.4 %project_own.4 = f32[1,640,256]{2,1,0:T(8,128)S(1)} custom-call(s32[1]{0:T(128)} %get-tuple-element.128.place_ref, bf16[1280,256]{1,0:T(8,128)(2,1)S(1)} %get-tuple-element.129.refs_0_, bf16[2,1280,256]{2,1,0:T(8,128)(2,1)S(1)} %get-tuple-element.130.refs_1_, bf16[320,1280]{1,0:T(8,128)(2,1)} %get-tuple-element.131.refs_2_, ...), custom_call_target="tpu_custom_call" | custom-call | tf_op jit(solution)/shard_map/cond/branch_1_fun/project_own/pallas_call | solution.py:709
  127.6 2.5 %project_own.5 = f32[1,640,256]{2,1,0:T(8,128)S(1)} custom-call(s32[1]{0:T(128)} %get-tuple-element.128.place_ref, bf16[1280,256]{1,0:T(8,128)(2,1)S(1)} %get-tuple-element.129.refs_0_, bf16[2,1280,256]{2,1,0:T(8,128)(2,1)S(1)} %get-tuple-element.130.refs_1_, bf16[320,1280]{1,0:T(8,128)(2,1)} %get-tuple-element.134.refs_2_, ...), custom_call_target="tpu_custom_call" | custom-call | tf_op jit(solution)/shard_map/cond/branch_1_fun/project_own/pallas_call | solution.py:709
  130.3 2.6 %assemble.1 = bf16[256,2560]{1,0:T(8,128)(2,1)} custom-call(s32[1]{0:T(128)S(6)} %select_n.12.place_ref, f32[640,256]{1,0:T(8,128)S(1)} %bitcast.17, bf16[640,256]{1,0:T(8,128)(2,1)} %get-tuple-element.237.refs_1_, f32[640,256]{1,0:T(8,128)S(1)} %get-tuple-element.243.refs_2_, bf16[640,256]{1,0:T(8,128)(2,1)S(1)} %get-tuple-element.244.refs_3_, ...), custom_call_target="tpu_custom_call" | custom-call | tf_op jit(solution)/shard_map/assemble/pallas_call | solution.py:771
  (93 shorter events, 46.3 us)
Async XLA Ops:
  0.0 55.6 %collective-permute-start.19 = (bf16[320,1280]{1,0:T(8,128)(2,1)}, bf16[320,1280]{1,0:T(8,128)(2,1)}, u32[]{:S(2)}, u32[]{:S(2)}) collective-permute-start(bf16[320,1280]{1,0:T(8,128)(2,1)} %bitcast.22), channel_id=1, source_target_pairs={{0,16},{4,20},{8,24},{12,28},{16,0},{20,4},{24,8},{28,12},{1,17},{... | collective-permute-start | bytes 2457608 | tf_op jit(solution)/shard_map/ppermute | solution.py:28
  4.0 51.6 %collective-permute-start.17 = (bf16[320,1280]{1,0:T(8,128)(2,1)}, bf16[320,1280]{1,0:T(8,128)(2,1)}, u32[]{:S(2)}, u32[]{:S(2)}) collective-permute-start(bf16[320,1280]{1,0:T(8,128)(2,1)} %bitcast.23), channel_id=1, source_target_pairs={{0,4},{4,0},{8,12},{12,8},{16,20},{20,16},{24,28},{28,24},{1,5},{5... | collective-permute-start | bytes 2457608 | tf_op jit(solution)/shard_map/ppermute | solution.py:28
  5.5 50.1 %collective-permute-start.18 = (bf16[320,1280]{1,0:T(8,128)(2,1)}, bf16[320,1280]{1,0:T(8,128)(2,1)}, u32[]{:S(2)}, u32[]{:S(2)}) collective-permute-start(bf16[320,1280]{1,0:T(8,128)(2,1)} %bitcast.24), channel_id=1, source_target_pairs={{0,8},{4,12},{8,0},{12,4},{16,24},{20,28},{24,16},{28,20},{1,9},{5... | collective-permute-start | bytes 2457608 | tf_op jit(solution)/shard_map/ppermute | solution.py:28
  9.0 4.9 %collective-permute-start.14 = (f32[2,20,256]{2,1,0:T(8,128)S(1)}, f32[2,20,256]{2,1,0:T(8,128)S(1)}, u32[]{:S(2)}, u32[]{:S(2)}) collective-permute-start(f32[2,20,256]{2,1,0:T(8,128)S(1)} %get-tuple-element.202), channel_id=1, source_target_pairs={{0,2},{1,3},{2,0},{3,1},{4,6},{5,7},{6,4},{7,5},{8,10},{9,11},{10,... | collective-permute-start | bytes 122888 | tf_op jit(solution)/shard_map/ppermute | solution.py:28
  13.9 8.3 %collective-permute-start.16 = (bf16[1280,128]{1,0:T(8,128)(2,1)S(1)}, bf16[1280,128]{1,0:T(8,128)(2,1)S(1)}, u32[]{:S(2)}, u32[]{:S(2)}) collective-permute-start(bf16[1280,128]{1,0:T(8,128)(2,1)S(1)} %get-tuple-element.206.refs_2_), channel_id=1, source_target_pairs={{0,2},{1,3},{2,0},{3,1},{4,6},{5,7},{6,4},{7,5},{8,10},{9,11},{10,... | collective-permute-start | bytes 983048 | tf_op jit(solution)/shard_map/ppermute | solution.py:28
  22.2 7.6 %collective-permute-start.13 = (bf16[1280,256]{1,0:T(8,128)(2,1)}, bf16[1280,256]{1,0:T(8,128)(2,1)S(1)}, u32[]{:S(2)}, u32[]{:S(2)}) collective-permute-start(bf16[1280,256]{1,0:T(8,128)(2,1)} %get-tuple-element.96), channel_id=1, source_target_pairs={{0,1},{1,0},{2,3},{3,2},{4,5},{5,4},{6,7},{7,6},{8,9},{9,8},{10,11... | collective-permute-start | bytes 1966088 | tf_op jit(solution)/shard_map/cond/branch_1_fun/ppermute | solution.py:28
  22.9 9.6 %collective-permute-start.12 = (bf16[1280,128]{1,0:T(8,128)(2,1)}, bf16[1280,128]{1,0:T(8,128)(2,1)S(1)}, u32[]{:S(2)}, u32[]{:S(2)}) collective-permute-start(bf16[1280,128]{1,0:T(8,128)(2,1)} %copy-done.8), channel_id=1, source_target_pairs={{0,2},{1,3},{2,0},{3,1},{4,6},{5,7},{6,4},{7,5},{8,10},{9,11},{10,... | collective-permute-start | bytes 983048 | tf_op jit(solution)/shard_map/cond/branch_1_fun/ppermute | solution.py:28
  33.7 23.9 %collective-permute-start.21 = (bf16[1280,384]{1,0:T(8,128)(2,1)}, bf16[1280,384]{1,0:T(8,128)(2,1)S(1)}, u32[]{:S(2)}, u32[]{:S(2)}) collective-permute-start(bf16[1280,384]{1,0:T(8,128)(2,1)} %get-tuple-element.215), channel_id=1, source_target_pairs={{0,2},{1,3},{2,0},{3,1},{4,6},{5,7},{6,4},{7,5},{8,10},{9,11},{10,... | collective-permute-start | bytes 2949128 | tf_op jit(solution)/shard_map/ppermute | solution.py:28
  34.4 8.9 %collective-permute-start.1 = (bf16[1312,128]{1,0:T(8,128)(2,1)S(1)}, bf16[1312,128]{1,0:T(8,128)(2,1)}, u32[]{:S(2)}, u32[]{:S(2)}) collective-permute-start(bf16[1312,128]{1,0:T(8,128)(2,1)S(1)} %get-tuple-element.107), channel_id=1, source_target_pairs={{0,4},{4,0},{8,12},{12,8},{16,20},{20,16},{24,28},{28,24},{1,5},{5... | collective-permute-start | bytes 1007624 | tf_op jit(solution)/shard_map/cond/branch_1_fun/ppermute | solution.py:28
  45.3 8.1 %collective-permute-start.2 = (bf16[1312,128]{1,0:T(8,128)(2,1)}, bf16[1312,128]{1,0:T(8,128)(2,1)}, u32[]{:S(2)}, u32[]{:S(2)}) collective-permute-start(bf16[1312,128]{1,0:T(8,128)(2,1)} %get-tuple-element.111), channel_id=1, source_target_pairs={{0,8},{4,12},{8,0},{12,4},{16,24},{20,28},{24,16},{28,20},{1,9},{5... | collective-permute-start | bytes 1007624 | tf_op jit(solution)/shard_map/cond/branch_1_fun/ppermute | solution.py:28
  55.7 18.6 %collective-permute-start.22 = (bf16[1312,128]{1,0:T(8,128)(2,1)}, bf16[1312,128]{1,0:T(8,128)(2,1)S(1)}, u32[]{:S(2)}, u32[]{:S(2)}) collective-permute-start(bf16[1312,128]{1,0:T(8,128)(2,1)} %get-tuple-element.213), channel_id=1, source_target_pairs={{0,16},{4,20},{8,24},{12,28},{16,0},{20,4},{24,8},{28,12},{1,17},{... | collective-permute-start | bytes 1007624 | tf_op jit(solution)/shard_map/ppermute | solution.py:28
  56.4 21.2 %collective-permute-start.23 = (bf16[320,1280]{1,0:T(8,128)(2,1)}, bf16[320,1280]{1,0:T(8,128)(2,1)}, u32[]{:S(2)}, u32[]{:S(2)}) collective-permute-start(bf16[320,1280]{1,0:T(8,128)(2,1)} %collective-permute-done.19), channel_id=1, source_target_pairs={{0,4},{4,0},{8,12},{12,8},{16,20},{20,16},{24,28},{28,24},{1,5},{5... | collective-permute-start | bytes 2457608 | tf_op jit(solution)/shard_map/ppermute | solution.py:28
  57.0 27.5 %collective-permute-start.27 = (bf16[320,1280]{1,0:T(8,128)(2,1)}, bf16[320,1280]{1,0:T(8,128)(2,1)}, u32[]{:S(2)}, u32[]{:S(2)}) collective-permute-start(bf16[320,1280]{1,0:T(8,128)(2,1)} %collective-permute-done.19), channel_id=1, source_target_pairs={{0,8},{4,12},{8,0},{12,4},{16,24},{20,28},{24,16},{28,20},{1,9},{5... | collective-permute-start | bytes 2457608 | tf_op jit(solution)/shard_map/ppermute | solution.py:28
  77.0 8.9 %collective-permute-start.24 = (bf16[2,1280,256]{2,1,0:T(8,128)(2,1)S(1)}, bf16[2,1280,256]{2,1,0:T(8,128)(2,1)S(1)}, u32[]{:S(2)}, u32[]{:S(2)}) collective-permute-start(bf16[2,1280,256]{2,1,0:T(8,128)(2,1)S(1)} %get-tuple-element.232), channel_id=1, source_target_pairs={{0,1},{1,0},{2,3},{3,2},{4,5},{5,4},{6,7},{7,6},{8,9},{9,8},{10,11... | collective-permute-start | bytes 3932168 | tf_op jit(solution)/shard_map/ppermute | solution.py:28
  77.0 8.9 %collective-permute-start.26 = (bf16[320,1280]{1,0:T(8,128)(2,1)}, bf16[320,1280]{1,0:T(8,128)(2,1)}, u32[]{:S(2)}, u32[]{:S(2)}) collective-permute-start(bf16[320,1280]{1,0:T(8,128)(2,1)} %collective-permute-done.17.refs_3_), channel_id=1, source_target_pairs={{0,1},{1,0},{2,3},{3,2},{4,5},{5,4},{6,7},{7,6},{8,9},{9,8},{10,11... | collective-permute-start | bytes 2457608 | tf_op jit(solution)/shard_map/ppermute | solution.py:28
  77.5 8.4 %collective-permute-start.25 = (bf16[320,1280]{1,0:T(8,128)(2,1)S(1)}, bf16[320,1280]{1,0:T(8,128)(2,1)}, u32[]{:S(2)}, u32[]{:S(2)}) collective-permute-start(bf16[320,1280]{1,0:T(8,128)(2,1)S(1)} %bitcast.26), channel_id=1, source_target_pairs={{0,1},{1,0},{2,3},{3,2},{4,5},{5,4},{6,7},{7,6},{8,9},{9,8},{10,11... | collective-permute-start | bytes 2457608 | tf_op jit(solution)/shard_map/ppermute | solution.py:28
  84.5 19.6 %collective-permute-start.29 = (bf16[320,1280]{1,0:T(8,128)(2,1)}, bf16[320,1280]{1,0:T(8,128)(2,1)}, u32[]{:S(2)}, u32[]{:S(2)}) collective-permute-start(bf16[320,1280]{1,0:T(8,128)(2,1)} %collective-permute-done.27), channel_id=1, source_target_pairs={{0,4},{4,0},{8,12},{12,8},{16,20},{20,16},{24,28},{28,24},{1,5},{5... | collective-permute-start | bytes 2457608 | tf_op jit(solution)/shard_map/ppermute | solution.py:28
  85.9 19.2 %collective-permute-start.28 = (bf16[320,1280]{1,0:T(8,128)(2,1)}, bf16[320,1280]{1,0:T(8,128)(2,1)}, u32[]{:S(2)}, u32[]{:S(2)}) collective-permute-start(bf16[320,1280]{1,0:T(8,128)(2,1)} %collective-permute-done.17.refs_3_), channel_id=1, source_target_pairs={{0,8},{4,12},{8,0},{12,4},{16,24},{20,28},{24,16},{28,20},{1,9},{5... | collective-permute-start | bytes 2457608 | tf_op jit(solution)/shard_map/ppermute | solution.py:28
  89.4 9.9 %collective-permute-start.5 = (bf16[640,256]{1,0:T(8,128)(2,1)S(1)}, bf16[640,256]{1,0:T(8,128)(2,1)}, u32[]{:S(2)}, u32[]{:S(2)}) collective-permute-start(bf16[640,256]{1,0:T(8,128)(2,1)S(1)} %bitcast.20), channel_id=1, source_target_pairs={{0,2},{1,3},{2,0},{3,1},{4,6},{5,7},{6,4},{7,5},{8,10},{9,11},{10,... | collective-permute-start | bytes 983048 | tf_op jit(solution)/shard_map/cond/branch_1_fun/ppermute | solution.py:28
  99.3 31.1 %collective-permute-start.30 = (bf16[640,256]{1,0:T(8,128)(2,1)}, bf16[640,256]{1,0:T(8,128)(2,1)S(1)}, u32[]{:S(2)}, u32[]{:S(2)}) collective-permute-start(bf16[640,256]{1,0:T(8,128)(2,1)} %bitcast.14), channel_id=1, source_target_pairs={{0,2},{1,3},{2,0},{3,1},{4,6},{5,7},{6,4},{7,5},{8,10},{9,11},{10,... | collective-permute-start | bytes 983048 | tf_op jit(solution)/shard_map/ppermute | solution.py:28
  105.7 6.8 %collective-permute-start.10 = (bf16[320,1280]{1,0:T(8,128)(2,1)}, bf16[320,1280]{1,0:T(8,128)(2,1)S(1)}, u32[]{:S(2)}, u32[]{:S(2)}) collective-permute-start(bf16[320,1280]{1,0:T(8,128)(2,1)} %get-tuple-element.135.refs_3_), channel_id=1, source_target_pairs={{0,1},{1,0},{2,3},{3,2},{4,5},{5,4},{6,7},{7,6},{8,9},{9,8},{10,11... | collective-permute-start | bytes 2457608 | tf_op jit(solution)/shard_map/cond/branch_1_fun/ppermute | solution.py:28
  105.7 6.8 %collective-permute-start.9 = (bf16[320,1280]{1,0:T(8,128)(2,1)}, bf16[320,1280]{1,0:T(8,128)(2,1)S(1)}, u32[]{:S(2)}, u32[]{:S(2)}) collective-permute-start(bf16[320,1280]{1,0:T(8,128)(2,1)} %get-tuple-element.134.refs_2_), channel_id=1, source_target_pairs={{0,1},{1,0},{2,3},{3,2},{4,5},{5,4},{6,7},{7,6},{8,9},{9,8},{10,11... | collective-permute-start | bytes 2457608 | tf_op jit(solution)/shard_map/cond/branch_1_fun/ppermute | solution.py:28
  111.5 9.8 %collective-permute-start.8 = (bf16[640,256]{1,0:T(8,128)(2,1)S(1)}, bf16[640,256]{1,0:T(8,128)(2,1)S(1)}, u32[]{:S(2)}, u32[]{:S(2)}) collective-permute-start(bf16[640,256]{1,0:T(8,128)(2,1)S(1)} %bitcast.21), channel_id=1, source_target_pairs={{0,2},{1,3},{2,0},{3,1},{4,6},{5,7},{6,4},{7,5},{8,10},{9,11},{10,... | collective-permute-start | bytes 983048 | tf_op jit(solution)/shard_map/cond/branch_1_fun/ppermute | solution.py:28
  121.3 9.0 %collective-permute-start.11 = (bf16[640,256]{1,0:T(8,128)(2,1)S(1)}, bf16[640,256]{1,0:T(8,128)(2,1)}, u32[]{:S(2)}, u32[]{:S(2)}) collective-permute-start(bf16[640,256]{1,0:T(8,128)(2,1)S(1)} %bitcast.19), channel_id=1, source_target_pairs={{0,2},{1,3},{2,0},{3,1},{4,6},{5,7},{6,4},{7,5},{8,10},{9,11},{10,... | collective-permute-start | bytes 983048 | tf_op jit(solution)/shard_map/cond/branch_1_fun/ppermute | solution.py:28
  (18 other events, 138.6 us)

commit v2 on v1

--- a/solution.py
+++ b/solution.py
@@ -234,7 +234,7 @@
 
 def merge_kernel(
     bit, head_count, place_ref, running_ref, total_ref, offset_ref, got_ref,
-    next_running_ref, next_total_ref, next_offset_ref, factor_ref, sent_ref,
+    next_total_ref, next_offset_ref, factor_ref, sent_ref, next_running_ref,
 ):
     channels = running_ref.shape[0]
     width = channels // head_count
@@ -366,33 +366,35 @@
                 send_ref[r // 2, at, :] = normed.astype(BF16)
 
 
-def project_kernel(place_ref, *refs):
+def project_kernel(*refs):
     *refs, out_ref = refs
     rows = out_ref.shape[0]
     kept_refs, other_refs, refs = refs[:rows], refs[rows : 2 * rows], refs[2 * rows :]
     count = len(refs) // 2
     weights, partners = refs[:count], refs[count:]
     width = weights[0].shape[0]
-    turn = place_ref[0] % count
     for i, (kept_ref, other_ref) in enumerate(zip(kept_refs, other_refs)):
         for j, (weight, partner) in enumerate(zip(weights, partners)):
             found = dot(weight[...], kept_ref[...]) + dot(partner[...], other_ref[0])
-            at = pl.ds(pl.multiple_of((turn ^ j) * width, width), width)
-            out_ref[i, at, :] = found.astype(out_ref.dtype)
-
-
-def assemble_kernel(place_ref, *refs):
-    out_ref = refs[-1]
-    width = refs[0].shape[0]
-    groups = out_ref.shape[1] // width
-    each = (len(refs) - 1) // groups
-    for p in range(groups):
-        own_ref, *far_refs = refs[p * each : (p + 1) * each]
-        total = own_ref[...]
-        for far_ref in far_refs:
-            total = total + far_ref[...].astype(F32)
-        start = pl.multiple_of((place_ref[0] ^ p) * width, width)
-        out_ref[:, pl.ds(start, width)] = jnp.transpose(total).astype(BF16)
+            out_ref[i, j * width : (j + 1) * width, :] = found.astype(out_ref.dtype)
+
+
+def assemble_kernel(groups, place_ref, *refs):
+    *refs, out_ref, columns_ref = refs
+    each = len(refs) // len(groups)
+    for g, group in enumerate(groups):
+        own_ref, *far_refs = refs[g * each : (g + 1) * each]
+        width = own_ref.shape[0] // len(group)
+        for j, r in enumerate(group):
+            rows = slice(j * width, (j + 1) * width)
+            total = own_ref[rows, :]
+            for far_ref in far_refs:
+                total = total + far_ref[rows, :].astype(F32)
+            start = pl.multiple_of((place_ref[0] ^ r) * width, width)
+            columns_ref[pl.ds(start, width), :] = total
+    for first in range(0, out_ref.shape[1], LANES):
+        at = slice(first, first + LANES)
+        out_ref[:, at] = jnp.transpose(columns_ref[at, :]).astype(BF16)
 
 
 def whole(shape):
@@ -548,18 +550,17 @@
     pair_rows = max(per_group // 2, 1) * state_size
 
     def step(bit, running, total, offset, got):
-        return kernel_call(
+        last = bit + 1 == near
+        shapes = [shape((extra, LANES), F32)] * 3 + [shape((features + extra, state_size))]
+        running_shape = shape((features, state_size), F32)
+        results = kernel_call(
             functools.partial(merge_kernel, bit, head_count),
             "merge",
-            (
-                shape((features, state_size), F32),
-                shape((extra, LANES), F32),
-                shape((extra, LANES), F32),
-                shape((extra, LANES), F32),
-                shape((features + extra, state_size)),
-            ),
+            tuple(shapes if last else shapes + [running_shape]),
             in_specs=[smem] + [vmem] * 4,
+            scratch_shapes=[pltpu.VMEM((features, state_size), F32)] if last else [],
         )(place1, running, total, offset, got)
+        return list(results) + [None] * last
 
     def chip_sum(
         keep, core_states, far_states, total, decays, level_class, level_table, state_in, state_out,
@@ -615,7 +616,7 @@
         states = []
         for bit in range(near):
             states.append(swap(sent, "ctx", 2**bit))
-            running, total, offset, factor, sent = step(bit, running, total, offset, states[-1])
+            total, offset, factor, sent, running = step(bit, running, total, offset, states[-1])
             factors.append(factor)
         return states, factors, sent
 
@@ -689,91 +690,96 @@
         ],
         out_specs=[whole((features, rows_dev))] * half + [whole((half, features, rows_dev))],
     )(me1, pre, readers, cross, factors[near], last_state, gains)
-    early_blocks = set(held)
     done = [held[r] for r in held if r not in (0, 1)] + [kept[0]]
+    early_blocks = sorted(held)
     held[3] = swap(tie(held[1], *done), "ctx", 2)
     for r in range(5, ctx_size, 2):
         if r not in held:
             held[r] = swap(tie(held[r ^ 1], *done), "ctx", 1)
 
-    count = 1
-    while count * columns % 128 and 2 * count <= ctx_size:
-        count *= 2
-
+    order = sorted(early_blocks, key=lambda r: (r // 2 * 2 not in early_blocks or r ^ 1 not in early_blocks, r))
+    order += [r for r in range(ctx_size) if r not in early_blocks]
+    count = 2
+    groups = [order[first : first + count] for first in range(0, ctx_size, count)]
     others = swap(sides, "head", 1)
-    firsts = list(range(0, ctx_size, count))
-    group_of = lambda first: range(first, first + count)
-
-    def project(name, first, kept, others, blocks, partners, kind):
+
+    def project(name, first, kept, others, group, blocks, partners, kind):
         rows = len(kept)
         return kernel_call(
             project_kernel,
             name,
             shape((rows, count * columns, rows_dev), kind),
-            in_specs=[smem]
-            + [whole((features, rows_dev))] * rows
+            in_specs=[whole((features, rows_dev))] * rows
             + [part(others, first + i) for i in range(rows)]
             + [whole((columns, features))] * (2 * count),
             out_specs=whole((rows, count * columns, rows_dev)),
             grid=(1,),
-        )(place1, *kept, *[others] * rows, *blocks, *partners)
-
-    def far_rows(first, kept, others, blocks, partners):
-        return project(
-            "project_far", 1, kept[1:], others,
-            [blocks[r] for r in group_of(first)], [partners[r] for r in group_of(first)], BF16,
-        )
-
-    def own_rows(first, kept, others, blocks, partners):
-        return project(
-            "project_own", 0, kept[:1], others,
-            [blocks[r] for r in group_of(first)], [partners[r] for r in group_of(first)], F32,
-        )[0]
+        )(*kept, *[others] * rows, *[blocks[r] for r in group], *[partners[r] for r in group])
+
+    def far_rows(group, kept, others, blocks, partners):
+        return project("project_far", 1, kept[1:], others, group, blocks, partners, BF16)
+
+    def own_rows(group, kept, others, blocks, partners):
+        return project("project_own", 0, kept[:1], others, group, blocks, partners, F32)[0]
 
     def send_rows(far, *after):
         far = tie(far, *after)
         return [swap(far[i - 1], "head", 2 * i) for i in range(1, half)]
 
+    def with_partners(blocks, partners):
+        more = {r: swap(blocks[r], "head", 1) for r in blocks if r not in partners}
+        return {**partners, **more}, more
+
     def first_groups(kept, others, blocks, partners):
-        more = {r: swap(blocks[r], "head", 1) for r in blocks if r not in partners}
-        partners = {**partners, **more}
-        fars = [far_rows(first, kept, others, blocks, partners) for first in early_groups]
-        return fars[1:], send_rows(fars[0]), more
-
-    def last_groups(kept, others, blocks, partners, early):
-        partners, results, arrived = dict(partners), {}, []
-        for first in late_groups:
-            for r in group_of(first):
-                if r not in partners:
-                    partners[r] = swap(blocks[r], "head", 1)
-            got = send_rows(far_rows(first, kept, others, blocks, partners), *arrived)
-            results[first] = [own_rows(first, kept, others, blocks, partners)] + got
-            arrived = got
-        owns = [own_rows(first, kept, others, early, partners) for first in early_groups[1:]]
-        return results, owns
-
-    early_groups = [f for f in firsts if all(r in early_blocks for r in group_of(f))] or firsts[:1]
-    late_groups = [f for f in firsts if f not in early_groups]
-    early = {r: held[r] for f in early_groups for r in group_of(f)}
-    late = {r: held[r] for f in late_groups for r in group_of(f)}
-    fars, got, more = fenced(first_groups, kept, others, early, partners)
-    partners = {**partners, **more}
-    sent_groups = [got]
-    for far in fars:
-        sent_groups.append(send_rows(far, *sent_groups[-1]))
-    own = own_rows(early_groups[0], [tie(kept[0], *fars)], others, early, partners)
-    if late_groups:
-        late[late_groups[0]] = tie(late[late_groups[0]], own)
-    results, owns = fenced(last_groups, kept, others, late, partners, early)
-    for first, own, got in zip(early_groups, [own] + owns, sent_groups):
-        results[first] = [own] + got
-    pieces = [piece for first in firsts for piece in results[first]]
+        partners, more = with_partners(blocks, partners)
+        got = send_rows(far_rows(groups[0], kept, others, blocks, partners))
+        return far_rows(groups[1], kept, others, blocks, partners), got, more
+
+    def middle_group(index):
+        def body(far, kept, others, blocks, partners):
+            partners, more = with_partners(blocks, partners)
+            return far_rows(groups[index], kept, others, blocks, partners), send_rows(far), more
+
+        return body
+
+    def last_group(kept, others, blocks, partners):
+        partners, more = with_partners(blocks, partners)
+        return far_rows(groups[-1], kept, others, blocks, partners), more
+
+    def some(array, group):
+        return {r: array[r] for r in group if r in array}
+
+    arrived = []
+    far, got, more = fenced(
+        first_groups, kept, others, some(held, groups[0] + groups[1]), some(partners, groups[0] + groups[1])
+    )
+    arrived.append(got)
+    partners.update(more)
+    for index in range(2, len(groups) - 1):
+        far, got, more = fenced(
+            middle_group(index), far, kept, others, some(held, groups[index]), some(partners, groups[index])
+        )
+        arrived.append(got)
+        partners.update(more)
+    got = send_rows(far, *[held[r] for r in groups[-1]])
+    arrived.append(got)
+    ahead = own_rows(groups[0], [tie(kept[0], far)], others, held, partners)
+    blocks = some(held, groups[-1])
+    blocks[groups[-1][0]] = tie(blocks[groups[-1][0]], ahead)
+    far, more = fenced(last_group, kept, others, blocks, some(partners, groups[-1]))
+    partners.update(more)
+    arrived.append(send_rows(far, *got))
+    pieces = []
+    for group, got in zip(groups, arrived):
+        own = ahead if group == groups[0] else own_rows(group, kept, others, held, partners)
+        pieces += [own] + got
     return kernel_call(
-        assemble_kernel,
+        functools.partial(assemble_kernel, groups),
         "assemble",
         shape((rows_dev, ctx_size * columns)),
         in_specs=[smem] + [vmem] * len(pieces),
-    )(place1 // count, *pieces)
+        scratch_shapes=[pltpu.VMEM((ctx_size * columns, rows_dev), F32)],
+    )(place1, *pieces)
 
 
 def solution(mesh):

time: 134 us -> 132 us (0.985)
  waiting for transfers between devices: 51.2 us -> 49.6 us
    ppermute x31, waiting for transfers between devices: 51.2 us -> 49.6 us  [swap(): return lax.ppermute(value, axis, pairs)]
  transfers between devices with their start and end apart: 31 -> 31, of which waited for: 16 -> 15; matrix products, arithmetic and copies ran while one was open for 3% -> 3% of each run, Pallas kernels for 39% -> 39%
where the time goes in v2:
time: 132 us; the launch traced here: 131 us
  Pallas kernels  54.6 us (41%)
  waiting for transfers between devices  49.6 us (38%)
  starting transfers between devices  20.5 us (16%)
  local copies, waits for them, and re-layouts  6.36 us (5%)
    ppermute x31, waiting for transfers between devices, swap(): return lax.ppermute(value, axis, pairs)  49.6 us
    pallas_call x8, Pallas kernels, project(): kernel_call(project_kernel, name, shape((rows, count * columns, rows_dev)...  23.7 us
    ppermute x31, starting transfers between devices, swap(): return lax.ppermute(value, axis, pairs)  20.5 us
    pallas_call x1, Pallas kernels, on_device(): kernel_call(functools.partial(local_kernel, near, pieces), 'local_levels'...  11 us
    pallas_call x2, Pallas kernels, step(): kernel_call(functools.partial(merge_kernel, bit, head_count), 'merge', tu...  3.96 us
    pallas_call x1, Pallas kernels, chip_sum(): kernel_call(functools.partial(factors_kernel, levels, heads_size), 'facto...  3.7 us
    pallas_call x1, Pallas kernels, on_device(): kernel_call(functools.partial(assemble_kernel, groups), 'assemble', shape...  2.78 us
  transfers between devices with their start and end apart: 31, of which 15 were waited for; matrix products, arithmetic and copies ran while one was open for 3% of the time, Pallas kernels for 39%

profile of v2, /device:TPU:0, one launch (start us, length us, event | category | flops | bytes accessed | tf_op | source)
XLA Modules:
  0.0 131.3 jit_solution(7872725816168218719)
XLA Ops:
  0.0 4.0 %collective-permute-start.18 = (bf16[320,1280]{1,0:T(8,128)(2,1)}, bf16[320,1280]{1,0:T(8,128)(2,1)}, u32[]{:S(2)}, u32[]{:S(2)}) collective-permute-start(bf16[320,1280]{1,0:T(8,128)(2,1)} %bitcast.23), channel_id=1, source_target_pairs={{0,16},{4,20},{8,24},{12,28},{16,0},{20,4},{24,8},{28,12},{1,17},{... | collective-permute-start | bytes 2457608 | tf_op jit(solution)/shard_map/ppermute | solution.py:28
  17.9 3.3 %conditional.6 = (bf16[2,1280,128]{2,1,0:T(8,128)(2,1)}, bf16[1280,128]{1,0:T(8,128)(2,1)S(1)}) conditional(s32[]{:T(128)} %convert_element_type.7, () %tuple.69, (bf16[2,1280,128]{2,1,0:T(8,128)(2,1)S(1)}, f32[2,1280,128]{2,1,0:T(8,128)S(1)}) %tuple.70), branch_computations={%region_0.0_spmd, %region_1.0_spmd} | conditional | bytes 2621496 | solution.py:456
  22.2 11.4 %conditional.7 = (f32[1280,128]{1,0:T(8,128)S(1)}, bf16[1312,128]{1,0:T(8,128)(2,1)S(1)}, f32[4,20,256]{2,1,0:T(8,128)}, f32[5,4,20,256]{3,2,1,0:T(8,128)}, f32[...) conditional(s32[]{:T(128)} %convert_element_type.7, () %tuple.68, ...), branch_computations={%region_2.0_spmd, %region_3.4_spmd} | conditional | bytes 7295176 | solution.py:456
  26.1 3.7 %factors.1 = (f32[4,20,256]{2,1,0:T(8,128)}, f32[5,4,20,256]{3,2,1,0:T(8,128)}, f32[3,4,20,256]{3,2,1,0:T(8,128)}, f32[26,20,128]{2,1,0:T(8,128)}, bf16[4,2,256,...) custom-call(f32[20,1024]{1,0:T(8,128)} %get-tuple-element.81.decay_r, ...), custom_call_target="tpu_custom_call" | custom-call | tf_op jit(solution)/shard_map/cond/branch_1_fun/factors/pallas_call | solution.py:581
  34.4 21.0 %conditional.8 = (bf16[1312,128]{1,0:T(8,128)(2,1)}, bf16[1312,128]{1,0:T(8,128)(2,1)}, f32[32,128]{1,0:T(8,128)S(1)}, f32[32,128]{1,0:T(8,128)S(1)}, f32[32,128]{1,0:T(8,128)S(1)}, /*index=5*/bf16[1312,128]{1,0:T(8,128)(2,1)}) conditional(s32[]{:T(128)} %convert_element_type.7, () %tuple.67, (bf16[1312,128]{1,0:T(8,128)(2,1)S(1)}, s32[1]{0:T(128)}, ...), branch_computations={%region_4.5_spmd, %region_5.6_spmd} | conditional | flops 12 | bytes 2719997 | solution.py:456
  35.0 8.3 %collective-permute-done.1.got_ref = bf16[1312,128]{1,0:T(8,128)(2,1)} collective-permute-done((bf16[1312,128]{1,0:T(8,128)(2,1)S(1)}, bf16[1312,128]{1,0:T(8,128)(2,1)}, u32[]{:S(2)}, u32[]{:S(2)}) %collective-permute-start.1) | collective-permute-done | bytes 335904 | tf_op jit(solution)/shard_map/cond/branch_1_fun/ppermute | solution.py:28
  45.7 7.7 %collective-permute-done.2.got_ref = bf16[1312,128]{1,0:T(8,128)(2,1)} collective-permute-done((bf16[1312,128]{1,0:T(8,128)(2,1)}, bf16[1312,128]{1,0:T(8,128)(2,1)}, u32[]{:S(2)}, u32[]{:S(2)}) %collective-permute-start.2) | collective-permute-done | bytes 335904 | tf_op jit(solution)/shard_map/cond/branch_1_fun/ppermute | solution.py:28
  57.7 11.0 %local_levels.1.pre_ref = f32[4,1280,256]{2,1,0:T(8,128)S(1)} custom-call(s32[1]{0:T(128)} %bitcast.6.me_ref, bf16[1280,256]{1,0:T(8,128)(2,1)S(1)} %get-tuple-element.185.refs_0_, bf16[1280,256]{1,0:T(8,128)(2,1)S(1)} %collective-permute-done.19.refs_1_, bf16[1280,128]{1,0:T(8,128)(2,1)S(1)} %collective-permute-done.15.refs_2_, ...), custom_call_target="tpu_custom_call" | custom-call | tf_op jit(solution)/shard_map/local_levels/pallas_call | solution.py:661
  68.7 5.4 %collective-permute-done.21.state_ref = bf16[1312,128]{1,0:T(8,128)(2,1)S(1)} collective-permute-done((bf16[1312,128]{1,0:T(8,128)(2,1)}, bf16[1312,128]{1,0:T(8,128)(2,1)S(1)}, u32[]{:S(2)}, u32[]{:S(2)}) %collective-permute-start.21) | collective-permute-done | bytes 335904 | tf_op jit(solution)/shard_map/ppermute | solution.py:28
  76.6 7.1 %collective-permute-done.22.refs_3_ = bf16[320,1280]{1,0:T(8,128)(2,1)} collective-permute-done((bf16[320,1280]{1,0:T(8,128)(2,1)}, bf16[320,1280]{1,0:T(8,128)(2,1)}, u32[]{:S(2)}, u32[]{:S(2)}) %collective-permute-start.22) | collective-permute-done | bytes 819232 | tf_op jit(solution)/shard_map/ppermute | solution.py:28
  84.6 13.1 %conditional.9 = (bf16[1,640,256]{2,1,0:T(8,128)(2,1)S(1)}, bf16[640,256]{1,0:T(8,128)(2,1)}, bf16[320,1280]{1,0:T(8,128)(2,1)}, bf16[320,1280]{1,0:T(8,128)(2,1)}) conditional(s32[]{:T(128)} %convert_element_type.7, () %tuple.79, (bf16[320,1280]{1,0:T(8,128)(2,1)}, bf16[320,1280]{1,0:T(8,128)(2,1)}, bf16[1280,256]{1,0:T(8,128)(2,1)S(1)}, ...), branch_computations={%region_6.7_spmd, %region_7.8_spmd} | conditional | bytes 7864472 | solution.py:456
  85.2 2.6 %project_far.5 = bf16[1,640,256]{2,1,0:T(8,128)(2,1)S(1)} custom-call(bf16[1280,256]{1,0:T(8,128)(2,1)S(1)} %get-tuple-element.111.refs_0_, bf16[2,1280,256]{2,1,0:T(8,128)(2,1)S(1)} %get-tuple-element.112.refs_1_, bf16[320,1280]{1,0:T(8,128)(2,1)S(1)} %get-tuple-element.115.refs_2_, bf16[320,1280]{1,0:T(8,128)(2,1)} %get-tuple-element.116.refs_3_, ...), custom_call_target="tpu_custom_call" | custom-call | tf_op jit(solution)/shard_map/cond/branch_1_fun/project_far/pallas_call | solution.py:708
  88.8 2.9 %project_far.4 = bf16[1,640,256]{2,1,0:T(8,128)(2,1)S(1)} custom-call(bf16[1280,256]{1,0:T(8,128)(2,1)S(1)} %get-tuple-element.111.refs_0_, bf16[2,1280,256]{2,1,0:T(8,128)(2,1)S(1)} %get-tuple-element.112.refs_1_, bf16[320,1280]{1,0:T(8,128)(2,1)} %get-tuple-element.113.refs_2_, bf16[320,1280]{1,0:T(8,128)(2,1)} %get-tuple-element.114.refs_3_, ...), custom_call_target="tpu_custom_call" | custom-call | tf_op jit(solution)/shard_map/cond/branch_1_fun/project_far/pallas_call | solution.py:708
  91.6 6.0 %collective-permute-done.5 = bf16[640,256]{1,0:T(8,128)(2,1)} collective-permute-done((bf16[640,256]{1,0:T(8,128)(2,1)S(1)}, bf16[640,256]{1,0:T(8,128)(2,1)}, u32[]{:S(2)}, u32[]{:S(2)}) %collective-permute-start.5) | collective-permute-done | bytes 327712 | tf_op jit(solution)/shard_map/cond/branch_1_fun/ppermute | solution.py:28
  97.7 10.2 %conditional.10 = (bf16[1,640,256]{2,1,0:T(8,128)(2,1)}, bf16[640,256]{1,0:T(8,128)(2,1)}, bf16[320,1280]{1,0:T(8,128)(2,1)}, bf16[320,1280]{1,0:T(8,128)(2,1)}) conditional(s32[]{:T(128)} %convert_element_type.7, () %tuple.77, (bf16[320,1280]{1,0:T(8,128)(2,1)}, bf16[320,1280]{1,0:T(8,128)(2,1)}, bf16[1280,256]{1,0:T(8,128)(2,1)S(1)}, ...), branch_computations={%region_8.9_spmd, %region_9.10_spmd} | conditional | bytes 7864472 | solution.py:456
  101.5 3.6 %project_far.6 = bf16[1,640,256]{2,1,0:T(8,128)(2,1)} custom-call(bf16[1280,256]{1,0:T(8,128)(2,1)S(1)} %get-tuple-element.119.refs_0_, bf16[2,1280,256]{2,1,0:T(8,128)(2,1)S(1)} %get-tuple-element.120.refs_1_, bf16[320,1280]{1,0:T(8,128)(2,1)} %get-tuple-element.121.refs_2_, bf16[320,1280]{1,0:T(8,128)(2,1)} %get-tuple-element.122.refs_3_, ...), custom_call_target="tpu_custom_call" | custom-call | tf_op jit(solution)/shard_map/cond/branch_1_fun/project_far/pallas_call | solution.py:708
  105.2 2.8 %collective-permute-done.8 = bf16[640,256]{1,0:T(8,128)(2,1)} collective-permute-done((bf16[640,256]{1,0:T(8,128)(2,1)S(1)}, bf16[640,256]{1,0:T(8,128)(2,1)}, u32[]{:S(2)}, u32[]{:S(2)}) %collective-permute-start.8) | collective-permute-done | bytes 327712 | tf_op jit(solution)/shard_map/cond/branch_1_fun/ppermute | solution.py:28
  108.8 3.0 %project_own.4 = f32[1,640,256]{2,1,0:T(8,128)S(1)} custom-call(bf16[1280,256]{1,0:T(8,128)(2,1)S(1)} %get-tuple-element.227.refs_0_, bf16[2,1280,256]{2,1,0:T(8,128)(2,1)S(1)} %collective-permute-done.23.refs_1_, bf16[320,1280]{1,0:T(8,128)(2,1)} %bitcast.26, bf16[320,1280]{1,0:T(8,128)(2,1)} %collective-permute-done.16.refs_3_, ...), custom_call_target="tpu_custom_call" | custom-call | tf_op jit(solution)/shard_map/project_own/pallas_call | solution.py:708
  111.8 6.8 %conditional.11 = (bf16[1,640,256]{2,1,0:T(8,128)(2,1)S(1)}, bf16[320,1280]{1,0:T(8,128)(2,1)}, bf16[320,1280]{1,0:T(8,128)(2,1)}) conditional(s32[]{:T(128)} %convert_element_type.7, () %tuple.88, (bf16[320,1280]{1,0:T(8,128)(2,1)}, bf16[320,1280]{1,0:T(8,128)(2,1)}, bf16[1280,256]{1,0:T(8,128)(2,1)S(1)}, ...), branch_computations={%region_10.11_spmd, %region_11.12_spmd} | conditional | bytes 6553704 | solution.py:456
  115.7 2.9 %project_far.7 = bf16[1,640,256]{2,1,0:T(8,128)(2,1)S(1)} custom-call(bf16[1280,256]{1,0:T(8,128)(2,1)S(1)} %get-tuple-element.124.refs_0_, bf16[2,1280,256]{2,1,0:T(8,128)(2,1)S(1)} %get-tuple-element.125.refs_1_, bf16[320,1280]{1,0:T(8,128)(2,1)} %get-tuple-element.126.refs_2_, bf16[320,1280]{1,0:T(8,128)(2,1)} %get-tuple-element.127.refs_3_, ...), custom_call_target="tpu_custom_call" | custom-call | tf_op jit(solution)/shard_map/cond/branch_1_fun/project_far/pallas_call | solution.py:708
  119.8 2.9 %project_own.7 = f32[1,640,256]{2,1,0:T(8,128)S(1)} custom-call(bf16[1280,256]{1,0:T(8,128)(2,1)S(1)} %get-tuple-element.227.refs_0_, bf16[2,1280,256]{2,1,0:T(8,128)(2,1)S(1)} %collective-permute-done.23.refs_1_, bf16[320,1280]{1,0:T(8,128)(2,1)} %collective-permute-done.27.refs_2_, bf16[320,1280]{1,0:T(8,128)(2,1)} %collective-permute-done.28.refs_3_, ...), custom_call_target="tpu_custom_call" | custom-call | tf_op jit(solution)/shard_map/project_own/pallas_call | solution.py:708
  122.7 2.9 %project_own.6 = f32[1,640,256]{2,1,0:T(8,128)S(1)} custom-call(bf16[1280,256]{1,0:T(8,128)(2,1)S(1)} %get-tuple-element.227.refs_0_, bf16[2,1280,256]{2,1,0:T(8,128)(2,1)S(1)} %collective-permute-done.23.refs_1_, bf16[320,1280]{1,0:T(8,128)(2,1)} %collective-permute-done.17.refs_2_, bf16[320,1280]{1,0:T(8,128)(2,1)} %collective-permute-done.22.refs_3_, ...), custom_call_target="tpu_custom_call" | custom-call | tf_op jit(solution)/shard_map/project_own/pallas_call | solution.py:708
  125.6 2.9 %project_own.5 = f32[1,640,256]{2,1,0:T(8,128)S(1)} custom-call(bf16[1280,256]{1,0:T(8,128)(2,1)S(1)} %get-tuple-element.227.refs_0_, bf16[2,1280,256]{2,1,0:T(8,128)(2,1)S(1)} %collective-permute-done.23.refs_1_, bf16[320,1280]{1,0:T(8,128)(2,1)} %collective-permute-done.18.refs_2_, bf16[320,1280]{1,0:T(8,128)(2,1)} %collective-permute-done.24.refs_3_, ...), custom_call_target="tpu_custom_call" | custom-call | tf_op jit(solution)/shard_map/project_own/pallas_call | solution.py:708
  128.5 2.8 %assemble.1 = bf16[256,2560]{1,0:T(8,128)(2,1)} custom-call(s32[1]{0:T(128)} %bitcast.5.place_ref, f32[640,256]{1,0:T(8,128)S(1)} %bitcast.17, bf16[640,256]{1,0:T(8,128)(2,1)} %get-tuple-element.228.refs_1_, f32[640,256]{1,0:T(8,128)S(1)} %bitcast.20, bf16[640,256]{1,0:T(8,128)(2,1)} %get-tuple-element.231.refs_3_, f32[640,256]{1,0:T(8,128)S(1)} %bitcast.19, ...), custom_call_target="tpu_custom_call" | custom-call | tf_op jit(solution)/shard_map/assemble/pallas_call | solution.py:776
  (94 shorter events, 48.5 us)
Async XLA Ops:
  0.0 55.4 %collective-permute-start.18 = (bf16[320,1280]{1,0:T(8,128)(2,1)}, bf16[320,1280]{1,0:T(8,128)(2,1)}, u32[]{:S(2)}, u32[]{:S(2)}) collective-permute-start(bf16[320,1280]{1,0:T(8,128)(2,1)} %bitcast.23), channel_id=1, source_target_pairs={{0,16},{4,20},{8,24},{12,28},{16,0},{20,4},{24,8},{28,12},{1,17},{... | collective-permute-start | bytes 2457608 | tf_op jit(solution)/shard_map/ppermute | solution.py:28
  4.0 51.4 %collective-permute-start.16 = (bf16[320,1280]{1,0:T(8,128)(2,1)}, bf16[320,1280]{1,0:T(8,128)(2,1)}, u32[]{:S(2)}, u32[]{:S(2)}) collective-permute-start(bf16[320,1280]{1,0:T(8,128)(2,1)} %bitcast.24), channel_id=1, source_target_pairs={{0,4},{4,0},{8,12},{12,8},{16,20},{20,16},{24,28},{28,24},{1,5},{5... | collective-permute-start | bytes 2457608 | tf_op jit(solution)/shard_map/ppermute | solution.py:28
  5.5 49.9 %collective-permute-start.17 = (bf16[320,1280]{1,0:T(8,128)(2,1)}, bf16[320,1280]{1,0:T(8,128)(2,1)}, u32[]{:S(2)}, u32[]{:S(2)}) collective-permute-start(bf16[320,1280]{1,0:T(8,128)(2,1)} %bitcast.25), channel_id=1, source_target_pairs={{0,8},{4,12},{8,0},{12,4},{16,24},{20,28},{24,16},{28,20},{1,9},{5... | collective-permute-start | bytes 2457608 | tf_op jit(solution)/shard_map/ppermute | solution.py:28
  9.0 4.9 %collective-permute-start.13 = (f32[2,20,256]{2,1,0:T(8,128)S(1)}, f32[2,20,256]{2,1,0:T(8,128)S(1)}, u32[]{:S(2)}, u32[]{:S(2)}) collective-permute-start(f32[2,20,256]{2,1,0:T(8,128)S(1)} %get-tuple-element.192), channel_id=1, source_target_pairs={{0,2},{1,3},{2,0},{3,1},{4,6},{5,7},{6,4},{7,5},{8,10},{9,11},{10,... | collective-permute-start | bytes 122888 | tf_op jit(solution)/shard_map/ppermute | solution.py:28
  13.9 8.3 %collective-permute-start.15 = (bf16[1280,128]{1,0:T(8,128)(2,1)S(1)}, bf16[1280,128]{1,0:T(8,128)(2,1)S(1)}, u32[]{:S(2)}, u32[]{:S(2)}) collective-permute-start(bf16[1280,128]{1,0:T(8,128)(2,1)S(1)} %get-tuple-element.196.refs_2_), channel_id=1, source_target_pairs={{0,2},{1,3},{2,0},{3,1},{4,6},{5,7},{6,4},{7,5},{8,10},{9,11},{10,... | collective-permute-start | bytes 983048 | tf_op jit(solution)/shard_map/ppermute | solution.py:28
  22.2 7.6 %collective-permute-start.12 = (bf16[1280,256]{1,0:T(8,128)(2,1)}, bf16[1280,256]{1,0:T(8,128)(2,1)S(1)}, u32[]{:S(2)}, u32[]{:S(2)}) collective-permute-start(bf16[1280,256]{1,0:T(8,128)(2,1)} %get-tuple-element.88), channel_id=1, source_target_pairs={{0,1},{1,0},{2,3},{3,2},{4,5},{5,4},{6,7},{7,6},{8,9},{9,8},{10,11... | collective-permute-start | bytes 1966088 | tf_op jit(solution)/shard_map/cond/branch_1_fun/ppermute | solution.py:28
  22.9 9.6 %collective-permute-start.11 = (bf16[1280,128]{1,0:T(8,128)(2,1)}, bf16[1280,128]{1,0:T(8,128)(2,1)S(1)}, u32[]{:S(2)}, u32[]{:S(2)}) collective-permute-start(bf16[1280,128]{1,0:T(8,128)(2,1)} %copy-done.8), channel_id=1, source_target_pairs={{0,2},{1,3},{2,0},{3,1},{4,6},{5,7},{6,4},{7,5},{8,10},{9,11},{10,... | collective-permute-start | bytes 983048 | tf_op jit(solution)/shard_map/cond/branch_1_fun/ppermute | solution.py:28
  33.6 23.6 %collective-permute-start.20 = (bf16[1280,384]{1,0:T(8,128)(2,1)}, bf16[1280,384]{1,0:T(8,128)(2,1)S(1)}, u32[]{:S(2)}, u32[]{:S(2)}) collective-permute-start(bf16[1280,384]{1,0:T(8,128)(2,1)} %get-tuple-element.205), channel_id=1, source_target_pairs={{0,2},{1,3},{2,0},{3,1},{4,6},{5,7},{6,4},{7,5},{8,10},{9,11},{10,... | collective-permute-start | bytes 2949128 | tf_op jit(solution)/shard_map/ppermute | solution.py:28
  34.4 8.9 %collective-permute-start.1 = (bf16[1312,128]{1,0:T(8,128)(2,1)S(1)}, bf16[1312,128]{1,0:T(8,128)(2,1)}, u32[]{:S(2)}, u32[]{:S(2)}) collective-permute-start(bf16[1312,128]{1,0:T(8,128)(2,1)S(1)} %get-tuple-element.99), channel_id=1, source_target_pairs={{0,4},{4,0},{8,12},{12,8},{16,20},{20,16},{24,28},{28,24},{1,5},{5... | collective-permute-start | bytes 1007624 | tf_op jit(solution)/shard_map/cond/branch_1_fun/ppermute | solution.py:28
  45.3 8.1 %collective-permute-start.2 = (bf16[1312,128]{1,0:T(8,128)(2,1)}, bf16[1312,128]{1,0:T(8,128)(2,1)}, u32[]{:S(2)}, u32[]{:S(2)}) collective-permute-start(bf16[1312,128]{1,0:T(8,128)(2,1)} %get-tuple-element.103), channel_id=1, source_target_pairs={{0,8},{4,12},{8,0},{12,4},{16,24},{20,28},{24,16},{28,20},{1,9},{5... | collective-permute-start | bytes 1007624 | tf_op jit(solution)/shard_map/cond/branch_1_fun/ppermute | solution.py:28
  55.5 18.6 %collective-permute-start.21 = (bf16[1312,128]{1,0:T(8,128)(2,1)}, bf16[1312,128]{1,0:T(8,128)(2,1)S(1)}, u32[]{:S(2)}, u32[]{:S(2)}) collective-permute-start(bf16[1312,128]{1,0:T(8,128)(2,1)} %get-tuple-element.203), channel_id=1, source_target_pairs={{0,16},{4,20},{8,24},{12,28},{16,0},{20,4},{24,8},{28,12},{1,17},{... | collective-permute-start | bytes 1007624 | tf_op jit(solution)/shard_map/ppermute | solution.py:28
  55.9 27.8 %collective-permute-start.22 = (bf16[320,1280]{1,0:T(8,128)(2,1)}, bf16[320,1280]{1,0:T(8,128)(2,1)}, u32[]{:S(2)}, u32[]{:S(2)}) collective-permute-start(bf16[320,1280]{1,0:T(8,128)(2,1)} %collective-permute-done.18.refs_2_), channel_id=1, source_target_pairs={{0,8},{4,12},{8,0},{12,4},{16,24},{20,28},{24,16},{28,20},{1,9},{5... | collective-permute-start | bytes 2457608 | tf_op jit(solution)/shard_map/ppermute | solution.py:28
  56.4 27.3 %collective-permute-start.24 = (bf16[320,1280]{1,0:T(8,128)(2,1)}, bf16[320,1280]{1,0:T(8,128)(2,1)}, u32[]{:S(2)}, u32[]{:S(2)}) collective-permute-start(bf16[320,1280]{1,0:T(8,128)(2,1)} %collective-permute-done.18.refs_2_), channel_id=1, source_target_pairs={{0,4},{4,0},{8,12},{12,8},{16,20},{20,16},{24,28},{28,24},{1,5},{5... | collective-permute-start | bytes 2457608 | tf_op jit(solution)/shard_map/ppermute | solution.py:28
  76.0 8.6 %collective-permute-start.23 = (bf16[2,1280,256]{2,1,0:T(8,128)(2,1)S(1)}, bf16[2,1280,256]{2,1,0:T(8,128)(2,1)S(1)}, u32[]{:S(2)}, u32[]{:S(2)}) collective-permute-start(bf16[2,1280,256]{2,1,0:T(8,128)(2,1)S(1)} %get-tuple-element.222), channel_id=1, source_target_pairs={{0,1},{1,0},{2,3},{3,2},{4,5},{5,4},{6,7},{7,6},{8,9},{9,8},{10,11... | collective-permute-start | bytes 3932168 | tf_op jit(solution)/shard_map/ppermute | solution.py:28
  76.1 8.5 %collective-permute-start.26 = (bf16[320,1280]{1,0:T(8,128)(2,1)}, bf16[320,1280]{1,0:T(8,128)(2,1)}, u32[]{:S(2)}, u32[]{:S(2)}) collective-permute-start(bf16[320,1280]{1,0:T(8,128)(2,1)} %collective-permute-done.16.refs_3_), channel_id=1, source_target_pairs={{0,1},{1,0},{2,3},{3,2},{4,5},{5,4},{6,7},{7,6},{8,9},{9,8},{10,11... | collective-permute-start | bytes 2457608 | tf_op jit(solution)/shard_map/ppermute | solution.py:28
  76.6 8.0 %collective-permute-start.25 = (bf16[320,1280]{1,0:T(8,128)(2,1)S(1)}, bf16[320,1280]{1,0:T(8,128)(2,1)}, u32[]{:S(2)}, u32[]{:S(2)}) collective-permute-start(bf16[320,1280]{1,0:T(8,128)(2,1)S(1)} %bitcast.27), channel_id=1, source_target_pairs={{0,1},{1,0},{2,3},{3,2},{4,5},{5,4},{6,7},{7,6},{8,9},{9,8},{10,11... | collective-permute-start | bytes 2457608 | tf_op jit(solution)/shard_map/ppermute | solution.py:28
  83.7 24.2 %collective-permute-start.27 = (bf16[320,1280]{1,0:T(8,128)(2,1)}, bf16[320,1280]{1,0:T(8,128)(2,1)}, u32[]{:S(2)}, u32[]{:S(2)}) collective-permute-start(bf16[320,1280]{1,0:T(8,128)(2,1)} %collective-permute-done.16.refs_3_), channel_id=1, source_target_pairs={{0,8},{4,12},{8,0},{12,4},{16,24},{20,28},{24,16},{28,20},{1,9},{5... | collective-permute-start | bytes 2457608 | tf_op jit(solution)/shard_map/ppermute | solution.py:28
  84.0 23.9 %collective-permute-start.28 = (bf16[320,1280]{1,0:T(8,128)(2,1)}, bf16[320,1280]{1,0:T(8,128)(2,1)}, u32[]{:S(2)}, u32[]{:S(2)}) collective-permute-start(bf16[320,1280]{1,0:T(8,128)(2,1)} %collective-permute-done.22.refs_3_), channel_id=1, source_target_pairs={{0,4},{4,0},{8,12},{12,8},{16,20},{20,16},{24,28},{28,24},{1,5},{5... | collective-permute-start | bytes 2457608 | tf_op jit(solution)/shard_map/ppermute | solution.py:28
  84.6 4.1 %collective-permute-start.3 = (bf16[320,1280]{1,0:T(8,128)(2,1)}, bf16[320,1280]{1,0:T(8,128)(2,1)}, u32[]{:S(2)}, u32[]{:S(2)}) collective-permute-start(bf16[320,1280]{1,0:T(8,128)(2,1)} %get-tuple-element.113.refs_2_), channel_id=1, source_target_pairs={{0,1},{1,0},{2,3},{3,2},{4,5},{5,4},{6,7},{7,6},{8,9},{9,8},{10,11... | collective-permute-start | bytes 2457608 | tf_op jit(solution)/shard_map/cond/branch_1_fun/ppermute | solution.py:28
  84.7 4.1 %collective-permute-start.4 = (bf16[320,1280]{1,0:T(8,128)(2,1)}, bf16[320,1280]{1,0:T(8,128)(2,1)}, u32[]{:S(2)}, u32[]{:S(2)}) collective-permute-start(bf16[320,1280]{1,0:T(8,128)(2,1)} %get-tuple-element.114.refs_3_), channel_id=1, source_target_pairs={{0,1},{1,0},{2,3},{3,2},{4,5},{5,4},{6,7},{7,6},{8,9},{9,8},{10,11... | collective-permute-start | bytes 2457608 | tf_op jit(solution)/shard_map/cond/branch_1_fun/ppermute | solution.py:28
  87.8 9.9 %collective-permute-start.5 = (bf16[640,256]{1,0:T(8,128)(2,1)S(1)}, bf16[640,256]{1,0:T(8,128)(2,1)}, u32[]{:S(2)}, u32[]{:S(2)}) collective-permute-start(bf16[640,256]{1,0:T(8,128)(2,1)S(1)} %bitcast.22), channel_id=1, source_target_pairs={{0,2},{1,3},{2,0},{3,1},{4,6},{5,7},{6,4},{7,5},{8,10},{9,11},{10,... | collective-permute-start | bytes 983048 | tf_op jit(solution)/shard_map/cond/branch_1_fun/ppermute | solution.py:28
  98.2 9.7 %collective-permute-start.8 = (bf16[640,256]{1,0:T(8,128)(2,1)S(1)}, bf16[640,256]{1,0:T(8,128)(2,1)}, u32[]{:S(2)}, u32[]{:S(2)}) collective-permute-start(bf16[640,256]{1,0:T(8,128)(2,1)S(1)} %bitcast.32), channel_id=1, source_target_pairs={{0,2},{1,3},{2,0},{3,1},{4,6},{5,7},{6,4},{7,5},{8,10},{9,11},{10,... | collective-permute-start | bytes 983048 | tf_op jit(solution)/shard_map/cond/branch_1_fun/ppermute | solution.py:28
  107.9 10.6 %collective-permute-start.29 = (bf16[640,256]{1,0:T(8,128)(2,1)}, bf16[640,256]{1,0:T(8,128)(2,1)S(1)}, u32[]{:S(2)}, u32[]{:S(2)}) collective-permute-start(bf16[640,256]{1,0:T(8,128)(2,1)} %bitcast.12), channel_id=1, source_target_pairs={{0,2},{1,3},{2,0},{3,1},{4,6},{5,7},{6,4},{7,5},{8,10},{9,11},{10,... | collective-permute-start | bytes 983048 | tf_op jit(solution)/shard_map/ppermute | solution.py:28
  118.6 9.9 %collective-permute-start.30 = (bf16[640,256]{1,0:T(8,128)(2,1)S(1)}, bf16[640,256]{1,0:T(8,128)(2,1)S(1)}, u32[]{:S(2)}, u32[]{:S(2)}) collective-permute-start(bf16[640,256]{1,0:T(8,128)(2,1)S(1)} %bitcast.33), channel_id=1, source_target_pairs={{0,2},{1,3},{2,0},{3,1},{4,6},{5,7},{6,4},{7,5},{8,10},{9,11},{10,... | collective-permute-start | bytes 983048 | tf_op jit(solution)/shard_map/ppermute | solution.py:28
  (18 other events, 154.6 us)

commit v3 on v2

--- a/solution.py
+++ b/solution.py
@@ -344,7 +344,7 @@
 def finish_kernel(
     half, me_ref, pre_ref, reader_ref, cross_ref, factor_ref, state_ref, gain_ref, *refs
 ):
-    keep_refs, send_ref = refs[:half], refs[half]
+    keep_refs, send_refs = refs[:half], refs[half:]
     groups, channels, _ = pre_ref.shape
     head_count = cross_ref.shape[2]
     width = channels // head_count
@@ -363,7 +363,7 @@
             if r % 2 == 0:
                 keep_refs[r // 2][at, :] = normed.astype(BF16)
             else:
-                send_ref[r // 2, at, :] = normed.astype(BF16)
+                send_refs[r // 2][at, :] = normed.astype(BF16)
 
 
 def project_kernel(*refs):
@@ -375,7 +375,7 @@
     width = weights[0].shape[0]
     for i, (kept_ref, other_ref) in enumerate(zip(kept_refs, other_refs)):
         for j, (weight, partner) in enumerate(zip(weights, partners)):
-            found = dot(weight[...], kept_ref[...]) + dot(partner[...], other_ref[0])
+            found = dot(weight[...], kept_ref[...]) + dot(partner[...], other_ref[...])
             out_ref[i, j * width : (j + 1) * width, :] = found.astype(out_ref.dtype)
 
 
@@ -610,7 +610,8 @@
         )(keep, core_states, total, *got_states)
         return running, sent, tables, moved
 
-    def near_steps(running, total, sent):
+    def near_steps(running, total, sent, beside):
+        beside = swap(beside, "head", 1)
         offset = jnp.zeros((extra, LANES), F32)
         factors = [jnp.broadcast_to((position % 2).astype(F32), (extra, LANES))]
         states = []
@@ -618,7 +619,7 @@
             states.append(swap(sent, "ctx", 2**bit))
             total, offset, factor, sent, running = step(bit, running, total, offset, states[-1])
             factors.append(factor)
-        return states, factors, sent
+        return states, factors, sent, beside
 
     running, sent, tables, moved = fenced(
         chip_sum, keep, core_states, tie(far_states, value_head), total, decays, level_class,
@@ -632,7 +633,8 @@
     for r in range(4, heads_size, 2):
         passed[r] = swap(tie(portion[r, 0], *after), "head", r)
         after = [passed[r]]
-    states, factors, sent = fenced(near_steps, running, total, sent)
+    sent = tie(sent, held[1])
+    states, factors, sent, beside = fenced(near_steps, running, total, sent, portion[1, 0])
     states = list(states)
     sent = tie(sent, *[held[2**bit] for bit in range(ctx_bits)])
     last_state = swap(sent, "ctx", 2**near)
@@ -643,14 +645,13 @@
             held[r] = swap(tie(held[r ^ low], sent), "ctx", low)
     for bit in range(2, ctx_bits):
         held[2**bit + 1] = swap(tie(held[2**bit], sent), "ctx", 1)
-    for r in (0, 1):
-        partners[r] = swap(tie(held[r], sent), "head", 1)
+    partners[0] = swap(tie(held[0], sent), "head", 1)
 
     skips = jnp.broadcast_to(skip_gain[:, None], (head_count, rows_dev))
     gains = norm_gain[:, None]
 
     lift, read, cross, merge, scores, masked, readers, pairs = tables
-    arrays = [portion[0, 0], swap(tie(portion[1, 0], sent), "head", 1), value_head]
+    arrays = [portion[0, 0], beside, value_head]
     pieces = [[(0, 0, rows_dev)], [(1, 0, rows_dev)], [(2, 0, early)]]
     for r in range(3, heads_size):
         first = rows_dev - early if r == 3 else 0
@@ -674,10 +675,10 @@
         me1, *arrays, lift, read, merge, scores, masked, readers, pairs, skips, cross,
         *factors[:near], *states,
     )
-    *kept, sides = kernel_call(
+    normed = kernel_call(
         functools.partial(finish_kernel, half),
         "finish",
-        tuple([shape((features, rows_dev))] * half + [shape((half, features, rows_dev))]),
+        tuple([shape((features, rows_dev))] * heads_size),
         grid=(1,),
         in_specs=[
             smem,
@@ -688,39 +689,30 @@
             whole((features + extra, state_size)),
             whole((features, 1)),
         ],
-        out_specs=[whole((features, rows_dev))] * half + [whole((half, features, rows_dev))],
+        out_specs=[whole((features, rows_dev))] * heads_size,
     )(me1, pre, readers, cross, factors[near], last_state, gains)
-    done = [held[r] for r in held if r not in (0, 1)] + [kept[0]]
+    kept, sides = normed[:half], normed[half:]
     early_blocks = sorted(held)
-    held[3] = swap(tie(held[1], *done), "ctx", 2)
-    for r in range(5, ctx_size, 2):
-        if r not in held:
-            held[r] = swap(tie(held[r ^ 1], *done), "ctx", 1)
-
     order = sorted(early_blocks, key=lambda r: (r // 2 * 2 not in early_blocks or r ^ 1 not in early_blocks, r))
     order += [r for r in range(ctx_size) if r not in early_blocks]
     count = 2
     groups = [order[first : first + count] for first in range(0, ctx_size, count)]
-    others = swap(sides, "head", 1)
-
-    def project(name, first, kept, others, group, blocks, partners, kind):
+    others = [swap(side, "head", 1) for side in sides[1:]]
+
+    def project(name, kept, others, group, blocks, partners, kind):
         rows = len(kept)
         return kernel_call(
             project_kernel,
             name,
             shape((rows, count * columns, rows_dev), kind),
-            in_specs=[whole((features, rows_dev))] * rows
-            + [part(others, first + i) for i in range(rows)]
-            + [whole((columns, features))] * (2 * count),
-            out_specs=whole((rows, count * columns, rows_dev)),
-            grid=(1,),
-        )(*kept, *[others] * rows, *[blocks[r] for r in group], *[partners[r] for r in group])
+            in_specs=[vmem] * (2 * rows + 2 * count),
+        )(*kept, *others, *[blocks[r] for r in group], *[partners[r] for r in group])
 
     def far_rows(group, kept, others, blocks, partners):
-        return project("project_far", 1, kept[1:], others, group, blocks, partners, BF16)
+        return project("project_far", kept[1:], others, group, blocks, partners, BF16)
 
     def own_rows(group, kept, others, blocks, partners):
-        return project("project_own", 0, kept[:1], others, group, blocks, partners, F32)[0]
+        return project("project_own", kept[:1], others, group, blocks, partners, F32)[0]
 
     def send_rows(far, *after):
         far = tie(far, *after)
@@ -730,49 +722,41 @@
         more = {r: swap(blocks[r], "head", 1) for r in blocks if r not in partners}
         return {**partners, **more}, more
 
-    def first_groups(kept, others, blocks, partners):
-        partners, more = with_partners(blocks, partners)
-        got = send_rows(far_rows(groups[0], kept, others, blocks, partners))
-        return far_rows(groups[1], kept, others, blocks, partners), got, more
-
-    def middle_group(index):
-        def body(far, kept, others, blocks, partners):
+    def group_of(index):
+        def body(kept, others, blocks, partners):
             partners, more = with_partners(blocks, partners)
-            return far_rows(groups[index], kept, others, blocks, partners), send_rows(far), more
+            return far_rows(groups[index], kept, others, blocks, partners), more
 
         return body
-
-    def last_group(kept, others, blocks, partners):
-        partners, more = with_partners(blocks, partners)
-        return far_rows(groups[-1], kept, others, blocks, partners), more
 
     def some(array, group):
         return {r: array[r] for r in group if r in array}
 
-    arrived = []
-    far, got, more = fenced(
-        first_groups, kept, others, some(held, groups[0] + groups[1]), some(partners, groups[0] + groups[1])
-    )
-    arrived.append(got)
-    partners.update(more)
-    for index in range(2, len(groups) - 1):
-        far, got, more = fenced(
-            middle_group(index), far, kept, others, some(held, groups[index]), some(partners, groups[index])
-        )
-        arrived.append(got)
+    arrived, owns = [], {}
+    for index, group in enumerate(groups):
+        last = index + 1 == len(groups)
+        blocks = some(held, group)
+        if last:
+            owns[0] = own_rows(groups[0], [tie(kept[0], far)], [own_other], held, partners)
+            blocks[group[0]] = tie(blocks[group[0]], owns[0])
+        far, more = fenced(group_of(index), kept, others, blocks, some(partners, group))
         partners.update(more)
-    got = send_rows(far, *[held[r] for r in groups[-1]])
-    arrived.append(got)
-    ahead = own_rows(groups[0], [tie(kept[0], far)], others, held, partners)
-    blocks = some(held, groups[-1])
-    blocks[groups[-1][0]] = tie(blocks[groups[-1][0]], ahead)
-    far, more = fenced(last_group, kept, others, blocks, some(partners, groups[-1]))
-    partners.update(more)
-    arrived.append(send_rows(far, *got))
+        after = list(arrived[-1]) if arrived else []
+        if index + 2 == len(groups):
+            after += [held[r] for r in groups[-1]]
+        arrived.append(send_rows(far, *after))
+        if index == 0:
+            ready = [held[r] for r in held if r not in (0, 1)] + [far]
+            held[3] = swap(tie(held[1], *ready), "ctx", 2)
+            for r in range(5, ctx_size, 2):
+                if r not in held:
+                    held[r] = swap(tie(held[r ^ 1], *ready), "ctx", 1)
+            own_other = swap(tie(sides[0], far), "head", 1)
     pieces = []
-    for group, got in zip(groups, arrived):
-        own = ahead if group == groups[0] else own_rows(group, kept, others, held, partners)
-        pieces += [own] + got
+    for index, (group, got) in enumerate(zip(groups, arrived)):
+        if index not in owns:
+            owns[index] = own_rows(group, kept, [own_other], held, partners)
+        pieces += [owns[index]] + got
     return kernel_call(
         functools.partial(assemble_kernel, groups),
         "assemble",

time: 132 us -> 137 us (1.038)
  starting transfers between devices: 20.5 us -> 24.8 us
    ppermute x31 -> x32, starting transfers between devices: 20.5 us -> 24.8 us  [swap(): return lax.ppermute(value, axis, pairs)]
    ppermute x31 -> x32, waiting for transfers between devices: 49.6 us -> 50.5 us  [swap(): return lax.ppermute(value, axis, pairs)]
  transfers between devices with their start and end apart: 31 -> 32, of which waited for: 15 -> 16; matrix products, arithmetic and copies ran while one was open for 3% -> 3% of each run, Pallas kernels for 39% -> 38%
where the time goes in v3:
time: 137 us
  Pallas kernels  55.3 us (40%)
  waiting for transfers between devices  50.5 us (37%)
  starting transfers between devices  24.8 us (18%)
  local copies, waits for them, and re-layouts  5.84 us (4%)
    ppermute x32, waiting for transfers between devices, swap(): return lax.ppermute(value, axis, pairs)  50.5 us
    ppermute x32, starting transfers between devices, swap(): return lax.ppermute(value, axis, pairs)  24.8 us
    pallas_call x8, Pallas kernels, project(): kernel_call(project_kernel, name, shape((rows, count * columns, rows_dev)...  24.7 us
    pallas_call x1, Pallas kernels, on_device(): kernel_call(functools.partial(local_kernel, near, pieces), 'local_levels'...  11 us
    pallas_call x2, Pallas kernels, step(): kernel_call(functools.partial(merge_kernel, bit, head_count), 'merge', tu...  3.75 us
    pallas_call x1, Pallas kernels, chip_sum(): kernel_call(functools.partial(factors_kernel, levels, heads_size), 'facto...  3.61 us
  transfers between devices with their start and end apart: 32, of which 16 were waited for; matrix products, arithmetic and copies ran while one was open for 3% of the time, Pallas kernels for 38%

profile of v3, /device:TPU:0, one launch (start us, length us, event | category | flops | bytes accessed | tf_op | source)
XLA Modules:
  0.0 136.7 jit_solution(3835262237940530446)
XLA Ops:
  1.9 3.0 %collective-permute-start.13 = (f32[2,20,256]{2,1,0:T(8,128)S(1)}, f32[2,20,256]{2,1,0:T(8,128)S(1)}, u32[]{:S(2)}, u32[]{:S(2)}) collective-permute-start(f32[2,20,256]{2,1,0:T(8,128)S(1)} %get-tuple-element.198), channel_id=1, source_target_pairs={{0,2},{1,3},{2,0},{3,1},{4,6},{5,7},{6,4},{7,5},{8,10},{9,11},{10,... | collective-permute-start | bytes 122888 | tf_op jit(solution)/shard_map/ppermute | solution.py:28
  10.5 2.6 %collective-permute-start.19 = (bf16[320,1280]{1,0:T(8,128)(2,1)}, bf16[320,1280]{1,0:T(8,128)(2,1)}, u32[]{:S(2)}, u32[]{:S(2)}) collective-permute-start(bf16[320,1280]{1,0:T(8,128)(2,1)} %bitcast.6.refs_2_), channel_id=1, source_target_pairs={{0,16},{4,20},{8,24},{12,28},{16,0},{20,4},{24,8},{28,12},{1,17},{... | collective-permute-start | bytes 2457608 | tf_op jit(solution)/shard_map/ppermute | solution.py:28
  18.1 3.3 %conditional.7 = (bf16[2,1280,128]{2,1,0:T(8,128)(2,1)}, bf16[1280,128]{1,0:T(8,128)(2,1)S(1)}) conditional(s32[]{:T(128)} %convert_element_type.7, () %tuple.78, (bf16[2,1280,128]{2,1,0:T(8,128)(2,1)S(1)}, f32[2,1280,128]{2,1,0:T(8,128)S(1)}) %tuple.79), branch_computations={%region_0.0_spmd, %region_1.0_spmd} | conditional | bytes 2621496 | solution.py:456
  21.4 11.8 %conditional.8 = (f32[1280,128]{1,0:T(8,128)S(1)}, bf16[1312,128]{1,0:T(8,128)(2,1)S(1)}, f32[4,20,256]{2,1,0:T(8,128)}, f32[5,4,20,256]{3,2,1,0:T(8,128)}, f32[...) conditional(s32[]{:T(128)} %convert_element_type.7, () %tuple.77, ...), branch_computations={%region_2.0_spmd, %region_3.4_spmd} | conditional | bytes 7295176 | solution.py:456
  25.3 3.6 %factors.1 = (f32[4,20,256]{2,1,0:T(8,128)}, f32[5,4,20,256]{3,2,1,0:T(8,128)}, f32[3,4,20,256]{3,2,1,0:T(8,128)}, f32[26,20,128]{2,1,0:T(8,128)}, bf16[4,2,256,...) custom-call(f32[20,1024]{1,0:T(8,128)S(1)} %get-tuple-element.83.dec, ...), custom_call_target="tpu_custom_call" | custom-call | tf_op jit(solution)/shard_map/cond/branch_1_fun/factors/pallas_call | solution.py:581
  34.7 23.0 %conditional.9 = (bf16[1312,128]{1,0:T(8,128)(2,1)}, bf16[1312,128]{1,0:T(8,128)(2,1)}, f32[32,128]{1,0:T(8,128)S(1)}, f32[32,128]{1,0:T(8,128)}, f32[32,128]{1,...) conditional(s32[]{:T(128)} %convert_element_type.7, () %tuple.76, ...), branch_computations={%region_4.5_spmd, %region_5.6_spmd} | conditional | flops 12 | bytes 5341485 | solution.py:456
  35.3 8.5 %collective-permute-done.1.got_ref = bf16[1312,128]{1,0:T(8,128)(2,1)} collective-permute-done((bf16[1312,128]{1,0:T(8,128)(2,1)S(1)}, bf16[1312,128]{1,0:T(8,128)(2,1)}, u32[]{:S(2)}, u32[]{:S(2)}) %collective-permute-start.1) | collective-permute-done | bytes 335904 | tf_op jit(solution)/shard_map/cond/branch_1_fun/ppermute | solution.py:28
  46.0 9.7 %collective-permute-done.2.got_ref = bf16[1312,128]{1,0:T(8,128)(2,1)} collective-permute-done((bf16[1312,128]{1,0:T(8,128)(2,1)S(1)}, bf16[1312,128]{1,0:T(8,128)(2,1)}, u32[]{:S(2)}, u32[]{:S(2)}) %collective-permute-start.2) | collective-permute-done | bytes 335904 | tf_op jit(solution)/shard_map/cond/branch_1_fun/ppermute | solution.py:28
  63.0 11.0 %local_levels.1.pre_ref = f32[4,1280,256]{2,1,0:T(8,128)S(1)} custom-call(s32[1]{0:T(128)} %bitcast.4.me_ref, bf16[1280,256]{1,0:T(8,128)(2,1)S(1)} %get-tuple-element.191.refs_0_, bf16[1280,256]{1,0:T(8,128)(2,1)} %get-tuple-element.209.refs_1_, bf16[1280,128]{1,0:T(8,128)(2,1)S(1)} %collective-permute-done.15.refs_2_, ...), custom_call_target="tpu_custom_call" | custom-call | tf_op jit(solution)/shard_map/local_levels/pallas_call | solution.py:662
  75.3 2.6 %finish.1 = (bf16[1280,256]{1,0:T(8,128)(2,1)S(1)}, bf16[1280,256]{1,0:T(8,128)(2,1)S(1)}, bf16[1280,256]{1,0:T(8,128)(2,1)S(1)}, bf16[1280,256]{1,0:T(8,128)(2,1)S(1)}) custom-call(s32[1]{0:T(128)} %bitcast.4.me_ref, f32[4,1280,256]{2,1,0:T(8,128)S(1)} %local_levels.1.pre_ref, bf16[4,256,256]{2,1,0:T(8,128)(2,1)S(1)} %get-tuple-element.216.refs_9_.reader_ref, ...), custom_call_target="tpu_custom_call" | custom-call | tf_op jit(solution)/shard_map/finish/pallas_call | solution.py:678
  80.2 5.8 %conditional.11 = (bf16[1,640,256]{2,1,0:T(8,128)(2,1)S(1)}, bf16[320,1280]{1,0:T(8,128)(2,1)}) conditional(s32[]{:T(128)} %convert_element_type.7, () %tuple.90, (bf16[320,1280]{1,0:T(8,128)(2,1)}, bf16[1280,256]{1,0:T(8,128)(2,1)S(1)}, bf16[1280,256]{1,0:T(8,128)(2,1)}, bf16[320,1280]{1,0:T(8,128)(2,1)}, bf16[320,1280]{1,0:T(8,128)(2,1)}) %tuple.92), branch_computations={%region_8.9_spmd, %region_9.10_spmd} | conditional | bytes 3276856 | solution.py:456
  80.3 2.5 %collective-permute-done.6.refs_5_ = bf16[320,1280]{1,0:T(8,128)(2,1)} collective-permute-done((bf16[320,1280]{1,0:T(8,128)(2,1)}, bf16[320,1280]{1,0:T(8,128)(2,1)}, u32[]{:S(2)}, u32[]{:S(2)}) %collective-permute-start.6) | collective-permute-done | bytes 819232 | tf_op jit(solution)/shard_map/cond/branch_1_fun/ppermute | solution.py:28
  82.9 3.1 %project_far.5 = bf16[1,640,256]{2,1,0:T(8,128)(2,1)S(1)} custom-call(bf16[1280,256]{1,0:T(8,128)(2,1)S(1)} %get-tuple-element.118.refs_0_, bf16[1280,256]{1,0:T(8,128)(2,1)} %get-tuple-element.119.refs_1_, bf16[320,1280]{1,0:T(8,128)(2,1)} %get-tuple-element.120.refs_2_, bf16[320,1280]{1,0:T(8,128)(2,1)} %get-tuple-element.121.refs_3_, ...), custom_call_target="tpu_custom_call" | custom-call | tf_op jit(solution)/shard_map/cond/branch_1_fun/project_far/pallas_call | solution.py:704
  89.3 6.9 %conditional.10 = (bf16[1,640,256]{2,1,0:T(8,128)(2,1)S(1)}, bf16[320,1280]{1,0:T(8,128)(2,1)}, bf16[320,1280]{1,0:T(8,128)(2,1)}) conditional(s32[]{:T(128)} %convert_element_type.7, () %tuple.86, (bf16[320,1280]{1,0:T(8,128)(2,1)}, bf16[320,1280]{1,0:T(8,128)(2,1)}, bf16[1280,256]{1,0:T(8,128)(2,1)S(1)}, bf16[1280,256]{1,0:T(8,128)(2,1)}) %tuple.88), branch_computations={%region_6.7_spmd, %region_7.8_spmd} | conditional | bytes 6553704 | solution.py:456
  93.2 3.1 %project_far.4 = bf16[1,640,256]{2,1,0:T(8,128)(2,1)S(1)} custom-call(bf16[1280,256]{1,0:T(8,128)(2,1)S(1)} %get-tuple-element.114.refs_0_, bf16[1280,256]{1,0:T(8,128)(2,1)} %get-tuple-element.115.refs_1_, bf16[320,1280]{1,0:T(8,128)(2,1)} %get-tuple-element.116.refs_2_, bf16[320,1280]{1,0:T(8,128)(2,1)} %get-tuple-element.117.refs_3_, ...), custom_call_target="tpu_custom_call" | custom-call | tf_op jit(solution)/shard_map/cond/branch_1_fun/project_far/pallas_call | solution.py:704
  96.3 7.0 %conditional.12 = (bf16[1,640,256]{2,1,0:T(8,128)(2,1)S(1)}, bf16[320,1280]{1,0:T(8,128)(2,1)}, bf16[320,1280]{1,0:T(8,128)(2,1)}) conditional(s32[]{:T(128)} %convert_element_type.7, () %tuple.94, (bf16[320,1280]{1,0:T(8,128)(2,1)}, bf16[320,1280]{1,0:T(8,128)(2,1)}, bf16[1280,256]{1,0:T(8,128)(2,1)S(1)}, bf16[1280,256]{1,0:T(8,128)(2,1)}) %tuple.95), branch_computations={%region_10.11_spmd, %region_11.12_spmd} | conditional | bytes 6553704 | solution.py:456
  100.2 3.1 %project_far.6 = bf16[1,640,256]{2,1,0:T(8,128)(2,1)S(1)} custom-call(bf16[1280,256]{1,0:T(8,128)(2,1)S(1)} %get-tuple-element.123.refs_0_, bf16[1280,256]{1,0:T(8,128)(2,1)} %get-tuple-element.124.refs_1_, bf16[320,1280]{1,0:T(8,128)(2,1)} %get-tuple-element.125.refs_2_, bf16[320,1280]{1,0:T(8,128)(2,1)} %get-tuple-element.126.refs_3_, ...), custom_call_target="tpu_custom_call" | custom-call | tf_op jit(solution)/shard_map/cond/branch_1_fun/project_far/pallas_call | solution.py:704
  103.5 10.0 %collective-permute-done.27.refs_3_ = bf16[640,256]{1,0:T(8,128)(2,1)S(1)} collective-permute-done((bf16[640,256]{1,0:T(8,128)(2,1)S(1)}, bf16[640,256]{1,0:T(8,128)(2,1)S(1)}, u32[]{:S(2)}, u32[]{:S(2)}) %collective-permute-start.27) | collective-permute-done | bytes 327712 | tf_op jit(solution)/shard_map/ppermute | solution.py:28
  113.8 3.0 %project_own.4 = f32[1,640,256]{2,1,0:T(8,128)S(1)} custom-call(bf16[1280,256]{1,0:T(8,128)(2,1)S(1)} %get-tuple-element.231.refs_0_, bf16[1280,256]{1,0:T(8,128)(2,1)S(1)} %collective-permute-done.24.refs_1_, bf16[320,1280]{1,0:T(8,128)(2,1)} %bitcast.6.refs_2_, bf16[320,1280]{1,0:T(8,128)(2,1)} %collective-permute-done.16.refs_3_, ...), custom_call_target="tpu_custom_call" | custom-call | tf_op jit(solution)/shard_map/project_own/pallas_call | solution.py:704
  116.8 7.7 %conditional.13 = (bf16[1,640,256]{2,1,0:T(8,128)(2,1)}, bf16[320,1280]{1,0:T(8,128)(2,1)}, bf16[320,1280]{1,0:T(8,128)(2,1)}) conditional(s32[]{:T(128)} %convert_element_type.7, () %tuple.100, (bf16[320,1280]{1,0:T(8,128)(2,1)}, bf16[320,1280]{1,0:T(8,128)(2,1)}, bf16[1280,256]{1,0:T(8,128)(2,1)S(1)}, bf16[1280,256]{1,0:T(8,128)(2,1)}) %tuple.120), branch_computations={%region_12.13_spmd, %region_13.14_spmd} | conditional | bytes 6553704 | solution.py:456
  120.7 3.8 %project_far.7 = bf16[1,640,256]{2,1,0:T(8,128)(2,1)} custom-call(bf16[1280,256]{1,0:T(8,128)(2,1)S(1)} %get-tuple-element.127.refs_0_, bf16[1280,256]{1,0:T(8,128)(2,1)} %get-tuple-element.128.refs_1_, bf16[320,1280]{1,0:T(8,128)(2,1)} %get-tuple-element.129.refs_2_, bf16[320,1280]{1,0:T(8,128)(2,1)} %get-tuple-element.130.refs_3_, ...), custom_call_target="tpu_custom_call" | custom-call | tf_op jit(solution)/shard_map/cond/branch_1_fun/project_far/pallas_call | solution.py:704
  126.3 2.9 %project_own.6 = f32[1,640,256]{2,1,0:T(8,128)S(1)} custom-call(bf16[1280,256]{1,0:T(8,128)(2,1)S(1)} %get-tuple-element.231.refs_0_, bf16[1280,256]{1,0:T(8,128)(2,1)S(1)} %collective-permute-done.24.refs_1_, bf16[320,1280]{1,0:T(8,128)(2,1)} %collective-permute-done.18.refs_2_, bf16[320,1280]{1,0:T(8,128)(2,1)} %collective-permute-done.21.refs_3_, ...), custom_call_target="tpu_custom_call" | custom-call | tf_op jit(solution)/shard_map/project_own/pallas_call | solution.py:704
  129.1 2.9 %project_own.5 = f32[1,640,256]{2,1,0:T(8,128)S(1)} custom-call(bf16[1280,256]{1,0:T(8,128)(2,1)S(1)} %get-tuple-element.231.refs_0_, bf16[1280,256]{1,0:T(8,128)(2,1)S(1)} %collective-permute-done.24.refs_1_, bf16[320,1280]{1,0:T(8,128)(2,1)} %collective-permute-done.19.refs_2_, bf16[320,1280]{1,0:T(8,128)(2,1)} %collective-permute-done.26.refs_3_, ...), custom_call_target="tpu_custom_call" | custom-call | tf_op jit(solution)/shard_map/project_own/pallas_call | solution.py:704
  132.0 2.9 %project_own.7 = f32[1,640,256]{2,1,0:T(8,128)S(1)} custom-call(bf16[1280,256]{1,0:T(8,128)(2,1)S(1)} %get-tuple-element.231.refs_0_, bf16[1280,256]{1,0:T(8,128)(2,1)S(1)} %collective-permute-done.24.refs_1_, bf16[320,1280]{1,0:T(8,128)(2,1)} %collective-permute-done.28.refs_2_, bf16[320,1280]{1,0:T(8,128)(2,1)} %collective-permute-done.29.refs_3_, ...), custom_call_target="tpu_custom_call" | custom-call | tf_op jit(solution)/shard_map/project_own/pallas_call | solution.py:704
  (93 shorter events, 58.2 us)
Async XLA Ops:
  1.9 6.4 %collective-permute-start.13 = (f32[2,20,256]{2,1,0:T(8,128)S(1)}, f32[2,20,256]{2,1,0:T(8,128)S(1)}, u32[]{:S(2)}, u32[]{:S(2)}) collective-permute-start(f32[2,20,256]{2,1,0:T(8,128)S(1)} %get-tuple-element.198), channel_id=1, source_target_pairs={{0,2},{1,3},{2,0},{3,1},{4,6},{5,7},{6,4},{7,5},{8,10},{9,11},{10,... | collective-permute-start | bytes 122888 | tf_op jit(solution)/shard_map/ppermute | solution.py:28
  8.3 13.1 %collective-permute-start.15 = (bf16[1280,128]{1,0:T(8,128)(2,1)S(1)}, bf16[1280,128]{1,0:T(8,128)(2,1)S(1)}, u32[]{:S(2)}, u32[]{:S(2)}) collective-permute-start(bf16[1280,128]{1,0:T(8,128)(2,1)S(1)} %get-tuple-element.202.refs_2_), channel_id=1, source_target_pairs={{0,2},{1,3},{2,0},{3,1},{4,6},{5,7},{6,4},{7,5},{8,10},{9,11},{10,... | collective-permute-start | bytes 983048 | tf_op jit(solution)/shard_map/ppermute | solution.py:28
  9.0 25.8 %collective-permute-start.16 = (bf16[320,1280]{1,0:T(8,128)(2,1)}, bf16[320,1280]{1,0:T(8,128)(2,1)}, u32[]{:S(2)}, u32[]{:S(2)}) collective-permute-start(bf16[320,1280]{1,0:T(8,128)(2,1)} %bitcast.6.refs_2_), channel_id=1, source_target_pairs={{0,4},{4,0},{8,12},{12,8},{16,20},{20,16},{24,28},{28,24},{1,5},{5... | collective-permute-start | bytes 2457608 | tf_op jit(solution)/shard_map/ppermute | solution.py:28
  10.5 47.2 %collective-permute-start.19 = (bf16[320,1280]{1,0:T(8,128)(2,1)}, bf16[320,1280]{1,0:T(8,128)(2,1)}, u32[]{:S(2)}, u32[]{:S(2)}) collective-permute-start(bf16[320,1280]{1,0:T(8,128)(2,1)} %bitcast.6.refs_2_), channel_id=1, source_target_pairs={{0,16},{4,20},{8,24},{12,28},{16,0},{20,4},{24,8},{28,12},{1,17},{... | collective-permute-start | bytes 2457608 | tf_op jit(solution)/shard_map/ppermute | solution.py:28
  13.0 44.6 %collective-permute-start.18 = (bf16[320,1280]{1,0:T(8,128)(2,1)}, bf16[320,1280]{1,0:T(8,128)(2,1)}, u32[]{:S(2)}, u32[]{:S(2)}) collective-permute-start(bf16[320,1280]{1,0:T(8,128)(2,1)} %bitcast.6.refs_2_), channel_id=1, source_target_pairs={{0,8},{4,12},{8,0},{12,4},{16,24},{20,28},{24,16},{28,20},{1,9},{5... | collective-permute-start | bytes 2457608 | tf_op jit(solution)/shard_map/ppermute | solution.py:28
  21.4 7.4 %collective-permute-start.12 = (bf16[1280,256]{1,0:T(8,128)(2,1)}, bf16[1280,256]{1,0:T(8,128)(2,1)S(1)}, u32[]{:S(2)}, u32[]{:S(2)}) collective-permute-start(bf16[1280,256]{1,0:T(8,128)(2,1)} %get-tuple-element.90), channel_id=1, source_target_pairs={{0,1},{1,0},{2,3},{3,2},{4,5},{5,4},{6,7},{7,6},{8,9},{9,8},{10,11... | collective-permute-start | bytes 1966088 | tf_op jit(solution)/shard_map/cond/branch_1_fun/ppermute | solution.py:28
  22.2 10.0 %collective-permute-start.11 = (bf16[1280,128]{1,0:T(8,128)(2,1)}, bf16[1280,128]{1,0:T(8,128)(2,1)S(1)}, u32[]{:S(2)}, u32[]{:S(2)}) collective-permute-start(bf16[1280,128]{1,0:T(8,128)(2,1)} %copy-done.6), channel_id=1, source_target_pairs={{0,2},{1,3},{2,0},{3,1},{4,6},{5,7},{6,4},{7,5},{8,10},{9,11},{10,... | collective-permute-start | bytes 983048 | tf_op jit(solution)/shard_map/cond/branch_1_fun/ppermute | solution.py:28
  33.3 29.0 %collective-permute-start.17 = (bf16[1280,384]{1,0:T(8,128)(2,1)}, bf16[1280,384]{1,0:T(8,128)(2,1)S(1)}, u32[]{:S(2)}, u32[]{:S(2)}) collective-permute-start(bf16[1280,384]{1,0:T(8,128)(2,1)} %get-tuple-element.210), channel_id=1, source_target_pairs={{0,2},{1,3},{2,0},{3,1},{4,6},{5,7},{6,4},{7,5},{8,10},{9,11},{10,... | collective-permute-start | bytes 2949128 | tf_op jit(solution)/shard_map/ppermute | solution.py:28
  34.7 9.1 %collective-permute-start.1 = (bf16[1312,128]{1,0:T(8,128)(2,1)S(1)}, bf16[1312,128]{1,0:T(8,128)(2,1)}, u32[]{:S(2)}, u32[]{:S(2)}) collective-permute-start(bf16[1312,128]{1,0:T(8,128)(2,1)S(1)} %get-tuple-element.101), channel_id=1, source_target_pairs={{0,4},{4,0},{8,12},{12,8},{16,20},{20,16},{24,28},{28,24},{1,5},{5... | collective-permute-start | bytes 1007624 | tf_op jit(solution)/shard_map/cond/branch_1_fun/ppermute | solution.py:28
  35.3 22.4 %collective-permute-start.3 = (bf16[1280,256]{1,0:T(8,128)(2,1)}, bf16[1280,256]{1,0:T(8,128)(2,1)}, u32[]{:S(2)}, u32[]{:S(2)}) collective-permute-start(bf16[1280,256]{1,0:T(8,128)(2,1)} %get-tuple-element.113), channel_id=1, source_target_pairs={{0,1},{1,0},{2,3},{3,2},{4,5},{5,4},{6,7},{7,6},{8,9},{9,8},{10,11... | collective-permute-start | bytes 1966088 | tf_op jit(solution)/shard_map/cond/branch_1_fun/ppermute | solution.py:28
  45.6 10.1 %collective-permute-start.2 = (bf16[1312,128]{1,0:T(8,128)(2,1)S(1)}, bf16[1312,128]{1,0:T(8,128)(2,1)}, u32[]{:S(2)}, u32[]{:S(2)}) collective-permute-start(bf16[1312,128]{1,0:T(8,128)(2,1)S(1)} %get-tuple-element.105), channel_id=1, source_target_pairs={{0,8},{4,12},{8,0},{12,4},{16,24},{20,28},{24,16},{28,20},{1,9},{5... | collective-permute-start | bytes 1007624 | tf_op jit(solution)/shard_map/cond/branch_1_fun/ppermute | solution.py:28
  57.7 17.6 %collective-permute-start.20 = (bf16[1312,128]{1,0:T(8,128)(2,1)}, bf16[1312,128]{1,0:T(8,128)(2,1)S(1)}, u32[]{:S(2)}, u32[]{:S(2)}) collective-permute-start(bf16[1312,128]{1,0:T(8,128)(2,1)} %get-tuple-element.225), channel_id=1, source_target_pairs={{0,16},{4,20},{8,24},{12,28},{16,0},{20,4},{24,8},{28,12},{1,17},{... | collective-permute-start | bytes 1007624 | tf_op jit(solution)/shard_map/ppermute | solution.py:28
  59.1 18.9 %collective-permute-start.23 = (bf16[320,1280]{1,0:T(8,128)(2,1)}, bf16[320,1280]{1,0:T(8,128)(2,1)}, u32[]{:S(2)}, u32[]{:S(2)}) collective-permute-start(bf16[320,1280]{1,0:T(8,128)(2,1)} %bitcast.6.refs_2_), channel_id=1, source_target_pairs={{0,1},{1,0},{2,3},{3,2},{4,5},{5,4},{6,7},{7,6},{8,9},{9,8},{10,11... | collective-permute-start | bytes 2457608 | tf_op jit(solution)/shard_map/ppermute | solution.py:28
  59.1 27.5 %collective-permute-start.21 = (bf16[320,1280]{1,0:T(8,128)(2,1)}, bf16[320,1280]{1,0:T(8,128)(2,1)}, u32[]{:S(2)}, u32[]{:S(2)}) collective-permute-start(bf16[320,1280]{1,0:T(8,128)(2,1)} %collective-permute-done.19.refs_2_), channel_id=1, source_target_pairs={{0,8},{4,12},{8,0},{12,4},{16,24},{20,28},{24,16},{28,20},{1,9},{5... | collective-permute-start | bytes 2457608 | tf_op jit(solution)/shard_map/ppermute | solution.py:28
  61.5 25.1 %collective-permute-start.26 = (bf16[320,1280]{1,0:T(8,128)(2,1)}, bf16[320,1280]{1,0:T(8,128)(2,1)}, u32[]{:S(2)}, u32[]{:S(2)}) collective-permute-start(bf16[320,1280]{1,0:T(8,128)(2,1)} %collective-permute-done.19.refs_2_), channel_id=1, source_target_pairs={{0,4},{4,0},{8,12},{12,8},{16,20},{20,16},{24,28},{28,24},{1,5},{5... | collective-permute-start | bytes 2457608 | tf_op jit(solution)/shard_map/ppermute | solution.py:28
  86.6 26.9 %collective-permute-start.28 = (bf16[320,1280]{1,0:T(8,128)(2,1)}, bf16[320,1280]{1,0:T(8,128)(2,1)}, u32[]{:S(2)}, u32[]{:S(2)}) collective-permute-start(bf16[320,1280]{1,0:T(8,128)(2,1)} %collective-permute-done.16.refs_3_), channel_id=1, source_target_pairs={{0,8},{4,12},{8,0},{12,4},{16,24},{20,28},{24,16},{28,20},{1,9},{5... | collective-permute-start | bytes 2457608 | tf_op jit(solution)/shard_map/ppermute | solution.py:28
  86.7 26.9 %collective-permute-start.29 = (bf16[320,1280]{1,0:T(8,128)(2,1)}, bf16[320,1280]{1,0:T(8,128)(2,1)}, u32[]{:S(2)}, u32[]{:S(2)}) collective-permute-start(bf16[320,1280]{1,0:T(8,128)(2,1)} %collective-permute-done.21.refs_3_), channel_id=1, source_target_pairs={{0,4},{4,0},{8,12},{12,8},{16,20},{20,16},{24,28},{28,24},{1,5},{5... | collective-permute-start | bytes 2457608 | tf_op jit(solution)/shard_map/ppermute | solution.py:28
  87.2 16.3 %collective-permute-start.25 = (bf16[640,256]{1,0:T(8,128)(2,1)S(1)}, bf16[640,256]{1,0:T(8,128)(2,1)S(1)}, u32[]{:S(2)}, u32[]{:S(2)}) collective-permute-start(bf16[640,256]{1,0:T(8,128)(2,1)S(1)} %bitcast.27), channel_id=1, source_target_pairs={{0,2},{1,3},{2,0},{3,1},{4,6},{5,7},{6,4},{7,5},{8,10},{9,11},{10,... | collective-permute-start | bytes 983048 | tf_op jit(solution)/shard_map/ppermute | solution.py:28
  89.3 3.8 %collective-permute-start.5 = (bf16[320,1280]{1,0:T(8,128)(2,1)}, bf16[320,1280]{1,0:T(8,128)(2,1)}, u32[]{:S(2)}, u32[]{:S(2)}) collective-permute-start(bf16[320,1280]{1,0:T(8,128)(2,1)} %get-tuple-element.117.refs_3_), channel_id=1, source_target_pairs={{0,1},{1,0},{2,3},{3,2},{4,5},{5,4},{6,7},{7,6},{8,9},{9,8},{10,11... | collective-permute-start | bytes 2457608 | tf_op jit(solution)/shard_map/cond/branch_1_fun/ppermute | solution.py:28
  103.3 10.5 %collective-permute-start.24 = (bf16[1280,256]{1,0:T(8,128)(2,1)S(1)}, bf16[1280,256]{1,0:T(8,128)(2,1)S(1)}, u32[]{:S(2)}, u32[]{:S(2)}) collective-permute-start(bf16[1280,256]{1,0:T(8,128)(2,1)S(1)} %get-tuple-element.235), channel_id=1, source_target_pairs={{0,1},{1,0},{2,3},{3,2},{4,5},{5,4},{6,7},{7,6},{8,9},{9,8},{10,11... | collective-permute-start | bytes 1966088 | tf_op jit(solution)/shard_map/ppermute | solution.py:28
  103.5 10.0 %collective-permute-start.27 = (bf16[640,256]{1,0:T(8,128)(2,1)S(1)}, bf16[640,256]{1,0:T(8,128)(2,1)S(1)}, u32[]{:S(2)}, u32[]{:S(2)}) collective-permute-start(bf16[640,256]{1,0:T(8,128)(2,1)S(1)} %bitcast.26), channel_id=1, source_target_pairs={{0,2},{1,3},{2,0},{3,1},{4,6},{5,7},{6,4},{7,5},{8,10},{9,11},{10,... | collective-permute-start | bytes 983048 | tf_op jit(solution)/shard_map/ppermute | solution.py:28
  113.5 11.0 %collective-permute-start.30 = (bf16[640,256]{1,0:T(8,128)(2,1)S(1)}, bf16[640,256]{1,0:T(8,128)(2,1)S(1)}, u32[]{:S(2)}, u32[]{:S(2)}) collective-permute-start(bf16[640,256]{1,0:T(8,128)(2,1)S(1)} %bitcast.25), channel_id=1, source_target_pairs={{0,2},{1,3},{2,0},{3,1},{4,6},{5,7},{6,4},{7,5},{8,10},{9,11},{10,... | collective-permute-start | bytes 983048 | tf_op jit(solution)/shard_map/ppermute | solution.py:28
  116.9 3.8 %collective-permute-start.9 = (bf16[320,1280]{1,0:T(8,128)(2,1)}, bf16[320,1280]{1,0:T(8,128)(2,1)}, u32[]{:S(2)}, u32[]{:S(2)}) collective-permute-start(bf16[320,1280]{1,0:T(8,128)(2,1)} %get-tuple-element.129.refs_2_), channel_id=1, source_target_pairs={{0,1},{1,0},{2,3},{3,2},{4,5},{5,4},{6,7},{7,6},{8,9},{9,8},{10,11... | collective-permute-start | bytes 2457608 | tf_op jit(solution)/shard_map/cond/branch_1_fun/ppermute | solution.py:28
  124.5 10.4 %collective-permute-start.31 = (bf16[640,256]{1,0:T(8,128)(2,1)}, bf16[640,256]{1,0:T(8,128)(2,1)S(1)}, u32[]{:S(2)}, u32[]{:S(2)}) collective-permute-start(bf16[640,256]{1,0:T(8,128)(2,1)} %bitcast.14), channel_id=1, source_target_pairs={{0,2},{1,3},{2,0},{3,1},{4,6},{5,7},{6,4},{7,5},{8,10},{9,11},{10,... | collective-permute-start | bytes 983048 | tf_op jit(solution)/shard_map/ppermute | solution.py:28
  (17 other events, 105.6 us)

commit v4 on v2

--- a/solution.py
+++ b/solution.py
@@ -733,12 +733,16 @@
     def first_groups(kept, others, blocks, partners):
         partners, more = with_partners(blocks, partners)
         got = send_rows(far_rows(groups[0], kept, others, blocks, partners))
-        return far_rows(groups[1], kept, others, blocks, partners), got, more
+        far = far_rows(groups[1], kept, others, blocks, partners)
+        return far, got, more, own_rows(groups[0], [tie(kept[0], far)], others, blocks, partners)
 
     def middle_group(index):
         def body(far, kept, others, blocks, partners):
-            partners, more = with_partners(blocks, partners)
-            return far_rows(groups[index], kept, others, blocks, partners), send_rows(far), more
+            known = partners
+            partners, more = with_partners({r: blocks[r] for r in groups[index]}, partners)
+            next_far = far_rows(groups[index], kept, others, blocks, partners)
+            own = own_rows(groups[index - 1], [tie(kept[0], next_far)], others, blocks, known)
+            return next_far, send_rows(far), more, own
 
         return body
 
@@ -750,29 +754,30 @@
         return {r: array[r] for r in group if r in array}
 
     arrived = []
-    far, got, more = fenced(
+    far, got, more, own = fenced(
         first_groups, kept, others, some(held, groups[0] + groups[1]), some(partners, groups[0] + groups[1])
     )
     arrived.append(got)
+    owns = [own]
     partners.update(more)
     for index in range(2, len(groups) - 1):
-        far, got, more = fenced(
-            middle_group(index), far, kept, others, some(held, groups[index]), some(partners, groups[index])
+        both = groups[index - 1] + groups[index]
+        far, got, more, own = fenced(
+            middle_group(index), far, kept, others, some(held, both), some(partners, both)
         )
         arrived.append(got)
+        owns.append(own)
         partners.update(more)
     got = send_rows(far, *[held[r] for r in groups[-1]])
     arrived.append(got)
-    ahead = own_rows(groups[0], [tie(kept[0], far)], others, held, partners)
-    blocks = some(held, groups[-1])
-    blocks[groups[-1][0]] = tie(blocks[groups[-1][0]], ahead)
-    far, more = fenced(last_group, kept, others, blocks, some(partners, groups[-1]))
+    far, more = fenced(last_group, kept, others, some(held, groups[-1]), some(partners, groups[-1]))
     partners.update(more)
     arrived.append(send_rows(far, *got))
     pieces = []
-    for group, got in zip(groups, arrived):
-        own = ahead if group == groups[0] else own_rows(group, kept, others, held, partners)
-        pieces += [own] + got
+    for index, (group, got) in enumerate(zip(groups, arrived)):
+        if index == len(owns):
+            owns.append(own_rows(group, kept, others, held, partners))
+        pieces += [owns[index]] + got
     return kernel_call(
         functools.partial(assemble_kernel, groups),
         "assemble",

time: 132 us -> 133 us (level)
  local copies, waits for them, and re-layouts: 6.36 us -> 4.72 us
    pallas_call x8, Pallas kernels: 23.7 us -> 21.2 us  [project(): kernel_call(project_kernel, name, shape((rows, count * columns, rows_dev)...]
    cond x3 -> x15, local copies, waits for them, and re-layouts: 2.49 us -> 0.83 us
  transfers between devices with their start and end apart: 31 -> 31, of which waited for: 15 -> 16; matrix products, arithmetic and copies ran while one was open for 3% -> 2% of each run, Pallas kernels for 39% -> 40%
where the time goes in v4:
time: 133 us
  Pallas kernels  55.6 us (42%)
  waiting for transfers between devices  50.3 us (38%)
  starting transfers between devices  21.7 us (16%)
  local copies, waits for them, and re-layouts  4.72 us (4%)
    ppermute x31, waiting for transfers between devices, swap(): return lax.ppermute(value, axis, pairs)  50.3 us
    ppermute x31, starting transfers between devices, swap(): return lax.ppermute(value, axis, pairs)  21.7 us
    pallas_call x8, Pallas kernels, project(): kernel_call(project_kernel, name, shape((rows, count * columns, rows_dev)...  21.2 us
    pallas_call x1, Pallas kernels, on_device(): kernel_call(functools.partial(local_kernel, near, pieces), 'local_levels'...  11 us
    pallas_call x2, Pallas kernels, step(): kernel_call(functools.partial(merge_kernel, bit, head_count), 'merge', tu...  4.1 us
    pallas_call x1, Pallas kernels, chip_sum(): kernel_call(functools.partial(factors_kernel, levels, heads_size), 'facto...  3.78 us
    pallas_call x1, Pallas kernels, on_device(): kernel_call(functools.partial(finish_kernel, half), 'finish', tuple([shap...  3.03 us
    pallas_call x1, Pallas kernels, on_device(): kernel_call(lambda me_ref, *refs: partial_state_kernel(pieces, *refs), 'p...  3.01 us
  transfers between devices with their start and end apart: 31, of which 16 were waited for; matrix products, arithmetic and copies ran while one was open for 2% of the time, Pallas kernels for 40%

profile of v4, /device:TPU:0, one launch (start us, length us, event | category | flops | bytes accessed | tf_op | source)
XLA Modules:
  0.0 132.7 jit_solution(10809290311956248297)
XLA Ops:
  0.0 4.0 %collective-permute-start.13 = (bf16[320,1280]{1,0:T(8,128)(2,1)}, bf16[320,1280]{1,0:T(8,128)(2,1)}, u32[]{:S(2)}, u32[]{:S(2)}) collective-permute-start(bf16[320,1280]{1,0:T(8,128)(2,1)} %bitcast.21), channel_id=1, source_target_pairs={{0,16},{4,20},{8,24},{12,28},{16,0},{20,4},{24,8},{28,12},{1,17},{... | collective-permute-start | bytes 2457608 | tf_op jit(solution)/shard_map/ppermute | solution.py:28
  15.9 3.0 %partial_states.1 = (f32[2,1280,128]{2,1,0:T(8,128)}, bf16[2,1280,128]{2,1,0:T(8,128)(2,1)S(1)}) custom-call(s32[1]{0:T(128)} %bitcast.9.me_ref, bf16[1280,256]{1,0:T(8,128)(2,1)S(1)} %get-tuple-element.205.refs_0_, bf16[1280,256]{1,0:T(8,128)(2,1)S(1)} %get-tuple-element.225.refs_1_, bf16[1280,128]{1,0:T(8,128)(2,1)S(1)} %get-tuple-element.216.refs_2_, ...), custom_call_target="tpu_custom_call" | custom-call | tf_op jit(solution)/shard_map/partial_states/pallas_call | solution.py:519
  18.9 3.5 %conditional.6 = (bf16[2,1280,128]{2,1,0:T(8,128)(2,1)}, bf16[1280,128]{1,0:T(8,128)(2,1)S(1)}) conditional(s32[]{:T(128)} %convert_element_type.7, () %tuple.70, (bf16[2,1280,128]{2,1,0:T(8,128)(2,1)S(1)}, f32[2,1280,128]{2,1,0:T(8,128)}) %tuple.71), branch_computations={%region_0.0_spmd, %region_1.0_spmd} | conditional | bytes 2621496 | solution.py:456
  22.4 12.3 %conditional.7 = (f32[1280,128]{1,0:T(8,128)}, bf16[1312,128]{1,0:T(8,128)(2,1)S(1)}, f32[4,20,256]{2,1,0:T(8,128)S(1)}, f32[5,4,20,256]{3,2,1,0:T(8,128)}, f32[...) conditional(s32[]{:T(128)} %convert_element_type.7, () %tuple.69, ...), branch_computations={%region_2.0_spmd, %region_3.4_spmd} | conditional | bytes 6123640 | solution.py:456
  24.7 3.8 %factors.1 = (f32[4,20,256]{2,1,0:T(8,128)S(1)}, f32[5,4,20,256]{3,2,1,0:T(8,128)}, f32[3,4,20,256]{3,2,1,0:T(8,128)}, f32[26,20,128]{2,1,0:T(8,128)}, bf16[4,2,...) custom-call(f32[20,1024]{1,0:T(8,128)S(1)} %get-tuple-element.93.dec, ...), custom_call_target="tpu_custom_call" | custom-call | tf_op jit(solution)/shard_map/cond/branch_1_fun/factors/pallas_call | solution.py:581
  29.4 3.2 %collective-permute-done.11.refs_0_ = bf16[1280,128]{1,0:T(8,128)(2,1)S(1)} collective-permute-done((bf16[1280,128]{1,0:T(8,128)(2,1)S(1)}, bf16[1280,128]{1,0:T(8,128)(2,1)S(1)}, u32[]{:S(2)}, u32[]{:S(2)}) %collective-permute-start.11) | collective-permute-done | bytes 327712 | tf_op jit(solution)/shard_map/cond/branch_1_fun/ppermute | solution.py:28
  35.9 21.9 %conditional.8 = (bf16[1312,128]{1,0:T(8,128)(2,1)}, bf16[1312,128]{1,0:T(8,128)(2,1)}, f32[32,128]{1,0:T(8,128)S(1)}, f32[32,128]{1,0:T(8,128)S(1)}, f32[32,128]{1,0:T(8,128)S(1)}, /*index=5*/bf16[1312,128]{1,0:T(8,128)(2,1)}) conditional(s32[]{:T(128)} %convert_element_type.7, () %tuple.68, (bf16[1312,128]{1,0:T(8,128)(2,1)S(1)}, s32[1]{0:T(128)}, ...), branch_computations={%region_4.5_spmd, %region_5.6_spmd} | conditional | flops 12 | bytes 2719997 | solution.py:456
  36.5 8.7 %collective-permute-done.1.got_ref = bf16[1312,128]{1,0:T(8,128)(2,1)} collective-permute-done((bf16[1312,128]{1,0:T(8,128)(2,1)S(1)}, bf16[1312,128]{1,0:T(8,128)(2,1)}, u32[]{:S(2)}, u32[]{:S(2)}) %collective-permute-start.1) | collective-permute-done | bytes 335904 | tf_op jit(solution)/shard_map/cond/branch_1_fun/ppermute | solution.py:28
  47.8 8.1 %collective-permute-done.2.got_ref = bf16[1312,128]{1,0:T(8,128)(2,1)} collective-permute-done((bf16[1312,128]{1,0:T(8,128)(2,1)}, bf16[1312,128]{1,0:T(8,128)(2,1)}, u32[]{:S(2)}, u32[]{:S(2)}) %collective-permute-start.2) | collective-permute-done | bytes 335904 | tf_op jit(solution)/shard_map/cond/branch_1_fun/ppermute | solution.py:28
  60.1 11.0 %local_levels.1.pre_ref = f32[4,1280,256]{2,1,0:T(8,128)S(1)} custom-call(s32[1]{0:T(128)} %bitcast.9.me_ref, bf16[1280,256]{1,0:T(8,128)(2,1)S(1)} %get-tuple-element.205.refs_0_, bf16[1280,256]{1,0:T(8,128)(2,1)S(1)} %collective-permute-done.20.refs_1_, bf16[1280,128]{1,0:T(8,128)(2,1)S(1)} %collective-permute-done.16.refs_2_, ...), custom_call_target="tpu_custom_call" | custom-call | tf_op jit(solution)/shard_map/local_levels/pallas_call | solution.py:661
  71.1 5.5 %collective-permute-done.22.state_ref = bf16[1312,128]{1,0:T(8,128)(2,1)S(1)} collective-permute-done((bf16[1312,128]{1,0:T(8,128)(2,1)}, bf16[1312,128]{1,0:T(8,128)(2,1)S(1)}, u32[]{:S(2)}, u32[]{:S(2)}) %collective-permute-start.22) | collective-permute-done | bytes 335904 | tf_op jit(solution)/shard_map/ppermute | solution.py:28
  76.6 3.0 %finish.1 = (bf16[1280,256]{1,0:T(8,128)(2,1)S(1)}, bf16[1280,256]{1,0:T(8,128)(2,1)S(1)}, bf16[2,1280,256]{2,1,0:T(8,128)(2,1)S(1)}) custom-call(s32[1]{0:T(128)} %bitcast.9.me_ref, f32[4,1280,256]{2,1,0:T(8,128)S(1)} %local_levels.1.pre_ref, bf16[4,256,256]{2,1,0:T(8,128)(2,1)} %get-tuple-element.232.refs_9_.reader_ref, f32[3,4,20,256]{3,2,1,0:T(8,128)S(1)} %copy-done.12, ...), custom_call_target="tpu_custom_call" | custom-call | tf_op jit(solution)/shard_map/finish/pallas_call | solution.py:677
  80.3 6.2 %collective-permute-done.26.refs_3_ = bf16[320,1280]{1,0:T(8,128)(2,1)} collective-permute-done((bf16[320,1280]{1,0:T(8,128)(2,1)}, bf16[320,1280]{1,0:T(8,128)(2,1)}, u32[]{:S(2)}, u32[]{:S(2)}) %collective-permute-start.26) | collective-permute-done | bytes 819232 | tf_op jit(solution)/shard_map/ppermute | solution.py:28
  87.9 12.6 %conditional.9 = (bf16[1,640,256]{2,1,0:T(8,128)(2,1)S(1)}, bf16[640,256]{1,0:T(8,128)(2,1)}, bf16[320,1280]{1,0:T(8,128)(2,1)S(1)}, bf16[320,1280]{1,0:T(8,128)(2,1)S(1)}, f32[640,256]{1,0:T(8,128)S(1)}) conditional(s32[]{:T(128)} %convert_element_type.7, () %tuple.67, (bf16[320,1280]{1,0:T(8,128)(2,1)}, bf16[320,1280]{1,0:T(8,128)(2,1)S(1)}, ...), branch_computations={%region_6.7_spmd, %region_7.8_spmd} | conditional | bytes 20971792 | solution.py:456
  91.5 2.7 %project_far.4 = bf16[1,640,256]{2,1,0:T(8,128)(2,1)S(1)} custom-call(bf16[1280,256]{1,0:T(8,128)(2,1)S(1)} %get-tuple-element.123.refs_0_, bf16[2,1280,256]{2,1,0:T(8,128)(2,1)S(1)} %get-tuple-element.124.refs_1_, bf16[320,1280]{1,0:T(8,128)(2,1)} %get-tuple-element.125.refs_2_, bf16[320,1280]{1,0:T(8,128)(2,1)S(1)} %get-tuple-element.126.refs_3_, ...), custom_call_target="tpu_custom_call" | custom-call | tf_op jit(solution)/shard_map/cond/branch_1_fun/project_far/pallas_call | solution.py:708
  96.6 3.9 %collective-permute-done.5 = bf16[640,256]{1,0:T(8,128)(2,1)} collective-permute-done((bf16[640,256]{1,0:T(8,128)(2,1)S(1)}, bf16[640,256]{1,0:T(8,128)(2,1)}, u32[]{:S(2)}, u32[]{:S(2)}) %collective-permute-start.5) | collective-permute-done | bytes 327712 | tf_op jit(solution)/shard_map/cond/branch_1_fun/ppermute | solution.py:28
  101.4 10.2 %conditional.10 = (bf16[1,640,256]{2,1,0:T(8,128)(2,1)S(1)}, bf16[640,256]{1,0:T(8,128)(2,1)}, bf16[320,1280]{1,0:T(8,128)(2,1)}, bf16[320,1280]{1,0:T(8,128)(2,1)}, f32[640,256]{1,0:T(8,128)S(1)}) conditional(s32[]{:T(128)} %convert_element_type.7, () %tuple.82, (bf16[320,1280]{1,0:T(8,128)(2,1)}, bf16[320,1280]{1,0:T(8,128)(2,1)}, ...), branch_computations={%region_8.9_spmd, %region_9.10_spmd} | conditional | bytes 17694964 | solution.py:456
  105.1 2.7 %project_far.6 = bf16[1,640,256]{2,1,0:T(8,128)(2,1)S(1)} custom-call(bf16[1280,256]{1,0:T(8,128)(2,1)S(1)} %get-tuple-element.133.refs_0_, bf16[2,1280,256]{2,1,0:T(8,128)(2,1)S(1)} %get-tuple-element.134.refs_1_, bf16[320,1280]{1,0:T(8,128)(2,1)} %get-tuple-element.135.refs_2_, bf16[320,1280]{1,0:T(8,128)(2,1)} %get-tuple-element.136.refs_3_, ...), custom_call_target="tpu_custom_call" | custom-call | tf_op jit(solution)/shard_map/cond/branch_1_fun/project_far/pallas_call | solution.py:708
  112.5 7.5 %conditional.11 = (bf16[1,640,256]{2,1,0:T(8,128)(2,1)}, bf16[320,1280]{1,0:T(8,128)(2,1)}, bf16[320,1280]{1,0:T(8,128)(2,1)}) conditional(s32[]{:T(128)} %convert_element_type.7, () %tuple.87, (bf16[320,1280]{1,0:T(8,128)(2,1)}, bf16[320,1280]{1,0:T(8,128)(2,1)}, bf16[1280,256]{1,0:T(8,128)(2,1)S(1)}, bf16[2,1280,256]{2,1,0:T(8,128)(2,1)S(1)}) %tuple.88), branch_computations={%region_10.11_spmd, %region_11.12_spmd} | conditional | bytes 6553704 | solution.py:456
  116.3 3.6 %project_far.7 = bf16[1,640,256]{2,1,0:T(8,128)(2,1)} custom-call(bf16[1280,256]{1,0:T(8,128)(2,1)S(1)} %get-tuple-element.144.refs_0_, bf16[2,1280,256]{2,1,0:T(8,128)(2,1)S(1)} %get-tuple-element.145.refs_1_, bf16[320,1280]{1,0:T(8,128)(2,1)} %get-tuple-element.146.refs_2_, bf16[320,1280]{1,0:T(8,128)(2,1)} %get-tuple-element.147.refs_3_, ...), custom_call_target="tpu_custom_call" | custom-call | tf_op jit(solution)/shard_map/cond/branch_1_fun/project_far/pallas_call | solution.py:708
  121.3 3.0 %project_own.7 = f32[1,640,256]{2,1,0:T(8,128)S(1)} custom-call(bf16[1280,256]{1,0:T(8,128)(2,1)S(1)} %get-tuple-element.244.refs_0_, bf16[2,1280,256]{2,1,0:T(8,128)(2,1)S(1)} %collective-permute-done.23.refs_1_, bf16[320,1280]{1,0:T(8,128)(2,1)} %collective-permute-done.27.refs_2_, bf16[320,1280]{1,0:T(8,128)(2,1)} %collective-permute-done.28.refs_3_, ...), custom_call_target="tpu_custom_call" | custom-call | tf_op jit(solution)/shard_map/project_own/pallas_call | solution.py:708
  124.3 2.5 %project_own.6 = f32[1,640,256]{2,1,0:T(8,128)S(1)} custom-call(bf16[1280,256]{1,0:T(8,128)(2,1)S(1)} %get-tuple-element.244.refs_0_, bf16[2,1280,256]{2,1,0:T(8,128)(2,1)S(1)} %collective-permute-done.23.refs_1_, bf16[320,1280]{1,0:T(8,128)(2,1)} %collective-permute-done.18.refs_2_, bf16[320,1280]{1,0:T(8,128)(2,1)} %collective-permute-done.26.refs_3_, ...), custom_call_target="tpu_custom_call" | custom-call | tf_op jit(solution)/shard_map/project_own/pallas_call | solution.py:708
  126.8 3.1 %collective-permute-done.30.refs_7_ = bf16[640,256]{1,0:T(8,128)(2,1)S(1)} collective-permute-done((bf16[640,256]{1,0:T(8,128)(2,1)}, bf16[640,256]{1,0:T(8,128)(2,1)S(1)}, u32[]{:S(2)}, u32[]{:S(2)}) %collective-permute-start.30) | collective-permute-done | bytes 327712 | tf_op jit(solution)/shard_map/ppermute | solution.py:28
  130.0 2.8 %assemble.1 = bf16[256,2560]{1,0:T(8,128)(2,1)} custom-call(s32[1]{0:T(128)} %bitcast.7.place_ref, f32[640,256]{1,0:T(8,128)S(1)} %copy-done.14, bf16[640,256]{1,0:T(8,128)(2,1)} %get-tuple-element.246.refs_1_, f32[640,256]{1,0:T(8,128)S(1)} %copy-done.16, bf16[640,256]{1,0:T(8,128)(2,1)} %get-tuple-element.251.refs_3_, f32[640,256]{1,0:T(8,128)S(1)} %bitcast.18, ...), custom_call_target="tpu_custom_call" | custom-call | tf_op jit(solution)/shard_map/assemble/pallas_call | solution.py:781
  (118 shorter events, 51.5 us)
Async XLA Ops:
  0.0 57.9 %collective-permute-start.13 = (bf16[320,1280]{1,0:T(8,128)(2,1)}, bf16[320,1280]{1,0:T(8,128)(2,1)}, u32[]{:S(2)}, u32[]{:S(2)}) collective-permute-start(bf16[320,1280]{1,0:T(8,128)(2,1)} %bitcast.21), channel_id=1, source_target_pairs={{0,16},{4,20},{8,24},{12,28},{16,0},{20,4},{24,8},{28,12},{1,17},{... | collective-permute-start | bytes 2457608 | tf_op jit(solution)/shard_map/ppermute | solution.py:28
  4.0 53.8 %collective-permute-start.18 = (bf16[320,1280]{1,0:T(8,128)(2,1)}, bf16[320,1280]{1,0:T(8,128)(2,1)}, u32[]{:S(2)}, u32[]{:S(2)}) collective-permute-start(bf16[320,1280]{1,0:T(8,128)(2,1)} %bitcast.22), channel_id=1, source_target_pairs={{0,8},{4,12},{8,0},{12,4},{16,24},{20,28},{24,16},{28,20},{1,9},{5... | collective-permute-start | bytes 2457608 | tf_op jit(solution)/shard_map/ppermute | solution.py:28
  5.6 52.3 %collective-permute-start.17 = (bf16[320,1280]{1,0:T(8,128)(2,1)}, bf16[320,1280]{1,0:T(8,128)(2,1)}, u32[]{:S(2)}, u32[]{:S(2)}) collective-permute-start(bf16[320,1280]{1,0:T(8,128)(2,1)} %bitcast.23), channel_id=1, source_target_pairs={{0,4},{4,0},{8,12},{12,8},{16,20},{20,16},{24,28},{28,24},{1,5},{5... | collective-permute-start | bytes 2457608 | tf_op jit(solution)/shard_map/ppermute | solution.py:28
  9.0 4.8 %collective-permute-start.14 = (f32[2,20,256]{2,1,0:T(8,128)S(1)}, f32[2,20,256]{2,1,0:T(8,128)S(1)}, u32[]{:S(2)}, u32[]{:S(2)}) collective-permute-start(f32[2,20,256]{2,1,0:T(8,128)S(1)} %get-tuple-element.212), channel_id=1, source_target_pairs={{0,2},{1,3},{2,0},{3,1},{4,6},{5,7},{6,4},{7,5},{8,10},{9,11},{10,... | collective-permute-start | bytes 122888 | tf_op jit(solution)/shard_map/ppermute | solution.py:28
  13.8 8.5 %collective-permute-start.16 = (bf16[1280,128]{1,0:T(8,128)(2,1)S(1)}, bf16[1280,128]{1,0:T(8,128)(2,1)S(1)}, u32[]{:S(2)}, u32[]{:S(2)}) collective-permute-start(bf16[1280,128]{1,0:T(8,128)(2,1)S(1)} %get-tuple-element.216.refs_2_), channel_id=1, source_target_pairs={{0,2},{1,3},{2,0},{3,1},{4,6},{5,7},{6,4},{7,5},{8,10},{9,11},{10,... | collective-permute-start | bytes 983048 | tf_op jit(solution)/shard_map/ppermute | solution.py:28
  22.4 6.1 %collective-permute-start.12 = (bf16[1280,256]{1,0:T(8,128)(2,1)}, bf16[1280,256]{1,0:T(8,128)(2,1)S(1)}, u32[]{:S(2)}, u32[]{:S(2)}) collective-permute-start(bf16[1280,256]{1,0:T(8,128)(2,1)} %get-tuple-element.100), channel_id=1, source_target_pairs={{0,1},{1,0},{2,3},{3,2},{4,5},{5,4},{6,7},{7,6},{8,9},{9,8},{10,11... | collective-permute-start | bytes 1966088 | tf_op jit(solution)/shard_map/cond/branch_1_fun/ppermute | solution.py:28
  22.6 10.0 %collective-permute-start.11 = (bf16[1280,128]{1,0:T(8,128)(2,1)S(1)}, bf16[1280,128]{1,0:T(8,128)(2,1)S(1)}, u32[]{:S(2)}, u32[]{:S(2)}) collective-permute-start(bf16[1280,128]{1,0:T(8,128)(2,1)S(1)} %get-tuple-element.92), channel_id=1, source_target_pairs={{0,2},{1,3},{2,0},{3,1},{4,6},{5,7},{6,4},{7,5},{8,10},{9,11},{10,... | collective-permute-start | bytes 983048 | tf_op jit(solution)/shard_map/cond/branch_1_fun/ppermute | solution.py:28
  34.7 24.9 %collective-permute-start.21 = (bf16[1280,384]{1,0:T(8,128)(2,1)}, bf16[1280,384]{1,0:T(8,128)(2,1)S(1)}, u32[]{:S(2)}, u32[]{:S(2)}) collective-permute-start(bf16[1280,384]{1,0:T(8,128)(2,1)} %get-tuple-element.226), channel_id=1, source_target_pairs={{0,2},{1,3},{2,0},{3,1},{4,6},{5,7},{6,4},{7,5},{8,10},{9,11},{10,... | collective-permute-start | bytes 2949128 | tf_op jit(solution)/shard_map/ppermute | solution.py:28
  35.9 9.3 %collective-permute-start.1 = (bf16[1312,128]{1,0:T(8,128)(2,1)S(1)}, bf16[1312,128]{1,0:T(8,128)(2,1)}, u32[]{:S(2)}, u32[]{:S(2)}) collective-permute-start(bf16[1312,128]{1,0:T(8,128)(2,1)S(1)} %get-tuple-element.111), channel_id=1, source_target_pairs={{0,4},{4,0},{8,12},{12,8},{16,20},{20,16},{24,28},{28,24},{1,5},{5... | collective-permute-start | bytes 1007624 | tf_op jit(solution)/shard_map/cond/branch_1_fun/ppermute | solution.py:28
  47.4 8.6 %collective-permute-start.2 = (bf16[1312,128]{1,0:T(8,128)(2,1)}, bf16[1312,128]{1,0:T(8,128)(2,1)}, u32[]{:S(2)}, u32[]{:S(2)}) collective-permute-start(bf16[1312,128]{1,0:T(8,128)(2,1)} %get-tuple-element.115), channel_id=1, source_target_pairs={{0,8},{4,12},{8,0},{12,4},{16,24},{20,28},{24,16},{28,20},{1,9},{5... | collective-permute-start | bytes 1007624 | tf_op jit(solution)/shard_map/cond/branch_1_fun/ppermute | solution.py:28
  58.0 18.6 %collective-permute-start.22 = (bf16[1312,128]{1,0:T(8,128)(2,1)}, bf16[1312,128]{1,0:T(8,128)(2,1)S(1)}, u32[]{:S(2)}, u32[]{:S(2)}) collective-permute-start(bf16[1312,128]{1,0:T(8,128)(2,1)} %get-tuple-element.223), channel_id=1, source_target_pairs={{0,16},{4,20},{8,24},{12,28},{16,0},{20,4},{24,8},{28,12},{1,17},{... | collective-permute-start | bytes 1007624 | tf_op jit(solution)/shard_map/ppermute | solution.py:28
  58.4 21.9 %collective-permute-start.19 = (bf16[320,1280]{1,0:T(8,128)(2,1)}, bf16[320,1280]{1,0:T(8,128)(2,1)S(1)}, u32[]{:S(2)}, u32[]{:S(2)}) collective-permute-start(bf16[320,1280]{1,0:T(8,128)(2,1)} %collective-permute-done.13), channel_id=1, source_target_pairs={{0,4},{4,0},{8,12},{12,8},{16,20},{20,16},{24,28},{28,24},{1,5},{5... | collective-permute-start | bytes 2457608 | tf_op jit(solution)/shard_map/ppermute | solution.py:28
  58.9 27.5 %collective-permute-start.26 = (bf16[320,1280]{1,0:T(8,128)(2,1)}, bf16[320,1280]{1,0:T(8,128)(2,1)}, u32[]{:S(2)}, u32[]{:S(2)}) collective-permute-start(bf16[320,1280]{1,0:T(8,128)(2,1)} %collective-permute-done.13), channel_id=1, source_target_pairs={{0,8},{4,12},{8,0},{12,4},{16,24},{20,28},{24,16},{28,20},{1,9},{5... | collective-permute-start | bytes 2457608 | tf_op jit(solution)/shard_map/ppermute | solution.py:28
  79.6 8.3 %collective-permute-start.23 = (bf16[2,1280,256]{2,1,0:T(8,128)(2,1)S(1)}, bf16[2,1280,256]{2,1,0:T(8,128)(2,1)S(1)}, u32[]{:S(2)}, u32[]{:S(2)}) collective-permute-start(bf16[2,1280,256]{2,1,0:T(8,128)(2,1)S(1)} %get-tuple-element.241), channel_id=1, source_target_pairs={{0,1},{1,0},{2,3},{3,2},{4,5},{5,4},{6,7},{7,6},{8,9},{9,8},{10,11... | collective-permute-start | bytes 3932168 | tf_op jit(solution)/shard_map/ppermute | solution.py:28
  79.7 8.2 %collective-permute-start.25 = (bf16[320,1280]{1,0:T(8,128)(2,1)}, bf16[320,1280]{1,0:T(8,128)(2,1)S(1)}, u32[]{:S(2)}, u32[]{:S(2)}) collective-permute-start(bf16[320,1280]{1,0:T(8,128)(2,1)} %collective-permute-done.17), channel_id=1, source_target_pairs={{0,1},{1,0},{2,3},{3,2},{4,5},{5,4},{6,7},{7,6},{8,9},{9,8},{10,11... | collective-permute-start | bytes 2457608 | tf_op jit(solution)/shard_map/ppermute | solution.py:28
  80.2 7.7 %collective-permute-start.24 = (bf16[320,1280]{1,0:T(8,128)(2,1)S(1)}, bf16[320,1280]{1,0:T(8,128)(2,1)S(1)}, u32[]{:S(2)}, u32[]{:S(2)}) collective-permute-start(bf16[320,1280]{1,0:T(8,128)(2,1)S(1)} %bitcast.24), channel_id=1, source_target_pairs={{0,1},{1,0},{2,3},{3,2},{4,5},{5,4},{6,7},{7,6},{8,9},{9,8},{10,11... | collective-permute-start | bytes 2457608 | tf_op jit(solution)/shard_map/ppermute | solution.py:28
  86.5 25.2 %collective-permute-start.28 = (bf16[320,1280]{1,0:T(8,128)(2,1)}, bf16[320,1280]{1,0:T(8,128)(2,1)}, u32[]{:S(2)}, u32[]{:S(2)}) collective-permute-start(bf16[320,1280]{1,0:T(8,128)(2,1)} %collective-permute-done.26.refs_3_), channel_id=1, source_target_pairs={{0,4},{4,0},{8,12},{12,8},{16,20},{20,16},{24,28},{28,24},{1,5},{5... | collective-permute-start | bytes 2457608 | tf_op jit(solution)/shard_map/ppermute | solution.py:28
  87.9 23.7 %collective-permute-start.27 = (bf16[320,1280]{1,0:T(8,128)(2,1)}, bf16[320,1280]{1,0:T(8,128)(2,1)}, u32[]{:S(2)}, u32[]{:S(2)}) collective-permute-start(bf16[320,1280]{1,0:T(8,128)(2,1)} %collective-permute-done.17), channel_id=1, source_target_pairs={{0,8},{4,12},{8,0},{12,4},{16,24},{20,28},{24,16},{28,20},{1,9},{5... | collective-permute-start | bytes 2457608 | tf_op jit(solution)/shard_map/ppermute | solution.py:28
  90.7 9.9 %collective-permute-start.5 = (bf16[640,256]{1,0:T(8,128)(2,1)S(1)}, bf16[640,256]{1,0:T(8,128)(2,1)}, u32[]{:S(2)}, u32[]{:S(2)}) collective-permute-start(bf16[640,256]{1,0:T(8,128)(2,1)S(1)} %bitcast.20), channel_id=1, source_target_pairs={{0,2},{1,3},{2,0},{3,1},{4,6},{5,7},{6,4},{7,5},{8,10},{9,11},{10,... | collective-permute-start | bytes 983048 | tf_op jit(solution)/shard_map/cond/branch_1_fun/ppermute | solution.py:28
  101.4 3.7 %collective-permute-start.7 = (bf16[320,1280]{1,0:T(8,128)(2,1)}, bf16[320,1280]{1,0:T(8,128)(2,1)S(1)}, u32[]{:S(2)}, u32[]{:S(2)}) collective-permute-start(bf16[320,1280]{1,0:T(8,128)(2,1)} %get-tuple-element.136.refs_3_), channel_id=1, source_target_pairs={{0,1},{1,0},{2,3},{3,2},{4,5},{5,4},{6,7},{7,6},{8,9},{9,8},{10,11... | collective-permute-start | bytes 2457608 | tf_op jit(solution)/shard_map/cond/branch_1_fun/ppermute | solution.py:28
  101.9 9.7 %collective-permute-start.8 = (bf16[640,256]{1,0:T(8,128)(2,1)S(1)}, bf16[640,256]{1,0:T(8,128)(2,1)}, u32[]{:S(2)}, u32[]{:S(2)}) collective-permute-start(bf16[640,256]{1,0:T(8,128)(2,1)S(1)} %bitcast.31), channel_id=1, source_target_pairs={{0,2},{1,3},{2,0},{3,1},{4,6},{5,7},{6,4},{7,5},{8,10},{9,11},{10,... | collective-permute-start | bytes 983048 | tf_op jit(solution)/shard_map/cond/branch_1_fun/ppermute | solution.py:28
  111.7 8.8 %collective-permute-start.29 = (bf16[640,256]{1,0:T(8,128)(2,1)S(1)}, bf16[640,256]{1,0:T(8,128)(2,1)S(1)}, u32[]{:S(2)}, u32[]{:S(2)}) collective-permute-start(bf16[640,256]{1,0:T(8,128)(2,1)S(1)} %bitcast.32), channel_id=1, source_target_pairs={{0,2},{1,3},{2,0},{3,1},{4,6},{5,7},{6,4},{7,5},{8,10},{9,11},{10,... | collective-permute-start | bytes 983048 | tf_op jit(solution)/shard_map/ppermute | solution.py:28
  112.5 3.8 %collective-permute-start.9 = (bf16[320,1280]{1,0:T(8,128)(2,1)}, bf16[320,1280]{1,0:T(8,128)(2,1)}, u32[]{:S(2)}, u32[]{:S(2)}) collective-permute-start(bf16[320,1280]{1,0:T(8,128)(2,1)} %get-tuple-element.146.refs_2_), channel_id=1, source_target_pairs={{0,1},{1,0},{2,3},{3,2},{4,5},{5,4},{6,7},{7,6},{8,9},{9,8},{10,11... | collective-permute-start | bytes 2457608 | tf_op jit(solution)/shard_map/cond/branch_1_fun/ppermute | solution.py:28
  120.5 9.5 %collective-permute-start.30 = (bf16[640,256]{1,0:T(8,128)(2,1)}, bf16[640,256]{1,0:T(8,128)(2,1)S(1)}, u32[]{:S(2)}, u32[]{:S(2)}) collective-permute-start(bf16[640,256]{1,0:T(8,128)(2,1)} %bitcast.14), channel_id=1, source_target_pairs={{0,2},{1,3},{2,0},{3,1},{4,6},{5,7},{6,4},{7,5},{8,10},{9,11},{10,... | collective-permute-start | bytes 983048 | tf_op jit(solution)/shard_map/ppermute | solution.py:28
  (30 other events, 155.5 us)

commit v5 on v4

--- a/solution.py
+++ b/solution.py
@@ -12,7 +12,7 @@
 LANES = 128
 F32 = jnp.float32
 BF16 = jnp.bfloat16
-VMEM_LIMIT = 40 * 1024 * 1024
+MIB = 1024 * 1024
 
 
 def dot(a, b):
@@ -434,12 +434,12 @@
     padded = -(-head_count // 8) * 8
     half = heads_size // 2
     near = ctx_bits - 1
-    params = pltpu.CompilerParams(vmem_limit_bytes=VMEM_LIMIT)
     cheap = pl.CostEstimate(flops=0, bytes_accessed=0, transcendentals=0)
     smem = pl.BlockSpec(memory_space=pltpu.SMEM)
     vmem = pl.BlockSpec(memory_space=pltpu.VMEM)
 
-    def kernel_call(body, name, out_shape, **kwargs):
+    def kernel_call(body, name, out_shape, mib=16, **kwargs):
+        params = pltpu.CompilerParams(vmem_limit_bytes=mib * MIB)
         return pl.pallas_call(
             body, out_shape=out_shape, compiler_params=params, cost_estimate=cheap, name=name, **kwargs
         )
@@ -662,6 +662,7 @@
         functools.partial(local_kernel, near, pieces),
         "local_levels",
         shape((heads_size, features, rows_dev), F32),
+        40,
         in_specs=[smem] + [vmem] * (len(arrays) + 9 + 2 * near),
         scratch_shapes=[
             pltpu.VMEM((features, rows_dev), BF16),
@@ -678,6 +679,7 @@
         functools.partial(finish_kernel, half),
         "finish",
         tuple([shape((features, rows_dev))] * half + [shape((half, features, rows_dev))]),
+        28,
         grid=(1,),
         in_specs=[
             smem,

time: 133 us -> 133 us (level)
  no operation moved by 1% of the time
where the time goes in v5:
time: 133 us; the launch traced here: 132 us
  Pallas kernels  54.9 us (41%)
  waiting for transfers between devices  50.3 us (38%)
  starting transfers between devices  21.6 us (16%)
  local copies, waits for them, and re-layouts  4.74 us (4%)
    ppermute x31, waiting for transfers between devices, swap(): return lax.ppermute(value, axis, pairs)  50.3 us
    ppermute x31, starting transfers between devices, swap(): return lax.ppermute(value, axis, pairs)  21.6 us
    pallas_call x8, Pallas kernels, project(): kernel_call(project_kernel, name, shape((rows, count * columns, rows_dev)...  20.4 us
    pallas_call x1, Pallas kernels, on_device(): kernel_call(functools.partial(local_kernel, near, pieces), 'local_levels'...  11 us
    pallas_call x2, Pallas kernels, step(): kernel_call(functools.partial(merge_kernel, bit, head_count), 'merge', tu...  4.1 us
    pallas_call x1, Pallas kernels, chip_sum(): kernel_call(functools.partial(factors_kernel, levels, heads_size), 'facto...  3.73 us
    pallas_call x1, Pallas kernels, on_device(): kernel_call(functools.partial(finish_kernel, half), 'finish', tuple([shap...  3.03 us
    pallas_call x1, Pallas kernels, on_device(): kernel_call(lambda me_ref, *refs: partial_state_kernel(pieces, *refs), 'p...  3.01 us
  transfers between devices with their start and end apart: 31, of which 16 were waited for; matrix products, arithmetic and copies ran while one was open for 2% of the time, Pallas kernels for 40%

profile of v5, /device:TPU:0, one launch (start us, length us, event | category | flops | bytes accessed | tf_op | source)
XLA Modules:
  0.0 131.9 jit_solution(9483276450675290153)
XLA Ops:
  0.0 4.0 %collective-permute-start.13 = (bf16[320,1280]{1,0:T(8,128)(2,1)}, bf16[320,1280]{1,0:T(8,128)(2,1)}, u32[]{:S(2)}, u32[]{:S(2)}) collective-permute-start(bf16[320,1280]{1,0:T(8,128)(2,1)} %bitcast.21), channel_id=1, source_target_pairs={{0,16},{4,20},{8,24},{12,28},{16,0},{20,4},{24,8},{28,12},{1,17},{... | collective-permute-start | bytes 2457608 | tf_op jit(solution)/shard_map/ppermute | solution.py:28
  15.9 3.0 %partial_states.1 = (f32[2,1280,128]{2,1,0:T(8,128)}, bf16[2,1280,128]{2,1,0:T(8,128)(2,1)S(1)}) custom-call(s32[1]{0:T(128)} %bitcast.9.me_ref, bf16[1280,256]{1,0:T(8,128)(2,1)S(1)} %get-tuple-element.205.refs_0_, bf16[1280,256]{1,0:T(8,128)(2,1)S(1)} %get-tuple-element.225.refs_1_, bf16[1280,128]{1,0:T(8,128)(2,1)S(1)} %get-tuple-element.216.refs_2_, ...), custom_call_target="tpu_custom_call" | custom-call | tf_op jit(solution)/shard_map/partial_states/pallas_call | solution.py:519
  18.9 3.5 %conditional.6 = (bf16[2,1280,128]{2,1,0:T(8,128)(2,1)}, bf16[1280,128]{1,0:T(8,128)(2,1)S(1)}) conditional(s32[]{:T(128)} %convert_element_type.7, () %tuple.70, (bf16[2,1280,128]{2,1,0:T(8,128)(2,1)S(1)}, f32[2,1280,128]{2,1,0:T(8,128)}) %tuple.71), branch_computations={%region_0.0_spmd, %region_1.0_spmd} | conditional | bytes 2621496 | solution.py:456
  22.4 12.4 %conditional.7 = (f32[1280,128]{1,0:T(8,128)}, bf16[1312,128]{1,0:T(8,128)(2,1)S(1)}, f32[4,20,256]{2,1,0:T(8,128)S(1)}, f32[5,4,20,256]{3,2,1,0:T(8,128)}, f32[...) conditional(s32[]{:T(128)} %convert_element_type.7, () %tuple.69, ...), branch_computations={%region_2.0_spmd, %region_3.4_spmd} | conditional | bytes 6123640 | solution.py:456
  24.7 3.7 %factors.1 = (f32[4,20,256]{2,1,0:T(8,128)S(1)}, f32[5,4,20,256]{3,2,1,0:T(8,128)}, f32[3,4,20,256]{3,2,1,0:T(8,128)}, f32[26,20,128]{2,1,0:T(8,128)}, bf16[4,2,...) custom-call(f32[20,1024]{1,0:T(8,128)S(1)} %get-tuple-element.93.dec, ...), custom_call_target="tpu_custom_call" | custom-call | tf_op jit(solution)/shard_map/cond/branch_1_fun/factors/pallas_call | solution.py:581
  29.4 3.2 %collective-permute-done.11.refs_0_ = bf16[1280,128]{1,0:T(8,128)(2,1)S(1)} collective-permute-done((bf16[1280,128]{1,0:T(8,128)(2,1)S(1)}, bf16[1280,128]{1,0:T(8,128)(2,1)S(1)}, u32[]{:S(2)}, u32[]{:S(2)}) %collective-permute-start.11) | collective-permute-done | bytes 327712 | tf_op jit(solution)/shard_map/cond/branch_1_fun/ppermute | solution.py:28
  36.0 21.9 %conditional.8 = (bf16[1312,128]{1,0:T(8,128)(2,1)}, bf16[1312,128]{1,0:T(8,128)(2,1)}, f32[32,128]{1,0:T(8,128)S(1)}, f32[32,128]{1,0:T(8,128)S(1)}, f32[32,128]{1,0:T(8,128)S(1)}, /*index=5*/bf16[1312,128]{1,0:T(8,128)(2,1)}) conditional(s32[]{:T(128)} %convert_element_type.7, () %tuple.68, (bf16[1312,128]{1,0:T(8,128)(2,1)S(1)}, s32[1]{0:T(128)}, ...), branch_computations={%region_4.5_spmd, %region_5.6_spmd} | conditional | flops 12 | bytes 2719997 | solution.py:456
  36.5 8.7 %collective-permute-done.1.got_ref = bf16[1312,128]{1,0:T(8,128)(2,1)} collective-permute-done((bf16[1312,128]{1,0:T(8,128)(2,1)S(1)}, bf16[1312,128]{1,0:T(8,128)(2,1)}, u32[]{:S(2)}, u32[]{:S(2)}) %collective-permute-start.1) | collective-permute-done | bytes 335904 | tf_op jit(solution)/shard_map/cond/branch_1_fun/ppermute | solution.py:28
  47.9 8.1 %collective-permute-done.2.got_ref = bf16[1312,128]{1,0:T(8,128)(2,1)} collective-permute-done((bf16[1312,128]{1,0:T(8,128)(2,1)}, bf16[1312,128]{1,0:T(8,128)(2,1)}, u32[]{:S(2)}, u32[]{:S(2)}) %collective-permute-start.2) | collective-permute-done | bytes 335904 | tf_op jit(solution)/shard_map/cond/branch_1_fun/ppermute | solution.py:28
  60.2 11.0 %local_levels.1.pre_ref = f32[4,1280,256]{2,1,0:T(8,128)S(1)} custom-call(s32[1]{0:T(128)} %bitcast.9.me_ref, bf16[1280,256]{1,0:T(8,128)(2,1)S(1)} %get-tuple-element.205.refs_0_, bf16[1280,256]{1,0:T(8,128)(2,1)S(1)} %collective-permute-done.20.refs_1_, bf16[1280,128]{1,0:T(8,128)(2,1)S(1)} %collective-permute-done.16.refs_2_, ...), custom_call_target="tpu_custom_call" | custom-call | tf_op jit(solution)/shard_map/local_levels/pallas_call | solution.py:661
  71.2 5.5 %collective-permute-done.22.state_ref = bf16[1312,128]{1,0:T(8,128)(2,1)S(1)} collective-permute-done((bf16[1312,128]{1,0:T(8,128)(2,1)}, bf16[1312,128]{1,0:T(8,128)(2,1)S(1)}, u32[]{:S(2)}, u32[]{:S(2)}) %collective-permute-start.22) | collective-permute-done | bytes 335904 | tf_op jit(solution)/shard_map/ppermute | solution.py:28
  76.6 3.0 %finish.1 = (bf16[1280,256]{1,0:T(8,128)(2,1)S(1)}, bf16[1280,256]{1,0:T(8,128)(2,1)S(1)}, bf16[2,1280,256]{2,1,0:T(8,128)(2,1)S(1)}) custom-call(s32[1]{0:T(128)} %bitcast.9.me_ref, f32[4,1280,256]{2,1,0:T(8,128)S(1)} %local_levels.1.pre_ref, bf16[4,256,256]{2,1,0:T(8,128)(2,1)} %get-tuple-element.232.refs_9_.reader_ref, f32[3,4,20,256]{3,2,1,0:T(8,128)S(1)} %copy-done.12, ...), custom_call_target="tpu_custom_call" | custom-call | tf_op jit(solution)/shard_map/finish/pallas_call | solution.py:678
  80.3 6.2 %collective-permute-done.26.refs_3_ = bf16[320,1280]{1,0:T(8,128)(2,1)} collective-permute-done((bf16[320,1280]{1,0:T(8,128)(2,1)}, bf16[320,1280]{1,0:T(8,128)(2,1)}, u32[]{:S(2)}, u32[]{:S(2)}) %collective-permute-start.26) | collective-permute-done | bytes 819232 | tf_op jit(solution)/shard_map/ppermute | solution.py:28
  88.0 12.6 %conditional.9 = (bf16[1,640,256]{2,1,0:T(8,128)(2,1)S(1)}, bf16[640,256]{1,0:T(8,128)(2,1)}, bf16[320,1280]{1,0:T(8,128)(2,1)S(1)}, bf16[320,1280]{1,0:T(8,128)(2,1)S(1)}, f32[640,256]{1,0:T(8,128)S(1)}) conditional(s32[]{:T(128)} %convert_element_type.7, () %tuple.67, (bf16[320,1280]{1,0:T(8,128)(2,1)}, bf16[320,1280]{1,0:T(8,128)(2,1)S(1)}, ...), branch_computations={%region_6.7_spmd, %region_7.8_spmd} | conditional | bytes 20971792 | solution.py:456
  91.6 2.7 %project_far.4 = bf16[1,640,256]{2,1,0:T(8,128)(2,1)S(1)} custom-call(bf16[1280,256]{1,0:T(8,128)(2,1)S(1)} %get-tuple-element.123.refs_0_, bf16[2,1280,256]{2,1,0:T(8,128)(2,1)S(1)} %get-tuple-element.124.refs_1_, bf16[320,1280]{1,0:T(8,128)(2,1)} %get-tuple-element.125.refs_2_, bf16[320,1280]{1,0:T(8,128)(2,1)S(1)} %get-tuple-element.126.refs_3_, ...), custom_call_target="tpu_custom_call" | custom-call | tf_op jit(solution)/shard_map/cond/branch_1_fun/project_far/pallas_call | solution.py:710
  94.4 2.3 %project_own.4 = f32[1,640,256]{2,1,0:T(8,128)S(1)} custom-call(bf16[1280,256]{1,0:T(8,128)(2,1)S(1)} %get-tuple-element.132.refs_0_, bf16[2,1280,256]{2,1,0:T(8,128)(2,1)S(1)} %get-tuple-element.124.refs_1_, bf16[320,1280]{1,0:T(8,128)(2,1)S(1)} %get-tuple-element.127.refs_2_, bf16[320,1280]{1,0:T(8,128)(2,1)} %get-tuple-element.128.refs_3_, ...), custom_call_target="tpu_custom_call" | custom-call | tf_op jit(solution)/shard_map/cond/branch_1_fun/project_own/pallas_call | solution.py:710
  96.7 3.9 %collective-permute-done.5 = bf16[640,256]{1,0:T(8,128)(2,1)} collective-permute-done((bf16[640,256]{1,0:T(8,128)(2,1)S(1)}, bf16[640,256]{1,0:T(8,128)(2,1)}, u32[]{:S(2)}, u32[]{:S(2)}) %collective-permute-start.5) | collective-permute-done | bytes 327712 | tf_op jit(solution)/shard_map/cond/branch_1_fun/ppermute | solution.py:28
  101.5 10.2 %conditional.10 = (bf16[1,640,256]{2,1,0:T(8,128)(2,1)S(1)}, bf16[640,256]{1,0:T(8,128)(2,1)}, bf16[320,1280]{1,0:T(8,128)(2,1)}, bf16[320,1280]{1,0:T(8,128)(2,1)}, f32[640,256]{1,0:T(8,128)S(1)}) conditional(s32[]{:T(128)} %convert_element_type.7, () %tuple.82, (bf16[320,1280]{1,0:T(8,128)(2,1)}, bf16[320,1280]{1,0:T(8,128)(2,1)}, ...), branch_computations={%region_8.9_spmd, %region_9.10_spmd} | conditional | bytes 17694964 | solution.py:456
  105.2 2.7 %project_far.6 = bf16[1,640,256]{2,1,0:T(8,128)(2,1)S(1)} custom-call(bf16[1280,256]{1,0:T(8,128)(2,1)S(1)} %get-tuple-element.133.refs_0_, bf16[2,1280,256]{2,1,0:T(8,128)(2,1)S(1)} %get-tuple-element.134.refs_1_, bf16[320,1280]{1,0:T(8,128)(2,1)} %get-tuple-element.135.refs_2_, bf16[320,1280]{1,0:T(8,128)(2,1)} %get-tuple-element.136.refs_3_, ...), custom_call_target="tpu_custom_call" | custom-call | tf_op jit(solution)/shard_map/cond/branch_1_fun/project_far/pallas_call | solution.py:710
  112.6 6.7 %conditional.11 = (bf16[1,640,256]{2,1,0:T(8,128)(2,1)S(1)}, bf16[320,1280]{1,0:T(8,128)(2,1)}, bf16[320,1280]{1,0:T(8,128)(2,1)}) conditional(s32[]{:T(128)} %convert_element_type.7, () %tuple.87, (bf16[320,1280]{1,0:T(8,128)(2,1)}, bf16[320,1280]{1,0:T(8,128)(2,1)}, bf16[1280,256]{1,0:T(8,128)(2,1)S(1)}, ...), branch_computations={%region_10.11_spmd, %region_11.12_spmd} | conditional | bytes 6553704 | solution.py:456
  116.4 2.9 %project_far.7 = bf16[1,640,256]{2,1,0:T(8,128)(2,1)S(1)} custom-call(bf16[1280,256]{1,0:T(8,128)(2,1)S(1)} %get-tuple-element.144.refs_0_, bf16[2,1280,256]{2,1,0:T(8,128)(2,1)S(1)} %get-tuple-element.145.refs_1_, bf16[320,1280]{1,0:T(8,128)(2,1)} %get-tuple-element.146.refs_2_, bf16[320,1280]{1,0:T(8,128)(2,1)} %get-tuple-element.147.refs_3_, ...), custom_call_target="tpu_custom_call" | custom-call | tf_op jit(solution)/shard_map/cond/branch_1_fun/project_far/pallas_call | solution.py:710
  121.3 3.0 %project_own.7 = f32[1,640,256]{2,1,0:T(8,128)S(1)} custom-call(bf16[1280,256]{1,0:T(8,128)(2,1)S(1)} %get-tuple-element.244.refs_0_, bf16[2,1280,256]{2,1,0:T(8,128)(2,1)S(1)} %collective-permute-done.23.refs_1_, bf16[320,1280]{1,0:T(8,128)(2,1)} %collective-permute-done.27.refs_2_, bf16[320,1280]{1,0:T(8,128)(2,1)} %collective-permute-done.28.refs_3_, ...), custom_call_target="tpu_custom_call" | custom-call | tf_op jit(solution)/shard_map/project_own/pallas_call | solution.py:710
  124.4 2.5 %project_own.6 = f32[1,640,256]{2,1,0:T(8,128)S(1)} custom-call(bf16[1280,256]{1,0:T(8,128)(2,1)S(1)} %get-tuple-element.244.refs_0_, bf16[2,1280,256]{2,1,0:T(8,128)(2,1)S(1)} %collective-permute-done.23.refs_1_, bf16[320,1280]{1,0:T(8,128)(2,1)} %collective-permute-done.18.refs_2_, bf16[320,1280]{1,0:T(8,128)(2,1)} %collective-permute-done.26.refs_3_, ...), custom_call_target="tpu_custom_call" | custom-call | tf_op jit(solution)/shard_map/project_own/pallas_call | solution.py:710
  129.1 2.8 %assemble.1 = bf16[256,2560]{1,0:T(8,128)(2,1)} custom-call(s32[1]{0:T(128)} %bitcast.7.place_ref, f32[640,256]{1,0:T(8,128)S(1)} %copy-done.14, bf16[640,256]{1,0:T(8,128)(2,1)} %get-tuple-element.246.refs_1_, f32[640,256]{1,0:T(8,128)S(1)} %copy-done.16, bf16[640,256]{1,0:T(8,128)(2,1)} %get-tuple-element.251.refs_3_, f32[640,256]{1,0:T(8,128)S(1)} %bitcast.18, ...), custom_call_target="tpu_custom_call" | custom-call | tf_op jit(solution)/shard_map/assemble/pallas_call | solution.py:783
  (118 shorter events, 52.3 us)
Async XLA Ops:
  0.0 57.9 %collective-permute-start.13 = (bf16[320,1280]{1,0:T(8,128)(2,1)}, bf16[320,1280]{1,0:T(8,128)(2,1)}, u32[]{:S(2)}, u32[]{:S(2)}) collective-permute-start(bf16[320,1280]{1,0:T(8,128)(2,1)} %bitcast.21), channel_id=1, source_target_pairs={{0,16},{4,20},{8,24},{12,28},{16,0},{20,4},{24,8},{28,12},{1,17},{... | collective-permute-start | bytes 2457608 | tf_op jit(solution)/shard_map/ppermute | solution.py:28
  4.0 53.9 %collective-permute-start.18 = (bf16[320,1280]{1,0:T(8,128)(2,1)}, bf16[320,1280]{1,0:T(8,128)(2,1)}, u32[]{:S(2)}, u32[]{:S(2)}) collective-permute-start(bf16[320,1280]{1,0:T(8,128)(2,1)} %bitcast.22), channel_id=1, source_target_pairs={{0,8},{4,12},{8,0},{12,4},{16,24},{20,28},{24,16},{28,20},{1,9},{5... | collective-permute-start | bytes 2457608 | tf_op jit(solution)/shard_map/ppermute | solution.py:28
  5.6 52.3 %collective-permute-start.17 = (bf16[320,1280]{1,0:T(8,128)(2,1)}, bf16[320,1280]{1,0:T(8,128)(2,1)}, u32[]{:S(2)}, u32[]{:S(2)}) collective-permute-start(bf16[320,1280]{1,0:T(8,128)(2,1)} %bitcast.23), channel_id=1, source_target_pairs={{0,4},{4,0},{8,12},{12,8},{16,20},{20,16},{24,28},{28,24},{1,5},{5... | collective-permute-start | bytes 2457608 | tf_op jit(solution)/shard_map/ppermute | solution.py:28
  9.0 4.9 %collective-permute-start.14 = (f32[2,20,256]{2,1,0:T(8,128)S(1)}, f32[2,20,256]{2,1,0:T(8,128)S(1)}, u32[]{:S(2)}, u32[]{:S(2)}) collective-permute-start(f32[2,20,256]{2,1,0:T(8,128)S(1)} %get-tuple-element.212), channel_id=1, source_target_pairs={{0,2},{1,3},{2,0},{3,1},{4,6},{5,7},{6,4},{7,5},{8,10},{9,11},{10,... | collective-permute-start | bytes 122888 | tf_op jit(solution)/shard_map/ppermute | solution.py:28
  13.9 8.5 %collective-permute-start.16 = (bf16[1280,128]{1,0:T(8,128)(2,1)S(1)}, bf16[1280,128]{1,0:T(8,128)(2,1)S(1)}, u32[]{:S(2)}, u32[]{:S(2)}) collective-permute-start(bf16[1280,128]{1,0:T(8,128)(2,1)S(1)} %get-tuple-element.216.refs_2_), channel_id=1, source_target_pairs={{0,2},{1,3},{2,0},{3,1},{4,6},{5,7},{6,4},{7,5},{8,10},{9,11},{10,... | collective-permute-start | bytes 983048 | tf_op jit(solution)/shard_map/ppermute | solution.py:28
  22.4 6.1 %collective-permute-start.12 = (bf16[1280,256]{1,0:T(8,128)(2,1)}, bf16[1280,256]{1,0:T(8,128)(2,1)S(1)}, u32[]{:S(2)}, u32[]{:S(2)}) collective-permute-start(bf16[1280,256]{1,0:T(8,128)(2,1)} %get-tuple-element.100), channel_id=1, source_target_pairs={{0,1},{1,0},{2,3},{3,2},{4,5},{5,4},{6,7},{7,6},{8,9},{9,8},{10,11... | collective-permute-start | bytes 1966088 | tf_op jit(solution)/shard_map/cond/branch_1_fun/ppermute | solution.py:28
  22.6 10.0 %collective-permute-start.11 = (bf16[1280,128]{1,0:T(8,128)(2,1)S(1)}, bf16[1280,128]{1,0:T(8,128)(2,1)S(1)}, u32[]{:S(2)}, u32[]{:S(2)}) collective-permute-start(bf16[1280,128]{1,0:T(8,128)(2,1)S(1)} %get-tuple-element.92), channel_id=1, source_target_pairs={{0,2},{1,3},{2,0},{3,1},{4,6},{5,7},{6,4},{7,5},{8,10},{9,11},{10,... | collective-permute-start | bytes 983048 | tf_op jit(solution)/shard_map/cond/branch_1_fun/ppermute | solution.py:28
  34.7 24.9 %collective-permute-start.21 = (bf16[1280,384]{1,0:T(8,128)(2,1)}, bf16[1280,384]{1,0:T(8,128)(2,1)S(1)}, u32[]{:S(2)}, u32[]{:S(2)}) collective-permute-start(bf16[1280,384]{1,0:T(8,128)(2,1)} %get-tuple-element.226), channel_id=1, source_target_pairs={{0,2},{1,3},{2,0},{3,1},{4,6},{5,7},{6,4},{7,5},{8,10},{9,11},{10,... | collective-permute-start | bytes 2949128 | tf_op jit(solution)/shard_map/ppermute | solution.py:28
  36.0 9.3 %collective-permute-start.1 = (bf16[1312,128]{1,0:T(8,128)(2,1)S(1)}, bf16[1312,128]{1,0:T(8,128)(2,1)}, u32[]{:S(2)}, u32[]{:S(2)}) collective-permute-start(bf16[1312,128]{1,0:T(8,128)(2,1)S(1)} %get-tuple-element.111), channel_id=1, source_target_pairs={{0,4},{4,0},{8,12},{12,8},{16,20},{20,16},{24,28},{28,24},{1,5},{5... | collective-permute-start | bytes 1007624 | tf_op jit(solution)/shard_map/cond/branch_1_fun/ppermute | solution.py:28
  47.4 8.6 %collective-permute-start.2 = (bf16[1312,128]{1,0:T(8,128)(2,1)}, bf16[1312,128]{1,0:T(8,128)(2,1)}, u32[]{:S(2)}, u32[]{:S(2)}) collective-permute-start(bf16[1312,128]{1,0:T(8,128)(2,1)} %get-tuple-element.115), channel_id=1, source_target_pairs={{0,8},{4,12},{8,0},{12,4},{16,24},{20,28},{24,16},{28,20},{1,9},{5... | collective-permute-start | bytes 1007624 | tf_op jit(solution)/shard_map/cond/branch_1_fun/ppermute | solution.py:28
  58.0 18.6 %collective-permute-start.22 = (bf16[1312,128]{1,0:T(8,128)(2,1)}, bf16[1312,128]{1,0:T(8,128)(2,1)S(1)}, u32[]{:S(2)}, u32[]{:S(2)}) collective-permute-start(bf16[1312,128]{1,0:T(8,128)(2,1)} %get-tuple-element.223), channel_id=1, source_target_pairs={{0,16},{4,20},{8,24},{12,28},{16,0},{20,4},{24,8},{28,12},{1,17},{... | collective-permute-start | bytes 1007624 | tf_op jit(solution)/shard_map/ppermute | solution.py:28
  58.4 21.9 %collective-permute-start.19 = (bf16[320,1280]{1,0:T(8,128)(2,1)}, bf16[320,1280]{1,0:T(8,128)(2,1)S(1)}, u32[]{:S(2)}, u32[]{:S(2)}) collective-permute-start(bf16[320,1280]{1,0:T(8,128)(2,1)} %collective-permute-done.13), channel_id=1, source_target_pairs={{0,4},{4,0},{8,12},{12,8},{16,20},{20,16},{24,28},{28,24},{1,5},{5... | collective-permute-start | bytes 2457608 | tf_op jit(solution)/shard_map/ppermute | solution.py:28
  59.0 27.5 %collective-permute-start.26 = (bf16[320,1280]{1,0:T(8,128)(2,1)}, bf16[320,1280]{1,0:T(8,128)(2,1)}, u32[]{:S(2)}, u32[]{:S(2)}) collective-permute-start(bf16[320,1280]{1,0:T(8,128)(2,1)} %collective-permute-done.13), channel_id=1, source_target_pairs={{0,8},{4,12},{8,0},{12,4},{16,24},{20,28},{24,16},{28,20},{1,9},{5... | collective-permute-start | bytes 2457608 | tf_op jit(solution)/shard_map/ppermute | solution.py:28
  79.7 8.3 %collective-permute-start.23 = (bf16[2,1280,256]{2,1,0:T(8,128)(2,1)S(1)}, bf16[2,1280,256]{2,1,0:T(8,128)(2,1)S(1)}, u32[]{:S(2)}, u32[]{:S(2)}) collective-permute-start(bf16[2,1280,256]{2,1,0:T(8,128)(2,1)S(1)} %get-tuple-element.241), channel_id=1, source_target_pairs={{0,1},{1,0},{2,3},{3,2},{4,5},{5,4},{6,7},{7,6},{8,9},{9,8},{10,11... | collective-permute-start | bytes 3932168 | tf_op jit(solution)/shard_map/ppermute | solution.py:28
  79.8 8.2 %collective-permute-start.25 = (bf16[320,1280]{1,0:T(8,128)(2,1)}, bf16[320,1280]{1,0:T(8,128)(2,1)S(1)}, u32[]{:S(2)}, u32[]{:S(2)}) collective-permute-start(bf16[320,1280]{1,0:T(8,128)(2,1)} %collective-permute-done.17), channel_id=1, source_target_pairs={{0,1},{1,0},{2,3},{3,2},{4,5},{5,4},{6,7},{7,6},{8,9},{9,8},{10,11... | collective-permute-start | bytes 2457608 | tf_op jit(solution)/shard_map/ppermute | solution.py:28
  80.3 7.7 %collective-permute-start.24 = (bf16[320,1280]{1,0:T(8,128)(2,1)S(1)}, bf16[320,1280]{1,0:T(8,128)(2,1)S(1)}, u32[]{:S(2)}, u32[]{:S(2)}) collective-permute-start(bf16[320,1280]{1,0:T(8,128)(2,1)S(1)} %bitcast.24), channel_id=1, source_target_pairs={{0,1},{1,0},{2,3},{3,2},{4,5},{5,4},{6,7},{7,6},{8,9},{9,8},{10,11... | collective-permute-start | bytes 2457608 | tf_op jit(solution)/shard_map/ppermute | solution.py:28
  86.5 25.2 %collective-permute-start.28 = (bf16[320,1280]{1,0:T(8,128)(2,1)}, bf16[320,1280]{1,0:T(8,128)(2,1)}, u32[]{:S(2)}, u32[]{:S(2)}) collective-permute-start(bf16[320,1280]{1,0:T(8,128)(2,1)} %collective-permute-done.26.refs_3_), channel_id=1, source_target_pairs={{0,4},{4,0},{8,12},{12,8},{16,20},{20,16},{24,28},{28,24},{1,5},{5... | collective-permute-start | bytes 2457608 | tf_op jit(solution)/shard_map/ppermute | solution.py:28
  88.0 23.7 %collective-permute-start.27 = (bf16[320,1280]{1,0:T(8,128)(2,1)}, bf16[320,1280]{1,0:T(8,128)(2,1)}, u32[]{:S(2)}, u32[]{:S(2)}) collective-permute-start(bf16[320,1280]{1,0:T(8,128)(2,1)} %collective-permute-done.17), channel_id=1, source_target_pairs={{0,8},{4,12},{8,0},{12,4},{16,24},{20,28},{24,16},{28,20},{1,9},{5... | collective-permute-start | bytes 2457608 | tf_op jit(solution)/shard_map/ppermute | solution.py:28
  90.8 9.9 %collective-permute-start.5 = (bf16[640,256]{1,0:T(8,128)(2,1)S(1)}, bf16[640,256]{1,0:T(8,128)(2,1)}, u32[]{:S(2)}, u32[]{:S(2)}) collective-permute-start(bf16[640,256]{1,0:T(8,128)(2,1)S(1)} %bitcast.20), channel_id=1, source_target_pairs={{0,2},{1,3},{2,0},{3,1},{4,6},{5,7},{6,4},{7,5},{8,10},{9,11},{10,... | collective-permute-start | bytes 983048 | tf_op jit(solution)/shard_map/cond/branch_1_fun/ppermute | solution.py:28
  101.5 3.7 %collective-permute-start.7 = (bf16[320,1280]{1,0:T(8,128)(2,1)}, bf16[320,1280]{1,0:T(8,128)(2,1)S(1)}, u32[]{:S(2)}, u32[]{:S(2)}) collective-permute-start(bf16[320,1280]{1,0:T(8,128)(2,1)} %get-tuple-element.136.refs_3_), channel_id=1, source_target_pairs={{0,1},{1,0},{2,3},{3,2},{4,5},{5,4},{6,7},{7,6},{8,9},{9,8},{10,11... | collective-permute-start | bytes 2457608 | tf_op jit(solution)/shard_map/cond/branch_1_fun/ppermute | solution.py:28
  102.0 9.7 %collective-permute-start.8 = (bf16[640,256]{1,0:T(8,128)(2,1)S(1)}, bf16[640,256]{1,0:T(8,128)(2,1)}, u32[]{:S(2)}, u32[]{:S(2)}) collective-permute-start(bf16[640,256]{1,0:T(8,128)(2,1)S(1)} %bitcast.31), channel_id=1, source_target_pairs={{0,2},{1,3},{2,0},{3,1},{4,6},{5,7},{6,4},{7,5},{8,10},{9,11},{10,... | collective-permute-start | bytes 983048 | tf_op jit(solution)/shard_map/cond/branch_1_fun/ppermute | solution.py:28
  111.7 8.8 %collective-permute-start.29 = (bf16[640,256]{1,0:T(8,128)(2,1)S(1)}, bf16[640,256]{1,0:T(8,128)(2,1)S(1)}, u32[]{:S(2)}, u32[]{:S(2)}) collective-permute-start(bf16[640,256]{1,0:T(8,128)(2,1)S(1)} %bitcast.32), channel_id=1, source_target_pairs={{0,2},{1,3},{2,0},{3,1},{4,6},{5,7},{6,4},{7,5},{8,10},{9,11},{10,... | collective-permute-start | bytes 983048 | tf_op jit(solution)/shard_map/ppermute | solution.py:28
  112.6 3.8 %collective-permute-start.9 = (bf16[320,1280]{1,0:T(8,128)(2,1)}, bf16[320,1280]{1,0:T(8,128)(2,1)}, u32[]{:S(2)}, u32[]{:S(2)}) collective-permute-start(bf16[320,1280]{1,0:T(8,128)(2,1)} %get-tuple-element.146.refs_2_), channel_id=1, source_target_pairs={{0,1},{1,0},{2,3},{3,2},{4,5},{5,4},{6,7},{7,6},{8,9},{9,8},{10,11... | collective-permute-start | bytes 2457608 | tf_op jit(solution)/shard_map/cond/branch_1_fun/ppermute | solution.py:28
  120.6 8.6 %collective-permute-start.30 = (bf16[640,256]{1,0:T(8,128)(2,1)S(1)}, bf16[640,256]{1,0:T(8,128)(2,1)S(1)}, u32[]{:S(2)}, u32[]{:S(2)}) collective-permute-start(bf16[640,256]{1,0:T(8,128)(2,1)S(1)} %bitcast.33), channel_id=1, source_target_pairs={{0,2},{1,3},{2,0},{3,1},{4,6},{5,7},{6,4},{7,5},{8,10},{9,11},{10,... | collective-permute-start | bytes 983048 | tf_op jit(solution)/shard_map/ppermute | solution.py:28
  (30 other events, 153.7 us)

commit v6 on v5

--- a/solution.py
+++ b/solution.py
@@ -740,11 +740,8 @@
 
     def middle_group(index):
         def body(far, kept, others, blocks, partners):
-            known = partners
-            partners, more = with_partners({r: blocks[r] for r in groups[index]}, partners)
-            next_far = far_rows(groups[index], kept, others, blocks, partners)
-            own = own_rows(groups[index - 1], [tie(kept[0], next_far)], others, blocks, known)
-            return next_far, send_rows(far), more, own
+            partners, more = with_partners(blocks, partners)
+            return far_rows(groups[index], kept, others, blocks, partners), send_rows(far), more
 
         return body
 
@@ -763,12 +760,10 @@
     owns = [own]
     partners.update(more)
     for index in range(2, len(groups) - 1):
-        both = groups[index - 1] + groups[index]
-        far, got, more, own = fenced(
-            middle_group(index), far, kept, others, some(held, both), some(partners, both)
+        far, got, more = fenced(
+            middle_group(index), far, kept, others, some(held, groups[index]), some(partners, groups[index])
         )
         arrived.append(got)
-        owns.append(own)
         partners.update(more)
     got = send_rows(far, *[held[r] for r in groups[-1]])
     arrived.append(got)

time: 133 us -> 131 us (0.985)
  local copies, waits for them, and re-layouts: 4.74 us -> 8 us
  Pallas kernels: 54.9 us -> 51.9 us
    cond x15 -> x7, local copies, waits for them, and re-layouts: 0.84 us -> 2.5 us
    unnamed x32 -> x30, local copies, waits for them, and re-layouts: 2.64 us -> 3.34 us
  transfers between devices with their start and end apart: 31 -> 31, of which waited for: 16 -> 16; matrix products, arithmetic and copies ran while one was open for 2% -> 3% of each run, Pallas kernels for 40% -> 38%
where the time goes in v6:
time: 131 us
  Pallas kernels  51.9 us (40%)
  waiting for transfers between devices  49.8 us (38%)
  starting transfers between devices  20.7 us (16%)
  local copies, waits for them, and re-layouts  8 us (6%)
    ppermute x31, waiting for transfers between devices, swap(): return lax.ppermute(value, axis, pairs)  49.8 us
    pallas_call x8, Pallas kernels, project(): kernel_call(project_kernel, name, shape((rows, count * columns, rows_dev)...  20.9 us
    ppermute x31, starting transfers between devices, swap(): return lax.ppermute(value, axis, pairs)  20.7 us
    pallas_call x1, Pallas kernels, on_device(): kernel_call(functools.partial(local_kernel, near, pieces), 'local_levels'...  11 us
    pallas_call x2, Pallas kernels, step(): kernel_call(functools.partial(merge_kernel, bit, head_count), 'merge', tu...  3.91 us
    pallas_call x1, Pallas kernels, chip_sum(): kernel_call(functools.partial(factors_kernel, levels, heads_size), 'facto...  3.7 us
    unnamed x30, local copies, waits for them, and re-layouts  3.34 us
    pallas_call x1, Pallas kernels, on_device(): kernel_call(functools.partial(assemble_kernel, groups), 'assemble', shape...  2.78 us
  transfers between devices with their start and end apart: 31, of which 16 were waited for; matrix products, arithmetic and copies ran while one was open for 3% of the time, Pallas kernels for 38%

profile of v6, /device:TPU:0, one launch (start us, length us, event | category | flops | bytes accessed | tf_op | source)
XLA Modules:
  0.0 130.7 jit_solution(13617106096071577957)
XLA Ops:
  0.0 4.0 %collective-permute-start.13 = (bf16[320,1280]{1,0:T(8,128)(2,1)}, bf16[320,1280]{1,0:T(8,128)(2,1)}, u32[]{:S(2)}, u32[]{:S(2)}) collective-permute-start(bf16[320,1280]{1,0:T(8,128)(2,1)} %bitcast.22), channel_id=1, source_target_pairs={{0,16},{4,20},{8,24},{12,28},{16,0},{20,4},{24,8},{28,12},{1,17},{... | collective-permute-start | bytes 2457608 | tf_op jit(solution)/shard_map/ppermute | solution.py:28
  17.9 3.3 %conditional.6 = (bf16[2,1280,128]{2,1,0:T(8,128)(2,1)}, bf16[1280,128]{1,0:T(8,128)(2,1)S(1)}) conditional(s32[]{:T(128)} %convert_element_type.7, () %tuple.69, (bf16[2,1280,128]{2,1,0:T(8,128)(2,1)S(1)}, f32[2,1280,128]{2,1,0:T(8,128)S(1)}) %tuple.70), branch_computations={%region_0.0_spmd, %region_1.0_spmd} | conditional | bytes 2621496 | solution.py:456
  22.2 11.4 %conditional.7 = (f32[1280,128]{1,0:T(8,128)S(1)}, bf16[1312,128]{1,0:T(8,128)(2,1)S(1)}, f32[4,20,256]{2,1,0:T(8,128)}, f32[5,4,20,256]{3,2,1,0:T(8,128)}, f32[...) conditional(s32[]{:T(128)} %convert_element_type.7, () %tuple.68, ...), branch_computations={%region_2.0_spmd, %region_3.4_spmd} | conditional | bytes 7295176 | solution.py:456
  26.2 3.7 %factors.1 = (f32[4,20,256]{2,1,0:T(8,128)}, f32[5,4,20,256]{3,2,1,0:T(8,128)}, f32[3,4,20,256]{3,2,1,0:T(8,128)}, f32[26,20,128]{2,1,0:T(8,128)}, bf16[4,2,256,...) custom-call(f32[20,1024]{1,0:T(8,128)} %get-tuple-element.83.decay_r, ...), custom_call_target="tpu_custom_call" | custom-call | tf_op jit(solution)/shard_map/cond/branch_1_fun/factors/pallas_call | solution.py:581
  34.4 20.9 %conditional.8 = (bf16[1312,128]{1,0:T(8,128)(2,1)}, bf16[1312,128]{1,0:T(8,128)(2,1)}, f32[32,128]{1,0:T(8,128)S(1)}, f32[32,128]{1,0:T(8,128)S(1)}, f32[32,128]{1,0:T(8,128)S(1)}, /*index=5*/bf16[1312,128]{1,0:T(8,128)(2,1)}) conditional(s32[]{:T(128)} %convert_element_type.7, () %tuple.67, (bf16[1312,128]{1,0:T(8,128)(2,1)S(1)}, s32[1]{0:T(128)}, ...), branch_computations={%region_4.5_spmd, %region_5.6_spmd} | conditional | flops 12 | bytes 2719997 | solution.py:456
  35.0 8.3 %collective-permute-done.1.got_ref = bf16[1312,128]{1,0:T(8,128)(2,1)} collective-permute-done((bf16[1312,128]{1,0:T(8,128)(2,1)S(1)}, bf16[1312,128]{1,0:T(8,128)(2,1)}, u32[]{:S(2)}, u32[]{:S(2)}) %collective-permute-start.1) | collective-permute-done | bytes 335904 | tf_op jit(solution)/shard_map/cond/branch_1_fun/ppermute | solution.py:28
  45.7 7.7 %collective-permute-done.2.got_ref = bf16[1312,128]{1,0:T(8,128)(2,1)} collective-permute-done((bf16[1312,128]{1,0:T(8,128)(2,1)}, bf16[1312,128]{1,0:T(8,128)(2,1)}, u32[]{:S(2)}, u32[]{:S(2)}) %collective-permute-start.2) | collective-permute-done | bytes 335904 | tf_op jit(solution)/shard_map/cond/branch_1_fun/ppermute | solution.py:28
  57.6 11.0 %local_levels.1.pre_ref = f32[4,1280,256]{2,1,0:T(8,128)S(1)} custom-call(s32[1]{0:T(128)} %bitcast.8.me_ref, bf16[1280,256]{1,0:T(8,128)(2,1)S(1)} %get-tuple-element.188.refs_0_, bf16[1280,256]{1,0:T(8,128)(2,1)S(1)} %collective-permute-done.20.refs_1_, bf16[1280,128]{1,0:T(8,128)(2,1)S(1)} %collective-permute-done.16.refs_2_, ...), custom_call_target="tpu_custom_call" | custom-call | tf_op jit(solution)/shard_map/local_levels/pallas_call | solution.py:661
  68.6 5.4 %collective-permute-done.22.state_ref = bf16[1312,128]{1,0:T(8,128)(2,1)S(1)} collective-permute-done((bf16[1312,128]{1,0:T(8,128)(2,1)}, bf16[1312,128]{1,0:T(8,128)(2,1)S(1)}, u32[]{:S(2)}, u32[]{:S(2)}) %collective-permute-start.22) | collective-permute-done | bytes 335904 | tf_op jit(solution)/shard_map/ppermute | solution.py:28
  76.6 7.4 %collective-permute-done.26.refs_3_ = bf16[320,1280]{1,0:T(8,128)(2,1)} collective-permute-done((bf16[320,1280]{1,0:T(8,128)(2,1)}, bf16[320,1280]{1,0:T(8,128)(2,1)}, u32[]{:S(2)}, u32[]{:S(2)}) %collective-permute-start.26) | collective-permute-done | bytes 819232 | tf_op jit(solution)/shard_map/ppermute | solution.py:28
  85.4 12.6 %conditional.9 = (bf16[1,640,256]{2,1,0:T(8,128)(2,1)S(1)}, bf16[640,256]{1,0:T(8,128)(2,1)}, bf16[320,1280]{1,0:T(8,128)(2,1)}, bf16[320,1280]{1,0:T(8,128)(2,1)}, f32[640,256]{1,0:T(8,128)S(1)}) conditional(s32[]{:T(128)} %convert_element_type.7, () %tuple.66, (bf16[320,1280]{1,0:T(8,128)(2,1)}, bf16[320,1280]{1,0:T(8,128)(2,1)S(1)}, ...), branch_computations={%region_6.7_spmd, %region_7.8_spmd} | conditional | bytes 14418136 | solution.py:456
  86.0 2.1 %project_far.5 = bf16[1,640,256]{2,1,0:T(8,128)(2,1)S(1)} custom-call(bf16[1280,256]{1,0:T(8,128)(2,1)S(1)} %get-tuple-element.113.refs_0_, bf16[2,1280,256]{2,1,0:T(8,128)(2,1)S(1)} %get-tuple-element.114.refs_1_, bf16[320,1280]{1,0:T(8,128)(2,1)S(1)} %get-tuple-element.117.refs_2_, bf16[320,1280]{1,0:T(8,128)(2,1)} %get-tuple-element.118.refs_3_, ...), custom_call_target="tpu_custom_call" | custom-call | tf_op jit(solution)/shard_map/cond/branch_1_fun/project_far/pallas_call | solution.py:710
  89.2 2.7 %project_far.4 = bf16[1,640,256]{2,1,0:T(8,128)(2,1)S(1)} custom-call(bf16[1280,256]{1,0:T(8,128)(2,1)S(1)} %get-tuple-element.113.refs_0_, bf16[2,1280,256]{2,1,0:T(8,128)(2,1)S(1)} %get-tuple-element.114.refs_1_, bf16[320,1280]{1,0:T(8,128)(2,1)} %get-tuple-element.115.refs_2_, bf16[320,1280]{1,0:T(8,128)(2,1)S(1)} %get-tuple-element.116.refs_3_, ...), custom_call_target="tpu_custom_call" | custom-call | tf_op jit(solution)/shard_map/cond/branch_1_fun/project_far/pallas_call | solution.py:710
  94.1 4.0 %collective-permute-done.5 = bf16[640,256]{1,0:T(8,128)(2,1)} collective-permute-done((bf16[640,256]{1,0:T(8,128)(2,1)S(1)}, bf16[640,256]{1,0:T(8,128)(2,1)}, u32[]{:S(2)}, u32[]{:S(2)}) %collective-permute-start.5) | collective-permute-done | bytes 327712 | tf_op jit(solution)/shard_map/cond/branch_1_fun/ppermute | solution.py:28
  98.9 10.2 %conditional.10 = (bf16[1,640,256]{2,1,0:T(8,128)(2,1)S(1)}, bf16[640,256]{1,0:T(8,128)(2,1)}, bf16[320,1280]{1,0:T(8,128)(2,1)}, bf16[320,1280]{1,0:T(8,128)(2,1)}) conditional(s32[]{:T(128)} %convert_element_type.7, () %tuple.81, (bf16[320,1280]{1,0:T(8,128)(2,1)}, bf16[320,1280]{1,0:T(8,128)(2,1)}, bf16[1280,256]{1,0:T(8,128)(2,1)S(1)}, ...), branch_computations={%region_8.9_spmd, %region_9.10_spmd} | conditional | bytes 7864472 | solution.py:456
  102.7 2.9 %project_far.6 = bf16[1,640,256]{2,1,0:T(8,128)(2,1)S(1)} custom-call(bf16[1280,256]{1,0:T(8,128)(2,1)S(1)} %get-tuple-element.123.refs_0_, bf16[2,1280,256]{2,1,0:T(8,128)(2,1)S(1)} %get-tuple-element.124.refs_1_, bf16[320,1280]{1,0:T(8,128)(2,1)} %get-tuple-element.125.refs_2_, bf16[320,1280]{1,0:T(8,128)(2,1)} %get-tuple-element.126.refs_3_, ...), custom_call_target="tpu_custom_call" | custom-call | tf_op jit(solution)/shard_map/cond/branch_1_fun/project_far/pallas_call | solution.py:710
  105.6 3.5 %collective-permute-done.8 = bf16[640,256]{1,0:T(8,128)(2,1)} collective-permute-done((bf16[640,256]{1,0:T(8,128)(2,1)S(1)}, bf16[640,256]{1,0:T(8,128)(2,1)}, u32[]{:S(2)}, u32[]{:S(2)}) %collective-permute-start.8) | collective-permute-done | bytes 327712 | tf_op jit(solution)/shard_map/cond/branch_1_fun/ppermute | solution.py:28
  110.7 6.7 %conditional.11 = (bf16[1,640,256]{2,1,0:T(8,128)(2,1)S(1)}, bf16[320,1280]{1,0:T(8,128)(2,1)}, bf16[320,1280]{1,0:T(8,128)(2,1)}) conditional(s32[]{:T(128)} %convert_element_type.7, () %tuple.86, (bf16[320,1280]{1,0:T(8,128)(2,1)}, bf16[320,1280]{1,0:T(8,128)(2,1)}, bf16[1280,256]{1,0:T(8,128)(2,1)S(1)}, ...), branch_computations={%region_10.11_spmd, %region_11.12_spmd} | conditional | bytes 6553704 | solution.py:456
  111.2 2.2 %collective-permute-done.10.refs_5_ = bf16[320,1280]{1,0:T(8,128)(2,1)} collective-permute-done((bf16[320,1280]{1,0:T(8,128)(2,1)}, bf16[320,1280]{1,0:T(8,128)(2,1)}, u32[]{:S(2)}, u32[]{:S(2)}) %collective-permute-start.10) | collective-permute-done | bytes 819232 | tf_op jit(solution)/shard_map/cond/branch_1_fun/ppermute | solution.py:28
  114.6 2.9 %project_far.7 = bf16[1,640,256]{2,1,0:T(8,128)(2,1)S(1)} custom-call(bf16[1280,256]{1,0:T(8,128)(2,1)S(1)} %get-tuple-element.128.refs_0_, bf16[2,1280,256]{2,1,0:T(8,128)(2,1)S(1)} %get-tuple-element.129.refs_1_, bf16[320,1280]{1,0:T(8,128)(2,1)} %get-tuple-element.130.refs_2_, bf16[320,1280]{1,0:T(8,128)(2,1)} %get-tuple-element.131.refs_3_, ...), custom_call_target="tpu_custom_call" | custom-call | tf_op jit(solution)/shard_map/cond/branch_1_fun/project_far/pallas_call | solution.py:710
  119.7 2.9 %project_own.7 = f32[1,640,256]{2,1,0:T(8,128)S(1)} custom-call(bf16[1280,256]{1,0:T(8,128)(2,1)S(1)} %get-tuple-element.227.refs_0_, bf16[2,1280,256]{2,1,0:T(8,128)(2,1)S(1)} %collective-permute-done.23.refs_1_, bf16[320,1280]{1,0:T(8,128)(2,1)} %collective-permute-done.27.refs_2_, bf16[320,1280]{1,0:T(8,128)(2,1)} %collective-permute-done.28.refs_3_, ...), custom_call_target="tpu_custom_call" | custom-call | tf_op jit(solution)/shard_map/project_own/pallas_call | solution.py:710
  122.6 3.0 %project_own.6 = f32[1,640,256]{2,1,0:T(8,128)S(1)} custom-call(bf16[1280,256]{1,0:T(8,128)(2,1)S(1)} %get-tuple-element.227.refs_0_, bf16[2,1280,256]{2,1,0:T(8,128)(2,1)S(1)} %collective-permute-done.23.refs_1_, bf16[320,1280]{1,0:T(8,128)(2,1)} %collective-permute-done.18.refs_2_, bf16[320,1280]{1,0:T(8,128)(2,1)} %collective-permute-done.26.refs_3_, ...), custom_call_target="tpu_custom_call" | custom-call | tf_op jit(solution)/shard_map/project_own/pallas_call | solution.py:710
  125.7 2.2 %project_own.5 = f32[1,640,256]{2,1,0:T(8,128)S(1)} custom-call(bf16[1280,256]{1,0:T(8,128)(2,1)S(1)} %get-tuple-element.227.refs_0_, bf16[2,1280,256]{2,1,0:T(8,128)(2,1)S(1)} %collective-permute-done.23.refs_1_, bf16[320,1280]{1,0:T(8,128)(2,1)} %collective-permute-done.13.refs_2_, bf16[320,1280]{1,0:T(8,128)(2,1)S(1)} %copy-done.8, ...), custom_call_target="tpu_custom_call" | custom-call | tf_op jit(solution)/shard_map/project_own/pallas_call | solution.py:710
  128.0 2.8 %assemble.1 = bf16[256,2560]{1,0:T(8,128)(2,1)} custom-call(s32[1]{0:T(128)} %bitcast.6.place_ref, f32[640,256]{1,0:T(8,128)S(1)} %copy-done.11, bf16[640,256]{1,0:T(8,128)(2,1)} %get-tuple-element.229.refs_1_, f32[640,256]{1,0:T(8,128)S(1)} %bitcast.19, bf16[640,256]{1,0:T(8,128)(2,1)} %get-tuple-element.233.refs_3_, f32[640,256]{1,0:T(8,128)S(1)} %bitcast.18, ...), custom_call_target="tpu_custom_call" | custom-call | tf_op jit(solution)/shard_map/assemble/pallas_call | solution.py:778
  (108 shorter events, 51.6 us)
Async XLA Ops:
  0.0 55.4 %collective-permute-start.13 = (bf16[320,1280]{1,0:T(8,128)(2,1)}, bf16[320,1280]{1,0:T(8,128)(2,1)}, u32[]{:S(2)}, u32[]{:S(2)}) collective-permute-start(bf16[320,1280]{1,0:T(8,128)(2,1)} %bitcast.22), channel_id=1, source_target_pairs={{0,16},{4,20},{8,24},{12,28},{16,0},{20,4},{24,8},{28,12},{1,17},{... | collective-permute-start | bytes 2457608 | tf_op jit(solution)/shard_map/ppermute | solution.py:28
  4.0 51.3 %collective-permute-start.18 = (bf16[320,1280]{1,0:T(8,128)(2,1)}, bf16[320,1280]{1,0:T(8,128)(2,1)}, u32[]{:S(2)}, u32[]{:S(2)}) collective-permute-start(bf16[320,1280]{1,0:T(8,128)(2,1)} %bitcast.23), channel_id=1, source_target_pairs={{0,8},{4,12},{8,0},{12,4},{16,24},{20,28},{24,16},{28,20},{1,9},{5... | collective-permute-start | bytes 2457608 | tf_op jit(solution)/shard_map/ppermute | solution.py:28
  5.6 49.8 %collective-permute-start.17 = (bf16[320,1280]{1,0:T(8,128)(2,1)}, bf16[320,1280]{1,0:T(8,128)(2,1)}, u32[]{:S(2)}, u32[]{:S(2)}) collective-permute-start(bf16[320,1280]{1,0:T(8,128)(2,1)} %bitcast.24), channel_id=1, source_target_pairs={{0,4},{4,0},{8,12},{12,8},{16,20},{20,16},{24,28},{28,24},{1,5},{5... | collective-permute-start | bytes 2457608 | tf_op jit(solution)/shard_map/ppermute | solution.py:28
  9.0 4.9 %collective-permute-start.14 = (f32[2,20,256]{2,1,0:T(8,128)S(1)}, f32[2,20,256]{2,1,0:T(8,128)S(1)}, u32[]{:S(2)}, u32[]{:S(2)}) collective-permute-start(f32[2,20,256]{2,1,0:T(8,128)S(1)} %get-tuple-element.195), channel_id=1, source_target_pairs={{0,2},{1,3},{2,0},{3,1},{4,6},{5,7},{6,4},{7,5},{8,10},{9,11},{10,... | collective-permute-start | bytes 122888 | tf_op jit(solution)/shard_map/ppermute | solution.py:28
  13.9 8.3 %collective-permute-start.16 = (bf16[1280,128]{1,0:T(8,128)(2,1)S(1)}, bf16[1280,128]{1,0:T(8,128)(2,1)S(1)}, u32[]{:S(2)}, u32[]{:S(2)}) collective-permute-start(bf16[1280,128]{1,0:T(8,128)(2,1)S(1)} %get-tuple-element.199.refs_2_), channel_id=1, source_target_pairs={{0,2},{1,3},{2,0},{3,1},{4,6},{5,7},{6,4},{7,5},{8,10},{9,11},{10,... | collective-permute-start | bytes 983048 | tf_op jit(solution)/shard_map/ppermute | solution.py:28
  22.2 7.6 %collective-permute-start.12 = (bf16[1280,256]{1,0:T(8,128)(2,1)}, bf16[1280,256]{1,0:T(8,128)(2,1)S(1)}, u32[]{:S(2)}, u32[]{:S(2)}) collective-permute-start(bf16[1280,256]{1,0:T(8,128)(2,1)} %get-tuple-element.90), channel_id=1, source_target_pairs={{0,1},{1,0},{2,3},{3,2},{4,5},{5,4},{6,7},{7,6},{8,9},{9,8},{10,11... | collective-permute-start | bytes 1966088 | tf_op jit(solution)/shard_map/cond/branch_1_fun/ppermute | solution.py:28
  23.0 9.6 %collective-permute-start.11 = (bf16[1280,128]{1,0:T(8,128)(2,1)}, bf16[1280,128]{1,0:T(8,128)(2,1)S(1)}, u32[]{:S(2)}, u32[]{:S(2)}) collective-permute-start(bf16[1280,128]{1,0:T(8,128)(2,1)} %copy-done.15), channel_id=1, source_target_pairs={{0,2},{1,3},{2,0},{3,1},{4,6},{5,7},{6,4},{7,5},{8,10},{9,11},{10,... | collective-permute-start | bytes 983048 | tf_op jit(solution)/shard_map/cond/branch_1_fun/ppermute | solution.py:28
  33.7 23.5 %collective-permute-start.21 = (bf16[1280,384]{1,0:T(8,128)(2,1)}, bf16[1280,384]{1,0:T(8,128)(2,1)S(1)}, u32[]{:S(2)}, u32[]{:S(2)}) collective-permute-start(bf16[1280,384]{1,0:T(8,128)(2,1)} %get-tuple-element.209), channel_id=1, source_target_pairs={{0,2},{1,3},{2,0},{3,1},{4,6},{5,7},{6,4},{7,5},{8,10},{9,11},{10,... | collective-permute-start | bytes 2949128 | tf_op jit(solution)/shard_map/ppermute | solution.py:28
  34.4 8.9 %collective-permute-start.1 = (bf16[1312,128]{1,0:T(8,128)(2,1)S(1)}, bf16[1312,128]{1,0:T(8,128)(2,1)}, u32[]{:S(2)}, u32[]{:S(2)}) collective-permute-start(bf16[1312,128]{1,0:T(8,128)(2,1)S(1)} %get-tuple-element.101), channel_id=1, source_target_pairs={{0,4},{4,0},{8,12},{12,8},{16,20},{20,16},{24,28},{28,24},{1,5},{5... | collective-permute-start | bytes 1007624 | tf_op jit(solution)/shard_map/cond/branch_1_fun/ppermute | solution.py:28
  45.3 8.1 %collective-permute-start.2 = (bf16[1312,128]{1,0:T(8,128)(2,1)}, bf16[1312,128]{1,0:T(8,128)(2,1)}, u32[]{:S(2)}, u32[]{:S(2)}) collective-permute-start(bf16[1312,128]{1,0:T(8,128)(2,1)} %get-tuple-element.105), channel_id=1, source_target_pairs={{0,8},{4,12},{8,0},{12,4},{16,24},{20,28},{24,16},{28,20},{1,9},{5... | collective-permute-start | bytes 1007624 | tf_op jit(solution)/shard_map/cond/branch_1_fun/ppermute | solution.py:28
  55.5 18.6 %collective-permute-start.22 = (bf16[1312,128]{1,0:T(8,128)(2,1)}, bf16[1312,128]{1,0:T(8,128)(2,1)S(1)}, u32[]{:S(2)}, u32[]{:S(2)}) collective-permute-start(bf16[1312,128]{1,0:T(8,128)(2,1)} %get-tuple-element.206), channel_id=1, source_target_pairs={{0,16},{4,20},{8,24},{12,28},{16,0},{20,4},{24,8},{28,12},{1,17},{... | collective-permute-start | bytes 1007624 | tf_op jit(solution)/shard_map/ppermute | solution.py:28
  55.9 20.7 %collective-permute-start.19 = (bf16[320,1280]{1,0:T(8,128)(2,1)}, bf16[320,1280]{1,0:T(8,128)(2,1)S(1)}, u32[]{:S(2)}, u32[]{:S(2)}) collective-permute-start(bf16[320,1280]{1,0:T(8,128)(2,1)} %collective-permute-done.13.refs_2_), channel_id=1, source_target_pairs={{0,4},{4,0},{8,12},{12,8},{16,20},{20,16},{24,28},{28,24},{1,5},{5... | collective-permute-start | bytes 2457608 | tf_op jit(solution)/shard_map/ppermute | solution.py:28
  56.4 27.5 %collective-permute-start.26 = (bf16[320,1280]{1,0:T(8,128)(2,1)}, bf16[320,1280]{1,0:T(8,128)(2,1)}, u32[]{:S(2)}, u32[]{:S(2)}) collective-permute-start(bf16[320,1280]{1,0:T(8,128)(2,1)} %collective-permute-done.13.refs_2_), channel_id=1, source_target_pairs={{0,8},{4,12},{8,0},{12,4},{16,24},{20,28},{24,16},{28,20},{1,9},{5... | collective-permute-start | bytes 2457608 | tf_op jit(solution)/shard_map/ppermute | solution.py:28
  75.9 9.5 %collective-permute-start.23 = (bf16[2,1280,256]{2,1,0:T(8,128)(2,1)S(1)}, bf16[2,1280,256]{2,1,0:T(8,128)(2,1)S(1)}, u32[]{:S(2)}, u32[]{:S(2)}) collective-permute-start(bf16[2,1280,256]{2,1,0:T(8,128)(2,1)S(1)} %get-tuple-element.224), channel_id=1, source_target_pairs={{0,1},{1,0},{2,3},{3,2},{4,5},{5,4},{6,7},{7,6},{8,9},{9,8},{10,11... | collective-permute-start | bytes 3932168 | tf_op jit(solution)/shard_map/ppermute | solution.py:28
  76.0 9.4 %collective-permute-start.25 = (bf16[320,1280]{1,0:T(8,128)(2,1)}, bf16[320,1280]{1,0:T(8,128)(2,1)S(1)}, u32[]{:S(2)}, u32[]{:S(2)}) collective-permute-start(bf16[320,1280]{1,0:T(8,128)(2,1)} %collective-permute-done.17), channel_id=1, source_target_pairs={{0,1},{1,0},{2,3},{3,2},{4,5},{5,4},{6,7},{7,6},{8,9},{9,8},{10,11... | collective-permute-start | bytes 2457608 | tf_op jit(solution)/shard_map/ppermute | solution.py:28
  76.5 8.9 %collective-permute-start.24 = (bf16[320,1280]{1,0:T(8,128)(2,1)S(1)}, bf16[320,1280]{1,0:T(8,128)(2,1)S(1)}, u32[]{:S(2)}, u32[]{:S(2)}) collective-permute-start(bf16[320,1280]{1,0:T(8,128)(2,1)S(1)} %bitcast.25), channel_id=1, source_target_pairs={{0,1},{1,0},{2,3},{3,2},{4,5},{5,4},{6,7},{7,6},{8,9},{9,8},{10,11... | collective-permute-start | bytes 2457608 | tf_op jit(solution)/shard_map/ppermute | solution.py:28
  84.0 25.1 %collective-permute-start.28 = (bf16[320,1280]{1,0:T(8,128)(2,1)}, bf16[320,1280]{1,0:T(8,128)(2,1)}, u32[]{:S(2)}, u32[]{:S(2)}) collective-permute-start(bf16[320,1280]{1,0:T(8,128)(2,1)} %collective-permute-done.26.refs_3_), channel_id=1, source_target_pairs={{0,4},{4,0},{8,12},{12,8},{16,20},{20,16},{24,28},{28,24},{1,5},{5... | collective-permute-start | bytes 2457608 | tf_op jit(solution)/shard_map/ppermute | solution.py:28
  85.4 23.7 %collective-permute-start.27 = (bf16[320,1280]{1,0:T(8,128)(2,1)}, bf16[320,1280]{1,0:T(8,128)(2,1)}, u32[]{:S(2)}, u32[]{:S(2)}) collective-permute-start(bf16[320,1280]{1,0:T(8,128)(2,1)} %collective-permute-done.17), channel_id=1, source_target_pairs={{0,8},{4,12},{8,0},{12,4},{16,24},{20,28},{24,16},{28,20},{1,9},{5... | collective-permute-start | bytes 2457608 | tf_op jit(solution)/shard_map/ppermute | solution.py:28
  88.2 9.9 %collective-permute-start.5 = (bf16[640,256]{1,0:T(8,128)(2,1)S(1)}, bf16[640,256]{1,0:T(8,128)(2,1)}, u32[]{:S(2)}, u32[]{:S(2)}) collective-permute-start(bf16[640,256]{1,0:T(8,128)(2,1)S(1)} %bitcast.21), channel_id=1, source_target_pairs={{0,2},{1,3},{2,0},{3,1},{4,6},{5,7},{6,4},{7,5},{8,10},{9,11},{10,... | collective-permute-start | bytes 983048 | tf_op jit(solution)/shard_map/cond/branch_1_fun/ppermute | solution.py:28
  98.9 3.8 %collective-permute-start.7 = (bf16[320,1280]{1,0:T(8,128)(2,1)}, bf16[320,1280]{1,0:T(8,128)(2,1)}, u32[]{:S(2)}, u32[]{:S(2)}) collective-permute-start(bf16[320,1280]{1,0:T(8,128)(2,1)} %get-tuple-element.126.refs_3_), channel_id=1, source_target_pairs={{0,1},{1,0},{2,3},{3,2},{4,5},{5,4},{6,7},{7,6},{8,9},{9,8},{10,11... | collective-permute-start | bytes 2457608 | tf_op jit(solution)/shard_map/cond/branch_1_fun/ppermute | solution.py:28
  99.4 9.7 %collective-permute-start.8 = (bf16[640,256]{1,0:T(8,128)(2,1)S(1)}, bf16[640,256]{1,0:T(8,128)(2,1)}, u32[]{:S(2)}, u32[]{:S(2)}) collective-permute-start(bf16[640,256]{1,0:T(8,128)(2,1)S(1)} %bitcast.31), channel_id=1, source_target_pairs={{0,2},{1,3},{2,0},{3,1},{4,6},{5,7},{6,4},{7,5},{8,10},{9,11},{10,... | collective-permute-start | bytes 983048 | tf_op jit(solution)/shard_map/cond/branch_1_fun/ppermute | solution.py:28
  109.8 9.0 %collective-permute-start.29 = (bf16[640,256]{1,0:T(8,128)(2,1)}, bf16[640,256]{1,0:T(8,128)(2,1)S(1)}, u32[]{:S(2)}, u32[]{:S(2)}) collective-permute-start(bf16[640,256]{1,0:T(8,128)(2,1)} %bitcast.32), channel_id=1, source_target_pairs={{0,2},{1,3},{2,0},{3,1},{4,6},{5,7},{6,4},{7,5},{8,10},{9,11},{10,... | collective-permute-start | bytes 983048 | tf_op jit(solution)/shard_map/ppermute | solution.py:28
  110.7 3.8 %collective-permute-start.9 = (bf16[320,1280]{1,0:T(8,128)(2,1)}, bf16[320,1280]{1,0:T(8,128)(2,1)}, u32[]{:S(2)}, u32[]{:S(2)}) collective-permute-start(bf16[320,1280]{1,0:T(8,128)(2,1)} %get-tuple-element.130.refs_2_), channel_id=1, source_target_pairs={{0,1},{1,0},{2,3},{3,2},{4,5},{5,4},{6,7},{7,6},{8,9},{9,8},{10,11... | collective-permute-start | bytes 2457608 | tf_op jit(solution)/shard_map/cond/branch_1_fun/ppermute | solution.py:28
  118.8 9.1 %collective-permute-start.30 = (bf16[640,256]{1,0:T(8,128)(2,1)S(1)}, bf16[640,256]{1,0:T(8,128)(2,1)S(1)}, u32[]{:S(2)}, u32[]{:S(2)}) collective-permute-start(bf16[640,256]{1,0:T(8,128)(2,1)S(1)} %bitcast.33), channel_id=1, source_target_pairs={{0,2},{1,3},{2,0},{3,1},{4,6},{5,7},{6,4},{7,5},{8,10},{9,11},{10,... | collective-permute-start | bytes 983048 | tf_op jit(solution)/shard_map/ppermute | solution.py:28
  (25 other events, 156.7 us)

commit v7 on v6

--- a/solution.py
+++ b/solution.py
@@ -391,10 +391,10 @@
             for far_ref in far_refs:
                 total = total + far_ref[rows, :].astype(F32)
             start = pl.multiple_of((place_ref[0] ^ r) * width, width)
-            columns_ref[pl.ds(start, width), :] = total
+            columns_ref[pl.ds(start, width), :] = total.astype(BF16)
     for first in range(0, out_ref.shape[1], LANES):
         at = slice(first, first + LANES)
-        out_ref[:, at] = jnp.transpose(columns_ref[at, :]).astype(BF16)
+        out_ref[:, at] = jnp.transpose(columns_ref[at, :])
 
 
 def whole(shape):
@@ -635,7 +635,8 @@
     states, factors, sent = fenced(near_steps, running, total, sent)
     states = list(states)
     sent = tie(sent, *[held[2**bit] for bit in range(ctx_bits)])
-    last_state = swap(sent, "ctx", 2**near)
+    upwards = [(source, source + 2**near) for source in range(ctx_size - 2**near)]
+    last_state = lax.ppermute(sent, "ctx", upwards)
 
     for r in range(2, ctx_size):
         low = r & -r
@@ -780,7 +781,7 @@
         "assemble",
         shape((rows_dev, ctx_size * columns)),
         in_specs=[smem] + [vmem] * len(pieces),
-        scratch_shapes=[pltpu.VMEM((ctx_size * columns, rows_dev), F32)],
+        scratch_shapes=[pltpu.VMEM((ctx_size * columns, rows_dev), BF16)],
     )(place1, *pieces)
 
 

time: 131 us -> 132 us (level)
  starting transfers between devices: 20.7 us -> 24.3 us
  waiting for transfers between devices: 49.8 us -> 47.1 us
    ppermute x31 -> x30, waiting for transfers between devices: 49.8 us -> 47.1 us  [swap(): return lax.ppermute(value, axis, pairs)]
    ppermute x0 -> x1, starting transfers between devices: none -> 2.44 us  [on_device(): last_state = lax.ppermute(sent, 'ctx', upwards)]
    ppermute x31 -> x30, starting transfers between devices: 20.7 us -> 21.9 us  [swap(): return lax.ppermute(value, axis, pairs)]
  transfers between devices with their start and end apart: 31 -> 31, of which waited for: 16 -> 15; matrix products, arithmetic and copies ran while one was open for 3% -> 3% of each run, Pallas kernels for 38% -> 37%
where the time goes in v7:
time: 132 us
  Pallas kernels  52 us (39%)
  waiting for transfers between devices  47.1 us (36%)
  starting transfers between devices  24.3 us (18%)
  local copies, waits for them, and re-layouts  8 us (6%)
    ppermute x30, waiting for transfers between devices, swap(): return lax.ppermute(value, axis, pairs)  47.1 us
    ppermute x30, starting transfers between devices, swap(): return lax.ppermute(value, axis, pairs)  21.9 us
    pallas_call x8, Pallas kernels, project(): kernel_call(project_kernel, name, shape((rows, count * columns, rows_dev)...  21.2 us
    pallas_call x1, Pallas kernels, on_device(): kernel_call(functools.partial(local_kernel, near, pieces), 'local_levels'...  10.8 us
    pallas_call x2, Pallas kernels, step(): kernel_call(functools.partial(merge_kernel, bit, head_count), 'merge', tu...  3.91 us
    pallas_call x1, Pallas kernels, chip_sum(): kernel_call(functools.partial(factors_kernel, levels, heads_size), 'facto...  3.7 us
    unnamed x30, local copies, waits for them, and re-layouts  3.34 us
    pallas_call x1, Pallas kernels, on_device(): kernel_call(functools.partial(assemble_kernel, groups), 'assemble', shape...  2.86 us
  transfers between devices with their start and end apart: 31, of which 15 were waited for; matrix products, arithmetic and copies ran while one was open for 3% of the time, Pallas kernels for 37%

profile of v7, /device:TPU:0, one launch (start us, length us, event | category | flops | bytes accessed | tf_op | source)
XLA Modules:
  0.0 131.8 jit_solution(12052815250440489545)
XLA Ops:
  0.0 4.0 %collective-permute-start.13 = (bf16[320,1280]{1,0:T(8,128)(2,1)}, bf16[320,1280]{1,0:T(8,128)(2,1)}, u32[]{:S(2)}, u32[]{:S(2)}) collective-permute-start(bf16[320,1280]{1,0:T(8,128)(2,1)} %bitcast.22), channel_id=1, source_target_pairs={{0,16},{4,20},{8,24},{12,28},{16,0},{20,4},{24,8},{28,12},{1,17},{... | collective-permute-start | bytes 2457608 | tf_op jit(solution)/shard_map/ppermute | solution.py:28
  17.9 3.3 %conditional.6 = (bf16[2,1280,128]{2,1,0:T(8,128)(2,1)}, bf16[1280,128]{1,0:T(8,128)(2,1)S(1)}) conditional(s32[]{:T(128)} %convert_element_type.7, () %tuple.69, (bf16[2,1280,128]{2,1,0:T(8,128)(2,1)S(1)}, f32[2,1280,128]{2,1,0:T(8,128)S(1)}) %tuple.70), branch_computations={%region_0.0_spmd, %region_1.0_spmd} | conditional | bytes 2621496 | solution.py:456
  22.2 11.4 %conditional.7 = (f32[1280,128]{1,0:T(8,128)S(1)}, bf16[1312,128]{1,0:T(8,128)(2,1)S(1)}, f32[4,20,256]{2,1,0:T(8,128)}, f32[5,4,20,256]{3,2,1,0:T(8,128)}, f32[...) conditional(s32[]{:T(128)} %convert_element_type.7, () %tuple.68, ...), branch_computations={%region_2.0_spmd, %region_3.4_spmd} | conditional | bytes 7295176 | solution.py:456
  26.2 3.7 %factors.1 = (f32[4,20,256]{2,1,0:T(8,128)}, f32[5,4,20,256]{3,2,1,0:T(8,128)}, f32[3,4,20,256]{3,2,1,0:T(8,128)}, f32[26,20,128]{2,1,0:T(8,128)}, bf16[4,2,256,...) custom-call(f32[20,1024]{1,0:T(8,128)} %get-tuple-element.83.decay_r, ...), custom_call_target="tpu_custom_call" | custom-call | tf_op jit(solution)/shard_map/cond/branch_1_fun/factors/pallas_call | solution.py:581
  34.4 20.9 %conditional.8 = (bf16[1312,128]{1,0:T(8,128)(2,1)}, bf16[1312,128]{1,0:T(8,128)(2,1)}, f32[32,128]{1,0:T(8,128)S(1)}, f32[32,128]{1,0:T(8,128)S(1)}, f32[32,128]{1,0:T(8,128)S(1)}, /*index=5*/bf16[1312,128]{1,0:T(8,128)(2,1)}) conditional(s32[]{:T(128)} %convert_element_type.7, () %tuple.67, (bf16[1312,128]{1,0:T(8,128)(2,1)S(1)}, s32[1]{0:T(128)}, ...), branch_computations={%region_4.5_spmd, %region_5.6_spmd} | conditional | flops 12 | bytes 2719997 | solution.py:456
  35.0 8.3 %collective-permute-done.1.got_ref = bf16[1312,128]{1,0:T(8,128)(2,1)} collective-permute-done((bf16[1312,128]{1,0:T(8,128)(2,1)S(1)}, bf16[1312,128]{1,0:T(8,128)(2,1)}, u32[]{:S(2)}, u32[]{:S(2)}) %collective-permute-start.1) | collective-permute-done | bytes 335904 | tf_op jit(solution)/shard_map/cond/branch_1_fun/ppermute | solution.py:28
  45.7 7.7 %collective-permute-done.2.got_ref = bf16[1312,128]{1,0:T(8,128)(2,1)} collective-permute-done((bf16[1312,128]{1,0:T(8,128)(2,1)}, bf16[1312,128]{1,0:T(8,128)(2,1)}, u32[]{:S(2)}, u32[]{:S(2)}) %collective-permute-start.2) | collective-permute-done | bytes 335904 | tf_op jit(solution)/shard_map/cond/branch_1_fun/ppermute | solution.py:28
  55.5 2.4 %collective-permute-start.22 = (bf16[1312,128]{1,0:T(8,128)(2,1)}, bf16[1312,128]{1,0:T(8,128)(2,1)S(1)}, u32[]{:S(2)}, u32[]{:S(2)}) collective-permute-start(bf16[1312,128]{1,0:T(8,128)(2,1)} %get-tuple-element.206), channel_id=1, source_target_pairs={{0,16},{4,20},{8,24},{12,28},{1,17},{5,21},{9,25},{13,29},{2,18},{... | collective-permute-start | bytes 1007624 | tf_op jit(solution)/shard_map/ppermute | solution.py:639
  59.4 10.8 %local_levels.1.pre_ref = f32[4,1280,256]{2,1,0:T(8,128)S(1)} custom-call(s32[1]{0:T(128)} %bitcast.8.me_ref, bf16[1280,256]{1,0:T(8,128)(2,1)S(1)} %get-tuple-element.188.refs_0_, bf16[1280,256]{1,0:T(8,128)(2,1)S(1)} %collective-permute-done.20.refs_1_, bf16[1280,128]{1,0:T(8,128)(2,1)S(1)} %collective-permute-done.16.refs_2_, ...), custom_call_target="tpu_custom_call" | custom-call | tf_op jit(solution)/shard_map/local_levels/pallas_call | solution.py:662
  72.8 5.7 %collective-permute-done.19.refs_3_ = bf16[320,1280]{1,0:T(8,128)(2,1)S(1)} collective-permute-done((bf16[320,1280]{1,0:T(8,128)(2,1)}, bf16[320,1280]{1,0:T(8,128)(2,1)S(1)}, u32[]{:S(2)}, u32[]{:S(2)}) %collective-permute-start.19) | collective-permute-done | bytes 819232 | tf_op jit(solution)/shard_map/ppermute | solution.py:28
  78.5 4.9 %collective-permute-done.26.refs_3_ = bf16[320,1280]{1,0:T(8,128)(2,1)} collective-permute-done((bf16[320,1280]{1,0:T(8,128)(2,1)}, bf16[320,1280]{1,0:T(8,128)(2,1)}, u32[]{:S(2)}, u32[]{:S(2)}) %collective-permute-start.26) | collective-permute-done | bytes 819232 | tf_op jit(solution)/shard_map/ppermute | solution.py:28
  84.0 2.5 %collective-permute-start.27 = (bf16[320,1280]{1,0:T(8,128)(2,1)}, bf16[320,1280]{1,0:T(8,128)(2,1)}, u32[]{:S(2)}, u32[]{:S(2)}) collective-permute-start(bf16[320,1280]{1,0:T(8,128)(2,1)} %collective-permute-done.17), channel_id=1, source_target_pairs={{0,8},{4,12},{8,0},{12,4},{16,24},{20,28},{24,16},{28,20},{1,9},{5... | collective-permute-start | bytes 2457608 | tf_op jit(solution)/shard_map/ppermute | solution.py:28
  86.5 12.6 %conditional.9 = (bf16[1,640,256]{2,1,0:T(8,128)(2,1)S(1)}, bf16[640,256]{1,0:T(8,128)(2,1)}, bf16[320,1280]{1,0:T(8,128)(2,1)}, bf16[320,1280]{1,0:T(8,128)(2,1)}, f32[640,256]{1,0:T(8,128)S(1)}) conditional(s32[]{:T(128)} %convert_element_type.7, () %tuple.66, (bf16[320,1280]{1,0:T(8,128)(2,1)}, bf16[320,1280]{1,0:T(8,128)(2,1)S(1)}, ...), branch_computations={%region_6.7_spmd, %region_7.8_spmd} | conditional | bytes 14418136 | solution.py:456
  90.2 2.7 %project_far.4 = bf16[1,640,256]{2,1,0:T(8,128)(2,1)S(1)} custom-call(bf16[1280,256]{1,0:T(8,128)(2,1)S(1)} %get-tuple-element.113.refs_0_, bf16[2,1280,256]{2,1,0:T(8,128)(2,1)S(1)} %get-tuple-element.114.refs_1_, bf16[320,1280]{1,0:T(8,128)(2,1)} %get-tuple-element.115.refs_2_, bf16[320,1280]{1,0:T(8,128)(2,1)S(1)} %get-tuple-element.116.refs_3_, ...), custom_call_target="tpu_custom_call" | custom-call | tf_op jit(solution)/shard_map/cond/branch_1_fun/project_far/pallas_call | solution.py:711
  92.9 2.4 %project_own.4 = f32[1,640,256]{2,1,0:T(8,128)S(1)} custom-call(bf16[1280,256]{1,0:T(8,128)(2,1)S(1)} %get-tuple-element.122.refs_0_, bf16[2,1280,256]{2,1,0:T(8,128)(2,1)S(1)} %get-tuple-element.114.refs_1_, bf16[320,1280]{1,0:T(8,128)(2,1)S(1)} %get-tuple-element.117.refs_2_, bf16[320,1280]{1,0:T(8,128)(2,1)} %get-tuple-element.118.refs_3_, ...), custom_call_target="tpu_custom_call" | custom-call | tf_op jit(solution)/shard_map/cond/branch_1_fun/project_own/pallas_call | solution.py:711
  95.3 3.8 %collective-permute-done.5 = bf16[640,256]{1,0:T(8,128)(2,1)} collective-permute-done((bf16[640,256]{1,0:T(8,128)(2,1)S(1)}, bf16[640,256]{1,0:T(8,128)(2,1)}, u32[]{:S(2)}, u32[]{:S(2)}) %collective-permute-start.5) | collective-permute-done | bytes 327712 | tf_op jit(solution)/shard_map/cond/branch_1_fun/ppermute | solution.py:28
  99.9 10.2 %conditional.10 = (bf16[1,640,256]{2,1,0:T(8,128)(2,1)S(1)}, bf16[640,256]{1,0:T(8,128)(2,1)}, bf16[320,1280]{1,0:T(8,128)(2,1)}, bf16[320,1280]{1,0:T(8,128)(2,1)}) conditional(s32[]{:T(128)} %convert_element_type.7, () %tuple.81, (bf16[320,1280]{1,0:T(8,128)(2,1)}, bf16[320,1280]{1,0:T(8,128)(2,1)}, bf16[1280,256]{1,0:T(8,128)(2,1)S(1)}, ...), branch_computations={%region_8.9_spmd, %region_9.10_spmd} | conditional | bytes 7864472 | solution.py:456
  103.8 2.9 %project_far.6 = bf16[1,640,256]{2,1,0:T(8,128)(2,1)S(1)} custom-call(bf16[1280,256]{1,0:T(8,128)(2,1)S(1)} %get-tuple-element.123.refs_0_, bf16[2,1280,256]{2,1,0:T(8,128)(2,1)S(1)} %get-tuple-element.124.refs_1_, bf16[320,1280]{1,0:T(8,128)(2,1)} %get-tuple-element.125.refs_2_, bf16[320,1280]{1,0:T(8,128)(2,1)} %get-tuple-element.126.refs_3_, ...), custom_call_target="tpu_custom_call" | custom-call | tf_op jit(solution)/shard_map/cond/branch_1_fun/project_far/pallas_call | solution.py:711
  106.7 3.5 %collective-permute-done.8 = bf16[640,256]{1,0:T(8,128)(2,1)} collective-permute-done((bf16[640,256]{1,0:T(8,128)(2,1)S(1)}, bf16[640,256]{1,0:T(8,128)(2,1)}, u32[]{:S(2)}, u32[]{:S(2)}) %collective-permute-start.8) | collective-permute-done | bytes 327712 | tf_op jit(solution)/shard_map/cond/branch_1_fun/ppermute | solution.py:28
  111.7 6.7 %conditional.11 = (bf16[1,640,256]{2,1,0:T(8,128)(2,1)S(1)}, bf16[320,1280]{1,0:T(8,128)(2,1)}, bf16[320,1280]{1,0:T(8,128)(2,1)}) conditional(s32[]{:T(128)} %convert_element_type.7, () %tuple.86, (bf16[320,1280]{1,0:T(8,128)(2,1)}, bf16[320,1280]{1,0:T(8,128)(2,1)}, bf16[1280,256]{1,0:T(8,128)(2,1)S(1)}, ...), branch_computations={%region_10.11_spmd, %region_11.12_spmd} | conditional | bytes 6553704 | solution.py:456
  115.6 2.9 %project_far.7 = bf16[1,640,256]{2,1,0:T(8,128)(2,1)S(1)} custom-call(bf16[1280,256]{1,0:T(8,128)(2,1)S(1)} %get-tuple-element.128.refs_0_, bf16[2,1280,256]{2,1,0:T(8,128)(2,1)S(1)} %get-tuple-element.129.refs_1_, bf16[320,1280]{1,0:T(8,128)(2,1)} %get-tuple-element.130.refs_2_, bf16[320,1280]{1,0:T(8,128)(2,1)} %get-tuple-element.131.refs_3_, ...), custom_call_target="tpu_custom_call" | custom-call | tf_op jit(solution)/shard_map/cond/branch_1_fun/project_far/pallas_call | solution.py:711
  120.7 2.9 %project_own.7 = f32[1,640,256]{2,1,0:T(8,128)S(1)} custom-call(bf16[1280,256]{1,0:T(8,128)(2,1)S(1)} %get-tuple-element.227.refs_0_, bf16[2,1280,256]{2,1,0:T(8,128)(2,1)S(1)} %collective-permute-done.23.refs_1_, bf16[320,1280]{1,0:T(8,128)(2,1)} %collective-permute-done.27.refs_2_, bf16[320,1280]{1,0:T(8,128)(2,1)} %collective-permute-done.28.refs_3_, ...), custom_call_target="tpu_custom_call" | custom-call | tf_op jit(solution)/shard_map/project_own/pallas_call | solution.py:711
  123.6 3.0 %project_own.6 = f32[1,640,256]{2,1,0:T(8,128)S(1)} custom-call(bf16[1280,256]{1,0:T(8,128)(2,1)S(1)} %get-tuple-element.227.refs_0_, bf16[2,1280,256]{2,1,0:T(8,128)(2,1)S(1)} %collective-permute-done.23.refs_1_, bf16[320,1280]{1,0:T(8,128)(2,1)} %collective-permute-done.18.refs_2_, bf16[320,1280]{1,0:T(8,128)(2,1)} %collective-permute-done.26.refs_3_, ...), custom_call_target="tpu_custom_call" | custom-call | tf_op jit(solution)/shard_map/project_own/pallas_call | solution.py:711
  129.0 2.9 %assemble.1 = bf16[256,2560]{1,0:T(8,128)(2,1)} custom-call(s32[1]{0:T(128)} %bitcast.6.place_ref, f32[640,256]{1,0:T(8,128)S(1)} %copy-done.11, bf16[640,256]{1,0:T(8,128)(2,1)} %get-tuple-element.229.refs_1_, f32[640,256]{1,0:T(8,128)S(1)} %bitcast.19, bf16[640,256]{1,0:T(8,128)(2,1)} %get-tuple-element.233.refs_3_, f32[640,256]{1,0:T(8,128)S(1)} %bitcast.18, ...), custom_call_target="tpu_custom_call" | custom-call | tf_op jit(solution)/shard_map/assemble/pallas_call | solution.py:779
  (108 shorter events, 54.4 us)
Async XLA Ops:
  0.0 55.4 %collective-permute-start.13 = (bf16[320,1280]{1,0:T(8,128)(2,1)}, bf16[320,1280]{1,0:T(8,128)(2,1)}, u32[]{:S(2)}, u32[]{:S(2)}) collective-permute-start(bf16[320,1280]{1,0:T(8,128)(2,1)} %bitcast.22), channel_id=1, source_target_pairs={{0,16},{4,20},{8,24},{12,28},{16,0},{20,4},{24,8},{28,12},{1,17},{... | collective-permute-start | bytes 2457608 | tf_op jit(solution)/shard_map/ppermute | solution.py:28
  4.0 51.3 %collective-permute-start.18 = (bf16[320,1280]{1,0:T(8,128)(2,1)}, bf16[320,1280]{1,0:T(8,128)(2,1)}, u32[]{:S(2)}, u32[]{:S(2)}) collective-permute-start(bf16[320,1280]{1,0:T(8,128)(2,1)} %bitcast.23), channel_id=1, source_target_pairs={{0,8},{4,12},{8,0},{12,4},{16,24},{20,28},{24,16},{28,20},{1,9},{5... | collective-permute-start | bytes 2457608 | tf_op jit(solution)/shard_map/ppermute | solution.py:28
  5.6 49.8 %collective-permute-start.17 = (bf16[320,1280]{1,0:T(8,128)(2,1)}, bf16[320,1280]{1,0:T(8,128)(2,1)}, u32[]{:S(2)}, u32[]{:S(2)}) collective-permute-start(bf16[320,1280]{1,0:T(8,128)(2,1)} %bitcast.24), channel_id=1, source_target_pairs={{0,4},{4,0},{8,12},{12,8},{16,20},{20,16},{24,28},{28,24},{1,5},{5... | collective-permute-start | bytes 2457608 | tf_op jit(solution)/shard_map/ppermute | solution.py:28
  9.0 4.9 %collective-permute-start.14 = (f32[2,20,256]{2,1,0:T(8,128)S(1)}, f32[2,20,256]{2,1,0:T(8,128)S(1)}, u32[]{:S(2)}, u32[]{:S(2)}) collective-permute-start(f32[2,20,256]{2,1,0:T(8,128)S(1)} %get-tuple-element.195), channel_id=1, source_target_pairs={{0,2},{1,3},{2,0},{3,1},{4,6},{5,7},{6,4},{7,5},{8,10},{9,11},{10,... | collective-permute-start | bytes 122888 | tf_op jit(solution)/shard_map/ppermute | solution.py:28
  13.9 8.3 %collective-permute-start.16 = (bf16[1280,128]{1,0:T(8,128)(2,1)S(1)}, bf16[1280,128]{1,0:T(8,128)(2,1)S(1)}, u32[]{:S(2)}, u32[]{:S(2)}) collective-permute-start(bf16[1280,128]{1,0:T(8,128)(2,1)S(1)} %get-tuple-element.199.refs_2_), channel_id=1, source_target_pairs={{0,2},{1,3},{2,0},{3,1},{4,6},{5,7},{6,4},{7,5},{8,10},{9,11},{10,... | collective-permute-start | bytes 983048 | tf_op jit(solution)/shard_map/ppermute | solution.py:28
  22.2 7.6 %collective-permute-start.12 = (bf16[1280,256]{1,0:T(8,128)(2,1)}, bf16[1280,256]{1,0:T(8,128)(2,1)S(1)}, u32[]{:S(2)}, u32[]{:S(2)}) collective-permute-start(bf16[1280,256]{1,0:T(8,128)(2,1)} %get-tuple-element.90), channel_id=1, source_target_pairs={{0,1},{1,0},{2,3},{3,2},{4,5},{5,4},{6,7},{7,6},{8,9},{9,8},{10,11... | collective-permute-start | bytes 1966088 | tf_op jit(solution)/shard_map/cond/branch_1_fun/ppermute | solution.py:28
  23.0 9.6 %collective-permute-start.11 = (bf16[1280,128]{1,0:T(8,128)(2,1)}, bf16[1280,128]{1,0:T(8,128)(2,1)S(1)}, u32[]{:S(2)}, u32[]{:S(2)}) collective-permute-start(bf16[1280,128]{1,0:T(8,128)(2,1)} %copy-done.15), channel_id=1, source_target_pairs={{0,2},{1,3},{2,0},{3,1},{4,6},{5,7},{6,4},{7,5},{8,10},{9,11},{10,... | collective-permute-start | bytes 983048 | tf_op jit(solution)/shard_map/cond/branch_1_fun/ppermute | solution.py:28
  33.7 25.6 %collective-permute-start.21 = (bf16[1280,384]{1,0:T(8,128)(2,1)}, bf16[1280,384]{1,0:T(8,128)(2,1)S(1)}, u32[]{:S(2)}, u32[]{:S(2)}) collective-permute-start(bf16[1280,384]{1,0:T(8,128)(2,1)} %get-tuple-element.209), channel_id=1, source_target_pairs={{0,2},{1,3},{2,0},{3,1},{4,6},{5,7},{6,4},{7,5},{8,10},{9,11},{10,... | collective-permute-start | bytes 2949128 | tf_op jit(solution)/shard_map/ppermute | solution.py:28
  34.4 8.9 %collective-permute-start.1 = (bf16[1312,128]{1,0:T(8,128)(2,1)S(1)}, bf16[1312,128]{1,0:T(8,128)(2,1)}, u32[]{:S(2)}, u32[]{:S(2)}) collective-permute-start(bf16[1312,128]{1,0:T(8,128)(2,1)S(1)} %get-tuple-element.101), channel_id=1, source_target_pairs={{0,4},{4,0},{8,12},{12,8},{16,20},{20,16},{24,28},{28,24},{1,5},{5... | collective-permute-start | bytes 1007624 | tf_op jit(solution)/shard_map/cond/branch_1_fun/ppermute | solution.py:28
  45.3 8.1 %collective-permute-start.2 = (bf16[1312,128]{1,0:T(8,128)(2,1)}, bf16[1312,128]{1,0:T(8,128)(2,1)}, u32[]{:S(2)}, u32[]{:S(2)}) collective-permute-start(bf16[1312,128]{1,0:T(8,128)(2,1)} %get-tuple-element.105), channel_id=1, source_target_pairs={{0,8},{4,12},{8,0},{12,4},{16,24},{20,28},{24,16},{28,20},{1,9},{5... | collective-permute-start | bytes 1007624 | tf_op jit(solution)/shard_map/cond/branch_1_fun/ppermute | solution.py:28
  55.4 3.9 %collective-permute-start.20 = (bf16[1280,256]{1,0:T(8,128)(2,1)S(1)}, bf16[1280,256]{1,0:T(8,128)(2,1)S(1)}, u32[]{:S(2)}, u32[]{:S(2)}) collective-permute-start(bf16[1280,256]{1,0:T(8,128)(2,1)S(1)} %get-tuple-element.208.refs_1_), channel_id=1, source_target_pairs={{0,1},{1,0},{2,3},{3,2},{4,5},{5,4},{6,7},{7,6},{8,9},{9,8},{10,11... | collective-permute-start | bytes 1966088 | tf_op jit(solution)/shard_map/ppermute | solution.py:28
  55.5 14.8 %collective-permute-start.22 = (bf16[1312,128]{1,0:T(8,128)(2,1)}, bf16[1312,128]{1,0:T(8,128)(2,1)S(1)}, u32[]{:S(2)}, u32[]{:S(2)}) collective-permute-start(bf16[1312,128]{1,0:T(8,128)(2,1)} %get-tuple-element.206), channel_id=1, source_target_pairs={{0,16},{4,20},{8,24},{12,28},{1,17},{5,21},{9,25},{13,29},{2,18},{... | collective-permute-start | bytes 1007624 | tf_op jit(solution)/shard_map/ppermute | solution.py:639
  57.9 20.6 %collective-permute-start.19 = (bf16[320,1280]{1,0:T(8,128)(2,1)}, bf16[320,1280]{1,0:T(8,128)(2,1)S(1)}, u32[]{:S(2)}, u32[]{:S(2)}) collective-permute-start(bf16[320,1280]{1,0:T(8,128)(2,1)} %collective-permute-done.13.refs_2_), channel_id=1, source_target_pairs={{0,4},{4,0},{8,12},{12,8},{16,20},{20,16},{24,28},{28,24},{1,5},{5... | collective-permute-start | bytes 2457608 | tf_op jit(solution)/shard_map/ppermute | solution.py:28
  58.5 24.8 %collective-permute-start.26 = (bf16[320,1280]{1,0:T(8,128)(2,1)}, bf16[320,1280]{1,0:T(8,128)(2,1)}, u32[]{:S(2)}, u32[]{:S(2)}) collective-permute-start(bf16[320,1280]{1,0:T(8,128)(2,1)} %collective-permute-done.13.refs_2_), channel_id=1, source_target_pairs={{0,8},{4,12},{8,0},{12,4},{16,24},{20,28},{24,16},{28,20},{1,9},{5... | collective-permute-start | bytes 2457608 | tf_op jit(solution)/shard_map/ppermute | solution.py:28
  72.2 14.3 %collective-permute-start.23 = (bf16[2,1280,256]{2,1,0:T(8,128)(2,1)S(1)}, bf16[2,1280,256]{2,1,0:T(8,128)(2,1)S(1)}, u32[]{:S(2)}, u32[]{:S(2)}) collective-permute-start(bf16[2,1280,256]{2,1,0:T(8,128)(2,1)S(1)} %get-tuple-element.224), channel_id=1, source_target_pairs={{0,1},{1,0},{2,3},{3,2},{4,5},{5,4},{6,7},{7,6},{8,9},{9,8},{10,11... | collective-permute-start | bytes 3932168 | tf_op jit(solution)/shard_map/ppermute | solution.py:28
  72.2 14.2 %collective-permute-start.25 = (bf16[320,1280]{1,0:T(8,128)(2,1)}, bf16[320,1280]{1,0:T(8,128)(2,1)S(1)}, u32[]{:S(2)}, u32[]{:S(2)}) collective-permute-start(bf16[320,1280]{1,0:T(8,128)(2,1)} %collective-permute-done.17), channel_id=1, source_target_pairs={{0,1},{1,0},{2,3},{3,2},{4,5},{5,4},{6,7},{7,6},{8,9},{9,8},{10,11... | collective-permute-start | bytes 2457608 | tf_op jit(solution)/shard_map/ppermute | solution.py:28
  72.7 13.7 %collective-permute-start.24 = (bf16[320,1280]{1,0:T(8,128)(2,1)S(1)}, bf16[320,1280]{1,0:T(8,128)(2,1)S(1)}, u32[]{:S(2)}, u32[]{:S(2)}) collective-permute-start(bf16[320,1280]{1,0:T(8,128)(2,1)S(1)} %bitcast.25), channel_id=1, source_target_pairs={{0,1},{1,0},{2,3},{3,2},{4,5},{5,4},{6,7},{7,6},{8,9},{9,8},{10,11... | collective-permute-start | bytes 2457608 | tf_op jit(solution)/shard_map/ppermute | solution.py:28
  83.4 26.8 %collective-permute-start.28 = (bf16[320,1280]{1,0:T(8,128)(2,1)}, bf16[320,1280]{1,0:T(8,128)(2,1)}, u32[]{:S(2)}, u32[]{:S(2)}) collective-permute-start(bf16[320,1280]{1,0:T(8,128)(2,1)} %collective-permute-done.26.refs_3_), channel_id=1, source_target_pairs={{0,4},{4,0},{8,12},{12,8},{16,20},{20,16},{24,28},{28,24},{1,5},{5... | collective-permute-start | bytes 2457608 | tf_op jit(solution)/shard_map/ppermute | solution.py:28
  84.0 26.2 %collective-permute-start.27 = (bf16[320,1280]{1,0:T(8,128)(2,1)}, bf16[320,1280]{1,0:T(8,128)(2,1)}, u32[]{:S(2)}, u32[]{:S(2)}) collective-permute-start(bf16[320,1280]{1,0:T(8,128)(2,1)} %collective-permute-done.17), channel_id=1, source_target_pairs={{0,8},{4,12},{8,0},{12,4},{16,24},{20,28},{24,16},{28,20},{1,9},{5... | collective-permute-start | bytes 2457608 | tf_op jit(solution)/shard_map/ppermute | solution.py:28
  89.2 9.9 %collective-permute-start.5 = (bf16[640,256]{1,0:T(8,128)(2,1)S(1)}, bf16[640,256]{1,0:T(8,128)(2,1)}, u32[]{:S(2)}, u32[]{:S(2)}) collective-permute-start(bf16[640,256]{1,0:T(8,128)(2,1)S(1)} %bitcast.21), channel_id=1, source_target_pairs={{0,2},{1,3},{2,0},{3,1},{4,6},{5,7},{6,4},{7,5},{8,10},{9,11},{10,... | collective-permute-start | bytes 983048 | tf_op jit(solution)/shard_map/cond/branch_1_fun/ppermute | solution.py:28
  99.9 3.8 %collective-permute-start.7 = (bf16[320,1280]{1,0:T(8,128)(2,1)}, bf16[320,1280]{1,0:T(8,128)(2,1)}, u32[]{:S(2)}, u32[]{:S(2)}) collective-permute-start(bf16[320,1280]{1,0:T(8,128)(2,1)} %get-tuple-element.126.refs_3_), channel_id=1, source_target_pairs={{0,1},{1,0},{2,3},{3,2},{4,5},{5,4},{6,7},{7,6},{8,9},{9,8},{10,11... | collective-permute-start | bytes 2457608 | tf_op jit(solution)/shard_map/cond/branch_1_fun/ppermute | solution.py:28
  100.4 9.7 %collective-permute-start.8 = (bf16[640,256]{1,0:T(8,128)(2,1)S(1)}, bf16[640,256]{1,0:T(8,128)(2,1)}, u32[]{:S(2)}, u32[]{:S(2)}) collective-permute-start(bf16[640,256]{1,0:T(8,128)(2,1)S(1)} %bitcast.31), channel_id=1, source_target_pairs={{0,2},{1,3},{2,0},{3,1},{4,6},{5,7},{6,4},{7,5},{8,10},{9,11},{10,... | collective-permute-start | bytes 983048 | tf_op jit(solution)/shard_map/cond/branch_1_fun/ppermute | solution.py:28
  110.9 9.0 %collective-permute-start.29 = (bf16[640,256]{1,0:T(8,128)(2,1)}, bf16[640,256]{1,0:T(8,128)(2,1)S(1)}, u32[]{:S(2)}, u32[]{:S(2)}) collective-permute-start(bf16[640,256]{1,0:T(8,128)(2,1)} %bitcast.32), channel_id=1, source_target_pairs={{0,2},{1,3},{2,0},{3,1},{4,6},{5,7},{6,4},{7,5},{8,10},{9,11},{10,... | collective-permute-start | bytes 983048 | tf_op jit(solution)/shard_map/ppermute | solution.py:28
  119.9 9.1 %collective-permute-start.30 = (bf16[640,256]{1,0:T(8,128)(2,1)S(1)}, bf16[640,256]{1,0:T(8,128)(2,1)S(1)}, u32[]{:S(2)}, u32[]{:S(2)}) collective-permute-start(bf16[640,256]{1,0:T(8,128)(2,1)S(1)} %bitcast.33), channel_id=1, source_target_pairs={{0,2},{1,3},{2,0},{3,1},{4,6},{5,7},{6,4},{7,5},{8,10},{9,11},{10,... | collective-permute-start | bytes 983048 | tf_op jit(solution)/shard_map/ppermute | solution.py:28
  (25 other events, 151.9 us)
